TPU v7x, 32 devices: a whole 2x2x4 slice. The times are simulated.
32 devices in a mesh: outer: 4 (over x, core), inner: 8 (over z, y).
Axes of the slice: x: 2, y: 2, z: 4, core: 2. Of those that a mesh axis runs over, the one named last changes fastest.
Arguments:
- inputs: bfloat16 [32768, 1024], P(('outer', 'inner')), may hold values from -6 to 6
- queries: bfloat16 [32768, 1024], P(('outer', 'inner')), may hold values from -6 to 6
- keys: bfloat16 [32768, 1024], P(('outer', 'inner')), may hold values from -6 to 6
- values: bfloat16 [32768, 1024], P(('outer', 'inner')), may hold values from -6 to 6
- out_grad: bfloat16 [32768, 1024], P(('outer', 'inner')), may hold values from -6 to 6
- master: float32 [1024, 1024], P('inner'), may hold values from -0.1875 to 0.1875
- moment1: float32 [1024, 1024], P('inner'), may hold values from -6 to 6
- moment2: float32 [1024, 1024], P('inner'), may hold values from 0.05 to 2
Outputs:
- query_grad: bfloat16 [32768, 1024], P(('outer', 'inner'))
- key_grad: bfloat16 [32768, 1024], P(('outer', 'inner'))
- new_master: float32 [1024, 1024], P('inner')
- new_moment1: float32 [1024, 1024], P('inner')
- new_moment2: float32 [1024, 1024], P('inner')
- weights: bfloat16 [1024, 1024], replicated
All inputs are finite; a program needn't handle non-finite values.
Results may differ from a plain program's by a relative error of at most 0.008.
Values may be sent and summed in bfloat16 or wider, within the bound.
No kernel may reach another device: no remote copies, remote signals or barrier semaphores. Data moves between devices by JAX's collectives and lax.ppermute only.
A program may use at most 192 MiB of HBM per device.

v0:
```python
import math

import jax
import jax.numpy as jnp
from jax import lax
from jax.sharding import PartitionSpec as P

H = 8
HD = 128
BLK = 512


def entering(array, axis, combine, identity, reverse):
    count, place = (lax.axis_size(axis), lax.axis_index(axis))
    everything = lax.all_gather(array, axis)
    start = jnp.broadcast_to(jnp.asarray(identity, array.dtype), array.shape)

    def turn(k, before):
        at = count - 1 - k if reverse else k
        reached = at > place if reverse else at < place
        new = combine(before, everything[at])
        return jnp.where(reached, new, before)

    return lax.fori_loop(0, count, turn, start)


def add_states(earlier, later):
    return earlier + later


def split_state(state):
    upper = state.astype(jnp.bfloat16)
    lower = (state - upper.astype(jnp.float32)).astype(jnp.bfloat16)
    return (upper, lower)


def state_times_query(form, rows, state):
    upper, lower = split_state(state)
    first = jnp.einsum(form, rows, upper, preferred_element_type=jnp.float32)
    return first + jnp.einsum(form, rows, lower, preferred_element_type=jnp.float32)


def local(inputs, queries, keys, values, out_grad, master, moment1, moment2):
    rows_here = inputs.shape[0]
    width = inputs.shape[1]
    n_outer = lax.axis_size("outer")
    n_inner = lax.axis_size("inner")
    total_tokens = rows_here * n_outer * n_inner
    att_scale = 1.0 / math.sqrt(HD * total_tokens)
    grad_scale = 1.0 / math.sqrt(total_tokens)
    blocks = rows_here // BLK
    shape_four = (blocks, BLK, H, HD)
    query_blocks = queries.reshape(shape_four)
    key_blocks = keys.reshape(shape_four)
    value_blocks = values.reshape(shape_four)
    grad_blocks = out_grad.reshape(shape_four)
    kv_block = jnp.einsum(
        "nthk,nthv->nhkv", key_blocks, value_blocks, preferred_element_type=jnp.float32
    )
    qg_block = jnp.einsum(
        "nthv,nthk->nhvk", grad_blocks, query_blocks, preferred_element_type=jnp.float32
    )
    own_kv = jnp.sum(kv_block, 0)
    own_qg = jnp.sum(qg_block, 0)
    zero_state = jnp.zeros_like(own_kv)
    kv_earlier = entering(own_kv, ("outer", "inner"), add_states, zero_state, False)
    qg_later = entering(own_qg, ("outer", "inner"), add_states, zero_state, True)
    key_value_prior = kv_earlier[None] + jnp.concatenate(
        [zero_state[None], jnp.cumsum(kv_block, 0)[:-1]], 0
    )
    qg_reverse = jnp.cumsum(qg_block[::-1], 0)[::-1]
    qg_after = qg_later[None] + jnp.concatenate([qg_reverse[1:], zero_state[None]], 0)
    causal = jnp.arange(BLK)[:, None] >= jnp.arange(BLK)[None, :]
    query_parts = []
    key_parts = []
    for block_number in range(blocks):
        query_b = query_blocks[block_number]
        key_block_rows = key_blocks[block_number]
        value_block_rows = value_blocks[block_number]
        block_gradient = grad_blocks[block_number]
        scores = jnp.einsum(
            "thv,shv->hts", block_gradient, value_block_rows, preferred_element_type=jnp.float32
        )
        scores = jnp.where(causal[None], scores, 0.0).astype(jnp.bfloat16)
        query_gradient = jnp.einsum(
            "hts,shk->thk", scores, key_block_rows, preferred_element_type=jnp.float32
        )
        query_gradient = query_gradient + state_times_query(
            "rgn,gfn->rgf", block_gradient, key_value_prior[block_number]
        )
        dkey = jnp.einsum("hts,thk->shk", scores, query_b, preferred_element_type=jnp.float32)
        dkey = dkey + state_times_query("shv,hvk->shk", value_block_rows, qg_after[block_number])
        query_parts.append((query_gradient * att_scale).astype(jnp.bfloat16).reshape(BLK, width))
        key_parts.append((dkey * att_scale).astype(jnp.bfloat16).reshape(BLK, width))
    query_grad = jnp.concatenate(query_parts, 0)
    key_grad = jnp.concatenate(key_parts, 0)
    product = lax.dot_general(
        inputs, key_grad, (((0,), (0,)), ((), ())), preferred_element_type=jnp.float32
    )
    shares = lax.psum_scatter(product * grad_scale, "inner", scatter_dimension=0, tiled=True)
    grad = lax.psum(shares, "outer")
    new_moment1 = 0.9 * moment1 + 0.1 * grad
    new_moment2 = 0.95 * moment2 + 0.05 * grad * grad
    new_master = master - 0.01 * (new_moment1 / (jnp.sqrt(new_moment2) + 1e-08) + 0.1 * master)
    weights = lax.all_gather(new_master.astype(jnp.bfloat16), "inner", axis=0, tiled=True)
    return (query_grad, key_grad, new_master, new_moment1, new_moment2, weights)


def solution(mesh):
    in_specs = (
        P(("outer", "inner"), None),
        P(("outer", "inner"), None),
        P(("outer", "inner"), None),
        P(("outer", "inner"), None),
        P(("outer", "inner"), None),
        P("inner", None),
        P("inner", None),
        P("inner", None),
    )
    out_specs = (
        P(("outer", "inner"), None),
        P(("outer", "inner"), None),
        P("inner", None),
        P("inner", None),
        P("inner", None),
        P(),
    )
    return jax.shard_map(local, mesh=mesh, in_specs=in_specs, out_specs=out_specs, check_vma=False)
```

profile of v0, /device:TPU:0, one launch (start us, length us, event | category | flops | bytes accessed | tf_op | source)
XLA Modules:
  0.0 506.6 jit_solution(17642497321647409861)
XLA Ops:
  7.2 2.4 copy.140
  10.2 2.9 fusion.43
  13.3 2.3 rev.4
  15.6 3.0 fusion.38
  23.2 3.2 fusion.40
  30.9 3.0 fusion.41
  36.2 2.3 copy.136
  38.6 5.1 %select_convert_fusion = bf16[8,512,512]{2,1,0:T(8,128)(2,1)} fusion(pred[512,512]{1,0:T(8,128)(4,1)S(1)} %iota_compare_fusion, bf16[512,8,128]{0,2,1:T(8,128)(2,1)} %bitcast.139, bf16[512,8,128]{0,2,1:T(8,128)(2,1)} %bitcast.145), kind=kOutput, calls=%fused_computation.2 | convolution fusion | flops 541065216 | bytes 6553600 | tf_op jit(solution)/shard_map/thv,shv->hts/dot_general | solution.py:81
  43.7 3.4 select_convert_fusion.1
  47.1 83.8 %all-gather.10.cloned.1.call-done = f32[256,128,128]{2,1,0:T(8,128)} async-done(((f32[8,128,128]{2,1,0:T(8,128)}), f32[256,128,128]{2,1,0:T(8,128)}) %all-gather.10.cloned.1.call-update) | async-done | bytes 16777232 | tf_op jit(solution)/shard_map/all_gather | solution.py:15
  130.9 40.2 %while.31 = (s32[]{:T(128)}, f32[8,128,128]{2,1,0:T(8,128)S(1)}, s32[]{:T(128)}, f32[32,8,128,128]{3,2,1,0:T(8,128)}, s32[]{:T(128)}, /*index=5*/s32[]{:T(128)}, s32[]{:T(128)}, s32[]{:T(128)}) while((s32[]{:T(128)}, f32[8,128,128]{2,1,0:T(8,128)S(1)}, s32[]{:T(128)}, f32[32,8,128,128]{3,2,1,0:T(8,128)}, s32[]{:T(128)}, ...), condition=%wide.region_6.7_spmd.clone, body=%wide.region_5.6_spmd.clone.sunk | while | flops 393224 | bytes 1573027 | solution.py:24
  179.7 2.4 copy.109
  182.1 5.2 %fusion.3 = bf16[512,8,128]{0,2,1:T(8,128)(2,1)} fusion(f32[8,128,512]{2,1,0:T(8,128)} %fusion.28, f32[8,128,512]{2,1,0:T(8,128)} %fusion.22, bf16[512,8,128]{0,2,1:T(8,128)(2,1)S(1)} %bitcast.152, bf16[8,512,512]{2,1,0:T(8,128)(2,1)} %select_convert_fusion.1), kind=kOutput, calls=%fused_computation.12 | convolution fusion | flops 538968064 | bytes 10485760 | tf_op jit(solution)/shard_map/hts,thk->shk/dot_general | solution.py:91
  187.3 2.4 copy.108
  192.4 4.4 multiply_bitcast_fusion
  202.3 81.3 %reduce-scatter.2.cloned.1.call-done = f32[128,1024]{0,1:T(8,128)} async-done(((f32[1024,1024]{0,1:T(8,128)}), f32[128,1024]{0,1:T(8,128)}) %reduce-scatter.2.cloned.1.call-update) | async-done | bytes 524304 | tf_op jit(solution)/shard_map/reduce_scatter | solution.py:100
  283.8 3.5 fusion.42
  295.6 23.5 %all-reduce.3.cloned.1.call-done = f32[128,1024]{0,1:T(8,128)} async-done(((f32[128,1024]{0,1:T(8,128)}), f32[128,1024]{0,1:T(8,128)}) %all-reduce.3.cloned.1.call-update) | async-done | bytes 524304 | tf_op jit(solution)/shard_map/psum | solution.py:101
  319.0 2.8 fusion.36
  321.9 116.1 %all-gather.8.cloned.1.call-done = f32[256,128,128]{2,1,0:T(8,128)} async-done(((f32[8,128,128]{2,1,0:T(8,128)}), f32[256,128,128]{2,1,0:T(8,128)}) %all-gather.8.cloned.1.call-update) | async-done | bytes 16777232 | tf_op jit(solution)/shard_map/all_gather | solution.py:15
  437.9 40.2 %while.30 = (s32[]{:T(128)}, f32[8,128,128]{2,1,0:T(8,128)S(1)}, s32[]{:T(128)}, f32[32,8,128,128]{3,2,1,0:T(8,128)}, s32[]{:T(128)}, /*index=5*/s32[]{:T(128)}) while((s32[]{:T(128)}, f32[8,128,128]{2,1,0:T(8,128)S(1)}, s32[]{:T(128)}, f32[32,8,128,128]{3,2,1,0:T(8,128)}, s32[]{:T(128)}, /*index=5*/s32[]{:T(128)}) %tuple.100), condition=%wide.region_2.3_spmd.clone, body=%wide.region_1.0_spmd.clone.sunk | while | flops 393220 | bytes 1572965 | solution.py:24
  481.5 2.5 fusion.5
  484.0 2.4 copy.95
  496.2 3.9 copy.117
  (168 shorter events, 129.2 us)
Async XLA Ops:
  7.2 185.2 %copy-start = (bf16[1024,1024]{1,0:T(8,128)(2,1)S(1)}, bf16[1024,1024]{1,0:T(8,128)(2,1)}, u32[]{:S(2)}) copy-start(bf16[1024,1024]{1,0:T(8,128)(2,1)} %param.12) | copy-start | bytes 6291460
  7.2 123.7 %all-gather.10.cloned.1.call-start = ((), (), s32[]{:S(2)}) async-start(), calls=%async_computation.5 | async-start | bytes 17301504 | tf_op jit(solution)/shard_map/all_gather | solution.py:15
  7.2 2.4 copy-start.11
  13.2 270.4 %reduce-scatter.2.cloned.1.call-start = ((), (), s32[]{:S(2)}) async-start(), calls=%async_computation.1 | async-start | bytes 4718592 | tf_op jit(solution)/shard_map/reduce_scatter | solution.py:100
  38.6 5.1 %copy-start.5 = (bf16[512,1024]{0,1:T(8,128)(2,1)S(1)}, bf16[512,1024]{0,1:T(8,128)(2,1)}, u32[]{:S(2)}) copy-start(bf16[512,1024]{0,1:T(8,128)(2,1)} %copy.134) | copy-start | bytes 3145732
  38.6 5.1 %copy-start.8 = (bf16[512,1024]{0,1:T(8,128)(2,1)S(1)}, bf16[512,1024]{0,1:T(8,128)(2,1)}, u32[]{:S(2)}) copy-start(bf16[512,1024]{0,1:T(8,128)(2,1)} %copy.135) | copy-start | bytes 3145732
  130.9 40.2 %copy-start.27 = (pred[2]{0:T(512)(128)(4,1)S(1)}, pred[2]{0:T(512)(128)(4,1)}, u32[]{:S(2)}) copy-start(pred[2]{0:T(512)(128)(4,1)} %constant.94.clone.1) | copy-start | bytes 10
  174.4 3.6 copy-start.3
  179.7 2.4 copy-start.15
  187.3 2.4 copy-start.19
  196.8 122.3 %all-reduce.3.cloned.1.call-start = ((), (), s32[]{:S(2)}) async-start(), calls=%async_computation.2 | async-start | bytes 1048576 | tf_op jit(solution)/shard_map/psum | solution.py:101
  198.3 2.0 copy-start.13
  200.3 83.5 %copy-start.24 = (bf16[128,8,8,128]{3,2,1,0:T(8,128)(2,1)S(1)}, bf16[128,8,8,128]{3,2,1,0:T(8,128)(2,1)}, u32[]{:S(2)}) copy-start(bf16[128,8,8,128]{3,2,1,0:T(8,128)(2,1)} %copy.139) | copy-start | bytes 6291460
  283.6 154.3 %all-gather.8.cloned.1.call-start = ((), (), s32[]{:S(2)}) async-start(), calls=%async_computation.4 | async-start | bytes 17301504 | tf_op jit(solution)/shard_map/all_gather | solution.py:15
  287.4 3.4 copy-start.26
  287.4 208.8 %all-gather.6.cloned.1.call-start = ((), (), s32[]{:S(2)}) async-start(), calls=%async_computation.3 | async-start | bytes 2359296 | tf_op jit(solution)/shard_map/all_gather | solution.py:105
  437.9 40.2 %copy-start.25 = (f32[1,8,128,128]{3,2,1,0:T(8,128)S(1)}, f32[1,8,128,128]{3,2,1,0:T(8,128)}, u32[]{:S(2)}) copy-start(f32[1,8,128,128]{3,2,1,0:T(8,128)} %slice.63) | copy-start | bytes 1572868
  479.3 2.2 copy-start.4
  484.0 2.4 copy-start.6
  486.4 2.2 copy-start.2
  486.8 2.2 copy-start.17
  491.7 2.5 copy-start.21
  493.2 2.0 copy-start.20
  495.2 4.9 copy-start.1
  (9 other events, 13.2 us)
Sparse Core Ops, SparseCore 0:
  13.3 117.5 all-gather.9
  196.9 86.6 reduce-scatter.1
  286.0 32.9 all-reduce.2
  323.0 114.8 all-gather.7
  440.0 49.2 all-gather.5
where the time goes:
time: 511 us; the launch traced here: 507 us
  waiting for transfers between devices  305 us (60%)
  other arithmetic  86.5 us (17%)
  local copies, waits for them, and re-layouts  62.8 us (12%)
  matrix products  36.4 us (7%)
  between operations  14.1 us (3%)
    all_gather x2, waiting for transfers between devices, entering(): everything = lax.all_gather(array, axis)  200 us
    reduce_scatter x1, waiting for transfers between devices, local(): lax.psum_scatter(product * grad_scale, 'inner', scatter_dimension=0, tile...  81.3 us
    select_n x64, other arithmetic, turn(): return jnp.where(reached, new, before)  78.7 us
    unnamed x71, local copies, waits for them, and re-layouts  36.2 us
    psum x1, waiting for transfers between devices, local(): grad = lax.psum(shares, 'outer')  23.5 us
  transfers between devices with their start and end apart: 5, of which 4 were waited for; matrix products, arithmetic and copies ran while one was open for 21% of the time, Pallas kernels for 0%

commit v1 on v0

v1 whole, which is shorter than its diff:
```python
import functools
import math

import jax
import jax.numpy as jnp
from jax import lax
from jax.experimental import pallas as pl
from jax.experimental.pallas import tpu as pltpu
from jax.sharding import PartitionSpec as P

HD = 128
SUB = 256
PAIR = 2 * HD
VMEM = 40 * 1024 * 1024
F32 = jnp.float32
BF16 = jnp.bfloat16


def mm(a, b, contract):
    return lax.dot_general(a, b, ((contract[:1], contract[1:]), ((), ())), preferred_element_type=F32)


def params():
    return pltpu.CompilerParams(vmem_limit_bytes=VMEM, dimension_semantics=("arbitrary",))


def cost(macs, moved):
    return pl.CostEstimate(flops=2 * macs, bytes_accessed=moved, transcendentals=0)


def states_body(pick, a_ref, b_ref, out_ref):
    for j in range(2):
        cols = slice(j * HD, (j + 1) * HD)
        out_ref[j] = mm(a_ref[:, cols], b_ref[:, cols], (0, 0)).astype(out_ref.dtype)


def states(a, b, pick, dtype):
    rows = a.shape[0]
    n = pick.shape[0]
    spec = pl.BlockSpec((rows, PAIR), lambda s, pick: (0, pick[s]))
    return pl.pallas_call(
        states_body,
        grid_spec=pltpu.PrefetchScalarGridSpec(
            num_scalar_prefetch=1,
            grid=(n,),
            in_specs=[spec, spec],
            out_specs=pl.BlockSpec((2, HD, HD), lambda s, pick: (s, 0, 0)),
        ),
        out_shape=jax.ShapeDtypeStruct((2 * n, HD, HD), dtype),
        compiler_params=params(),
        cost_estimate=cost(n * rows * 2 * HD * HD, 4 * n * rows * PAIR),
    )(pick, a, b)


def key_inside_body(scale, g_ref, q_ref, v_ref, out_ref):
    rows = g_ref.shape[0]
    later = lax.broadcasted_iota(jnp.int32, (SUB, SUB), 1) >= lax.broadcasted_iota(jnp.int32, (SUB, SUB), 0)
    for j in range(2):
        cols = slice(j * HD, (j + 1) * HD)
        state = None
        for b in reversed(range(rows // SUB)):
            here = slice(b * SUB, (b + 1) * SUB)
            g, q, v = g_ref[here, cols], q_ref[here, cols], v_ref[here, cols]
            scores = jnp.where(later, mm(v, g, (1, 1)), 0.0).astype(BF16)
            total = mm(scores, q, (1, 0))
            if state is not None:
                total = total + mm(v, state.astype(BF16), (1, 0))
            out_ref[here, cols] = (total * scale).astype(out_ref.dtype)
            if b:
                term = mm(g, q, (0, 0))
                state = term if state is None else state + term


def key_inside(g, q, v, scale):
    rows, width = g.shape
    spec = pl.BlockSpec((rows, PAIR), lambda s: (0, s))
    return pl.pallas_call(
        functools.partial(key_inside_body, scale),
        grid=(width // PAIR,),
        in_specs=[spec] * 3,
        out_specs=spec,
        out_shape=jax.ShapeDtypeStruct((rows, width), BF16),
        compiler_params=params(),
        cost_estimate=cost(rows * width * (2 * SUB + 2 * HD), 8 * rows * width),
    )(g, q, v)


def head_of(ref_own, ref_oth, other, at):
    return jnp.where(other, ref_oth[at], ref_own[at])


def query_body(scale, half, g_ref, k_ref, v_ref, own_ref, oth_ref, out_ref):
    rows = g_ref.shape[0]
    step = pl.program_id(0)
    heads_half = own_ref.shape[0]
    earlier = lax.broadcasted_iota(jnp.int32, (SUB, SUB), 0) >= lax.broadcasted_iota(jnp.int32, (SUB, SUB), 1)
    for j in range(2):
        cols = slice(j * HD, (j + 1) * HD)
        head = step * 2 + j
        other = (head // heads_half) != half[0]
        state = head_of(own_ref, oth_ref, other, lax.rem(head, heads_half)).astype(F32)
        for b in range(rows // SUB):
            here = slice(b * SUB, (b + 1) * SUB)
            g, k, v = g_ref[here, cols], k_ref[here, cols], v_ref[here, cols]
            scores = jnp.where(earlier, mm(g, v, (1, 1)), 0.0).astype(BF16)
            total = mm(scores, k, (1, 0)) + mm(g, state.astype(BF16), (1, 0))
            out_ref[here, cols] = (total * scale).astype(out_ref.dtype)
            if b + 1 < rows // SUB:
                state = state + mm(v, k, (0, 0))


def query_side(g, k, v, own, oth, half, scale):
    rows, width = g.shape
    spec = pl.BlockSpec((rows, PAIR), lambda s, half: (0, s))
    whole = pl.BlockSpec(own.shape, lambda s, half: (0, 0, 0))
    return pl.pallas_call(
        functools.partial(query_body, scale),
        grid_spec=pltpu.PrefetchScalarGridSpec(
            num_scalar_prefetch=1,
            grid=(width // PAIR,),
            in_specs=[spec] * 3 + [whole] * 2,
            out_specs=spec,
        ),
        out_shape=jax.ShapeDtypeStruct((rows, width), BF16),
        compiler_params=params(),
        cost_estimate=cost(rows * width * (2 * SUB + 2 * HD), 8 * rows * width),
    )(half, g, k, v, own, oth)


def turned_body(parts, place, in_ref, out_ref):
    step = pl.program_id(0)
    turned = in_ref[...].T
    size = turned.shape[0] // parts
    for j in range(parts):
        at = pl.multiple_of(place[step * parts + j] * size, size)
        out_ref[pl.ds(at, size), :] = turned[j * size : (j + 1) * size, :]


def turned_inputs(inputs, place):
    rows, width = inputs.shape
    block = width // place.shape[0]
    cols = max(block, HD)
    return pl.pallas_call(
        functools.partial(turned_body, cols // block),
        grid_spec=pltpu.PrefetchScalarGridSpec(
            num_scalar_prefetch=1,
            grid=(width // cols,),
            in_specs=[pl.BlockSpec((rows, cols), lambda s, place: (0, s))],
            out_specs=pl.BlockSpec((width, rows), lambda s, place: (0, 0)),
        ),
        out_shape=jax.ShapeDtypeStruct((width, rows), BF16),
        compiler_params=params(),
        cost_estimate=cost(0, 4 * rows * width),
    )(place, inputs)


def key_product_body(scale, grad_scale, n_inner, pick, half, *refs):
    inside_ref, v_ref, own_ref, oth_ref, inputs_ref = refs[:5]
    key_ref, p_ref, q_ref = refs[-3:]
    heads_half = own_ref.shape[0]
    quarter = pick[pl.program_id(0)]
    heads = v_ref.shape[1] // HD
    parts = []
    for j in range(heads):
        cols = slice(j * HD, (j + 1) * HD)
        head = quarter * heads + j
        other = (head // heads_half) != half[0]
        state = head_of(own_ref, oth_ref, other, lax.rem(head, heads_half))
        total = inside_ref[:, cols].astype(F32) + mm(v_ref[:, cols], state, (1, 0)) * scale
        parts.append(total.astype(BF16))
    key_grad = jnp.concatenate(parts, 1)
    key_ref[...] = key_grad
    product = (mm(inputs_ref[...], key_grad, (1, 0)) * grad_scale).astype(BF16)
    size = product.shape[0] // n_inner
    for r in range(n_inner):
        p_ref[0, r] = product[r * size : r * size + size // 2]
        q_ref[0, r] = product[r * size + size // 2 : (r + 1) * size]


def key_product(inside, v, own, oth, turned, pick, half, scale, grad_scale, n_inner, n_outer, before):
    rows, width = v.shape
    cols = width // n_outer
    n = pick.shape[0]
    d = turned.shape[0]
    part = d // n_inner // 2
    spec = pl.BlockSpec((rows, cols), lambda s, pick, half: (0, pick[s]))
    whole = pl.BlockSpec(own.shape, lambda s, pick, half: (0, 0, 0))
    in_specs = [spec, spec, whole, whole, pl.BlockSpec((d, rows), lambda s, pick, half: (0, 0))]
    args = [inside, v, own, oth, turned]
    aliases = {}
    if before is not None:
        in_specs.append(pl.BlockSpec(memory_space=pl.ANY))
        args.append(before)
        aliases = {2 + len(args) - 1: 0}
    piece = pl.BlockSpec((1, n_inner, part, cols), lambda s, pick, half: (s, 0, 0, 0))
    return pl.pallas_call(
        functools.partial(key_product_body, scale, grad_scale, n_inner),
        grid_spec=pltpu.PrefetchScalarGridSpec(
            num_scalar_prefetch=2, grid=(n,), in_specs=in_specs, out_specs=[spec, piece, piece]
        ),
        out_shape=[
            jax.ShapeDtypeStruct((rows, width), BF16),
            jax.ShapeDtypeStruct((n, n_inner, part, cols), BF16),
            jax.ShapeDtypeStruct((n, n_inner, part, cols), BF16),
        ],
        input_output_aliases=aliases,
        compiler_params=params(),
        cost_estimate=cost(n * cols * rows * (d + HD), 2 * rows * (d + 4 * n * cols)),
    )(pick, half, *args)


def adam(grad, master, moment1, moment2):
    new_moment1 = 0.9 * moment1 + 0.1 * grad
    new_moment2 = 0.95 * moment2 + 0.05 * grad * grad
    new_master = master - 0.01 * (new_moment1 / (jnp.sqrt(new_moment2) + 1e-08) + 0.1 * master)
    return new_master, new_moment1, new_moment2


def adam_own_body(pick, keep_ref, came_ref, master_ref, m1_ref, m2_ref, grad_ref, weight_ref):
    part = keep_ref.shape[1]
    for j in range(2):
        here = slice(j * part, (j + 1) * part)
        grad = (keep_ref[j].astype(F32) + came_ref[j].astype(F32)).astype(BF16)
        grad_ref[here, :] = grad
        new_master, _, _ = adam(grad.astype(F32), master_ref[here, :], m1_ref[here, :], m2_ref[here, :])
        weight_ref[j] = new_master.astype(BF16)


def adam_own(keep, came, master, moment1, moment2, pick):
    _, part, cols = keep.shape
    rows = 2 * part
    whole = pl.BlockSpec(keep.shape, lambda s, pick: (0, 0, 0))
    state = pl.BlockSpec((rows, cols), lambda s, pick: (0, pick[s]))
    return pl.pallas_call(
        adam_own_body,
        grid_spec=pltpu.PrefetchScalarGridSpec(
            num_scalar_prefetch=1,
            grid=(1,),
            in_specs=[whole, whole, state, state, state],
            out_specs=[pl.BlockSpec((rows, cols), lambda s, pick: (0, 0)), whole],
        ),
        out_shape=[jax.ShapeDtypeStruct((rows, cols), BF16), jax.ShapeDtypeStruct(keep.shape, BF16)],
        compiler_params=params(),
        cost_estimate=cost(rows * cols, 24 * rows * cols),
    )(pick, keep, came, master, moment1, moment2)


def adam_all_body(pick, grad_ref, master_ref, m1_ref, m2_ref, out_ref, out1_ref, out2_ref):
    out_ref[...], out1_ref[...], out2_ref[...] = adam(
        grad_ref[0].astype(F32), master_ref[...], m1_ref[...], m2_ref[...]
    )


def adam_all(grads, master, moment1, moment2, pick):
    n, rows, cols = grads.shape
    state = pl.BlockSpec((rows, cols), lambda s, pick: (0, pick[s]))
    return pl.pallas_call(
        adam_all_body,
        grid_spec=pltpu.PrefetchScalarGridSpec(
            num_scalar_prefetch=1,
            grid=(n,),
            in_specs=[pl.BlockSpec((1, rows, cols), lambda s, pick: (s, 0, 0)), state, state, state],
            out_specs=[state] * 3,
        ),
        out_shape=[jax.ShapeDtypeStruct(master.shape, F32)] * 3,
        compiler_params=params(),
        cost_estimate=cost(n * rows * cols, 26 * n * rows * cols),
    )(pick, grads, master, moment1, moment2)


def assemble_body(pick, p_place, q_place, *refs):
    p_ref, q_ref, out_ref = refs[0], refs[1], refs[-1]
    _, n_inner, part, _ = p_ref.shape
    for r in range(n_inner):
        at = pl.multiple_of(p_place[r] * (2 * part), 2 * part)
        out_ref[pl.ds(at, part), :] = p_ref[0, r]
        at = pl.multiple_of(q_place[r] * (2 * part) + part, part)
        out_ref[pl.ds(at, part), :] = q_ref[0, r]


def assemble(p, q, pick, p_place, q_place, d, width, before):
    n, n_inner, part, cols = p.shape
    piece = pl.BlockSpec((1, n_inner, part, cols), lambda s, *_: (s, 0, 0, 0))
    in_specs = [piece, piece]
    args = [p, q]
    aliases = {}
    if before is not None:
        in_specs.append(pl.BlockSpec(memory_space=pl.ANY))
        args.append(before)
        aliases = {5: 0}
    return pl.pallas_call(
        assemble_body,
        grid_spec=pltpu.PrefetchScalarGridSpec(
            num_scalar_prefetch=3,
            grid=(n,),
            in_specs=in_specs,
            out_specs=pl.BlockSpec((d, cols), lambda s, pick, *_: (0, pick[s])),
        ),
        out_shape=jax.ShapeDtypeStruct((d, width), BF16),
        input_output_aliases=aliases,
        compiler_params=params(),
        cost_estimate=cost(0, 4 * n * d * cols),
    )(pick, p_place, q_place, *args)


def swap(x, axis, bit):
    n = lax.axis_size(axis)
    return lax.ppermute(x, axis, [(i, i ^ (1 << bit)) for i in range(n)])


def bit_of(axis, bit):
    return (lax.axis_index(axis) >> bit) & 1


def bits(axis):
    return (lax.axis_size(axis) - 1).bit_length()


def scan_states(own, oth_sent, reverse):
    side = 0 if reverse else 1
    mine = bit_of("inner", 0) == side
    came = swap(oth_sent, "inner", 0).astype(F32)
    total = own + came
    outside = jnp.zeros_like(own)
    levels = [("inner", b) for b in range(1, bits("inner"))] + [("outer", b) for b in range(bits("outer"))]
    for n, (axis, bit) in enumerate(levels):
        got = swap(total.astype(BF16), axis, bit).astype(F32)
        outside = outside + jnp.where(bit_of(axis, bit) == side, got, 0.0)
        if n + 1 < len(levels):
            total = total + got
    give = (outside + jnp.where(mine, 0.0, own)).astype(BF16)
    back = swap(give, "inner", 0)
    return (outside + jnp.where(mine, came, 0.0)).astype(BF16), back


def reversed_bits(value, n_bits):
    out = 0
    for b in range(n_bits):
        out = out | (((value >> b) & 1) << (n_bits - 1 - b))
    return out


def fold(x, axis_at, axis, bit):
    size = x.shape[axis_at] // 2
    keep = lax.slice_in_dim(x, 0, size, axis=axis_at)
    got = swap(lax.slice_in_dim(x, size, 2 * size, axis=axis_at).astype(BF16), axis, bit)
    return keep.astype(F32) + got.astype(F32)


def local(inputs, queries, keys, values, out_grad, master, moment1, moment2):
    rows_here, width = queries.shape
    d = inputs.shape[1]
    n_outer = lax.axis_size("outer")
    n_inner = lax.axis_size("inner")
    o_bits, i_bits = bits("outer"), bits("inner")
    total_tokens = rows_here * n_outer * n_inner
    att_scale = 1.0 / math.sqrt(HD * total_tokens)
    grad_scale = 1.0 / math.sqrt(total_tokens)
    outer, inner = lax.axis_index("outer"), lax.axis_index("inner")
    y = bit_of("inner", 0)
    half = jnp.reshape(y, (1,)).astype(jnp.int32)
    pairs = width // PAIR
    own_pairs = (jnp.arange(pairs // 2) + y * (pairs // 2)).astype(jnp.int32)
    oth_pairs = (jnp.arange(pairs // 2) + (1 - y) * (pairs // 2)).astype(jnp.int32)

    qg_sent = states(out_grad, queries, oth_pairs, BF16)
    qg_own = states(out_grad, queries, own_pairs, F32)
    qg_mine, qg_other = scan_states(qg_own, qg_sent, True)

    inside = key_inside(out_grad, queries, values, att_scale)
    position = reversed_bits(jnp.arange(n_inner) ^ inner, i_bits).astype(jnp.int32)
    turned = turned_inputs(inputs, position)

    rel = jnp.arange(n_outer // 2, dtype=jnp.int32) * 2
    far = ((rel + 1) ^ outer).astype(jnp.int32)
    near = (rel ^ outer).astype(jnp.int32)
    ends = (half, att_scale, grad_scale, n_inner, n_outer)
    key_grad, p_far, q_far = key_product(inside, values, qg_mine, qg_other, turned, far, *ends, None)
    key_grad, p_near, q_near = key_product(inside, values, qg_mine, qg_other, turned, near, *ends, key_grad)

    p = p_near.astype(F32) + swap(p_far, "outer", 0).astype(F32)
    q = q_near.astype(F32) + swap(q_far, "outer", 0).astype(F32)
    for b in reversed(range(1, o_bits)):
        p = fold(p, 0, "outer", b)
    p = fold(p, 1, "inner", 0)
    q = fold(q, 1, "inner", 0)
    for b in reversed(range(1, o_bits)):
        q = fold(q, 0, "outer", b)
    both = jnp.stack([p[0], q[0]], 0)
    for b in range(1, i_bits - 1):
        both = fold(both, 1, "inner", b)
    keep = both[:, 0]
    came = swap(both[:, 1].astype(BF16), "inner", i_bits - 1)
    mine = jnp.reshape(outer, (1,)).astype(jnp.int32)
    grad, weight = adam_own(keep, came, master, moment1, moment2, mine)

    both = weight[:, None]
    for b in reversed(range(1, i_bits)):
        both = jnp.concatenate([both, swap(both, "inner", b)], 1)
    p, q = both[0][None], both[1][None]
    p = jnp.concatenate([p, swap(p, "inner", 0)], 1)
    for b in range(1, o_bits):
        p = jnp.concatenate([p, swap(p, "outer", b)], 0)
        q = jnp.concatenate([q, swap(q, "outer", b)], 0)
    q = jnp.concatenate([q, swap(q, "inner", 0)], 1)
    p_more, q_more = swap(p, "outer", 0), swap(q, "outer", 0)
    place = (reversed_bits(jnp.arange(n_inner), i_bits) ^ inner).astype(jnp.int32)
    weights = assemble(p, q, near, place, place, d, width, None)
    weights = assemble(p_more, q_more, far, place, place, d, width, weights)

    grads = grad[None]
    for b in range(1, o_bits):
        grads = jnp.concatenate([grads, swap(grads, "outer", b)], 0)
    grads = jnp.concatenate([grads, swap(grads, "outer", 0)], 0)
    new_master, new_moment1, new_moment2 = adam_all(
        grads, master, moment1, moment2, jnp.concatenate([near, far], 0)
    )

    kv_sent = states(values, keys, oth_pairs, BF16)
    kv_own = states(values, keys, own_pairs, F32)
    kv_mine, kv_other = scan_states(kv_own, kv_sent, False)
    query_grad = query_side(out_grad, keys, values, kv_mine, kv_other, half, att_scale)
    return (query_grad, key_grad, new_master, new_moment1, new_moment2, weights)


def solution(mesh):
    tokens = P(("outer", "inner"), None)
    rows = P("inner", None)
    return jax.shard_map(
        local,
        mesh=mesh,
        in_specs=(tokens,) * 5 + (rows,) * 3,
        out_specs=(tokens, tokens, rows, rows, rows, P()),
        check_vma=False,
    )
```

time: 511 us -> 129 us (0.25)
  waiting for transfers between devices: 305 us -> 44 us
  other arithmetic: 86.5 us -> 7.91 us
  local copies, waits for them, and re-layouts: 62.8 us -> 9.07 us
  matrix products: 36.4 us -> 0 us
  starting transfers between devices: 0.38 us -> 33.4 us
  Pallas kernels: 0 us -> 32.8 us
  between operations: 14.1 us -> 1.08 us
    all_gather x3 -> x0, waiting for transfers between devices: 200 us -> none  [the longest x2 200 us: entering(): everything = lax.all_gather(array, axis)]
    reduce_scatter x1 -> x0, waiting for transfers between devices: 81.3 us -> none  [local(): lax.psum_scatter(product * grad_scale, 'inner', scatter_dimension=0, tile...]
    select_n x64 -> x0, other arithmetic: 78.7 us -> none  [turn(): return jnp.where(reached, new, before)]
    ppermute x0 -> x30, waiting for transfers between devices: none -> 44 us  [swap(): return lax.ppermute(x, axis, [(i, i ^ 1 << bit) for i in range(n)])]
    dot_general x17 -> x0, matrix products: 36.4 us -> none  [the longest x2 8.45 us: local(): jnp.einsum('thv,shv->hts', block_gradient, value_block_rows, preferred_el...]
    ppermute x0 -> x30, starting transfers between devices: none -> 33.4 us  [swap(): return lax.ppermute(x, axis, [(i, i ^ 1 << bit) for i in range(n)])]
    pallas_call x0 -> x13, Pallas kernels: none -> 32.8 us  [the longest x1 6.87 us: query_side(): pl.pallas_call(functools.partial(query_body, scale), grid_spec=pltpu.Pref...]
    unnamed x71 -> x34, local copies, waits for them, and re-layouts: 36.2 us -> 8.86 us
  transfers between devices with their start and end apart: 5 -> 30, of which waited for: 4 -> 16; matrix products, arithmetic and copies ran while one was open for 21% -> 6% of each run, Pallas kernels for 0% -> 21%
where the time goes in v1:
time: 129 us; the launch traced here: 128 us
  waiting for transfers between devices  44 us (34%)
  starting transfers between devices  33.4 us (26%)
  Pallas kernels  32.8 us (25%)
  local copies, waits for them, and re-layouts  9.07 us (7%)
  other arithmetic  7.91 us (6%)
    ppermute x30, waiting for transfers between devices, swap(): return lax.ppermute(x, axis, [(i, i ^ 1 << bit) for i in range(n)])  44 us
    ppermute x30, starting transfers between devices, swap(): return lax.ppermute(x, axis, [(i, i ^ 1 << bit) for i in range(n)])  33.4 us
    unnamed x34, local copies, waits for them, and re-layouts  8.86 us
    pallas_call x1, Pallas kernels, query_side(): pl.pallas_call(functools.partial(query_body, scale), grid_spec=pltpu.Pref...  6.87 us
    pallas_call x4, Pallas kernels, states(): pl.pallas_call(states_body, grid_spec=pltpu.PrefetchScalarGridSpec(num_sc...  6.28 us
    pallas_call x2, Pallas kernels, key_product(): pl.pallas_call(functools.partial(key_product_body, scale, grad_scale, n_i...  6 us
    pallas_call x1, Pallas kernels, key_inside(): pl.pallas_call(functools.partial(key_inside_body, scale), grid=(width //...  5.68 us
    convert_element_type x8, other arithmetic, scan_states(): got = swap(total.astype(BF16), axis, bit).astype(F32)  4.15 us
  transfers between devices with their start and end apart: 30, of which 16 were waited for; matrix products, arithmetic and copies ran while one was open for 6% of the time, Pallas kernels for 21%

profile of v1, /device:TPU:0, one launch (start us, length us, event | category | flops | bytes accessed | tf_op | source)
XLA Modules:
  0.0 128.3 jit_solution(11879105062366236945)
XLA Ops:
  5.4 3.0 %collective-permute-start.6 = (bf16[4,128,128]{2,1,0:T(8,128)(2,1)S(1)}, bf16[4,128,128]{2,1,0:T(8,128)(2,1)S(1)}, u32[]{:S(2)}, u32[]{:S(2)}) collective-permute-start(bf16[4,128,128]{2,1,0:T(8,128)(2,1)S(1)} %shard_map.132), channel_id=1, source_target_pairs={{0,1},{1,0},{2,3},{3,2},{4,5},{5,4},{6,7},{7,6},{8,9},{9,8},{10,11... | collective-permute-start | bytes 393224 | tf_op jit(solution)/shard_map/ppermute | solution.py:308
  12.0 1.9 %collective-permute-start.7 = (bf16[4,128,128]{2,1,0:T(8,128)(2,1)S(1)}, bf16[4,128,128]{2,1,0:T(8,128)(2,1)S(1)}, u32[]{:S(2)}, u32[]{:S(2)}) collective-permute-start(bf16[4,128,128]{2,1,0:T(8,128)(2,1)S(1)} %fusion.17), channel_id=1, source_target_pairs={{0,2},{1,3},{2,0},{3,1},{4,6},{5,7},{6,4},{7,5},{8,10},{9,11},{10,... | collective-permute-start | bytes 393224 | tf_op jit(solution)/shard_map/ppermute | solution.py:308
  13.8 3.2 %collective-permute-done.7 = bf16[4,128,128]{2,1,0:T(8,128)(2,1)S(1)} collective-permute-done((bf16[4,128,128]{2,1,0:T(8,128)(2,1)S(1)}, bf16[4,128,128]{2,1,0:T(8,128)(2,1)S(1)}, u32[]{:S(2)}, u32[]{:S(2)}) %collective-permute-start.7) | collective-permute-done | bytes 131104 | tf_op jit(solution)/shard_map/ppermute | solution.py:308
  17.1 2.9 %collective-permute-start.8 = (bf16[4,128,128]{2,1,0:T(8,128)(2,1)S(1)}, bf16[4,128,128]{2,1,0:T(8,128)(2,1)S(1)}, u32[]{:S(2)}, u32[]{:S(2)}) collective-permute-start(bf16[4,128,128]{2,1,0:T(8,128)(2,1)S(1)} %fusion.31), channel_id=1, source_target_pairs={{0,4},{1,5},{2,6},{3,7},{4,0},{5,1},{6,2},{7,3},{8,12},{9,13},{10,... | collective-permute-start | bytes 393224 | tf_op jit(solution)/shard_map/ppermute | solution.py:308
  19.9 4.5 %collective-permute-done.8 = bf16[4,128,128]{2,1,0:T(8,128)(2,1)S(1)} collective-permute-done((bf16[4,128,128]{2,1,0:T(8,128)(2,1)S(1)}, bf16[4,128,128]{2,1,0:T(8,128)(2,1)S(1)}, u32[]{:S(2)}, u32[]{:S(2)}) %collective-permute-start.8) | collective-permute-done | bytes 131104 | tf_op jit(solution)/shard_map/ppermute | solution.py:308
  26.0 1.8 %collective-permute-start.10 = (bf16[4,128,128]{2,1,0:T(8,128)(2,1)S(1)}, bf16[4,128,128]{2,1,0:T(8,128)(2,1)S(1)}, u32[]{:S(2)}, u32[]{:S(2)}) collective-permute-start(bf16[4,128,128]{2,1,0:T(8,128)(2,1)S(1)} %fusion.11), channel_id=1, source_target_pairs={{0,16},{8,24},{16,0},{24,8},{1,17},{9,25},{17,1},{25,9},{2,18},{10... | collective-permute-start | bytes 393224 | tf_op jit(solution)/shard_map/ppermute | solution.py:308
  30.9 5.7 %shard_map.130.refs_0_ = bf16[1024,1024]{1,0:T(8,128)(2,1)S(1)} custom-call(bf16[1024,1024]{1,0:T(8,128)(2,1)S(1)} %copy-done.3, bf16[1024,1024]{1,0:T(8,128)(2,1)S(1)} %copy-done.9, bf16[1024,1024]{1,0:T(8,128)(2,1)S(1)} %copy-done), custom_call_target="tpu_custom_call" | custom-call | flops 1610612736 | bytes 8388608 | tf_op jit(solution)/shard_map/pallas_call | solution.py:77
  38.4 2.1 %shard_map.133.refs_4_ = bf16[1024,1024]{1,0:T(8,128)(2,1)S(1)} custom-call(s32[8]{0:T(128)S(1)} %shift-left_or_fusion.place, bf16[1024,1024]{1,0:T(8,128)(2,1)S(1)} %copy-done.10), custom_call_target="tpu_custom_call" | custom-call | bytes 4194304 | tf_op jit(solution)/shard_map/pallas_call | solution.py:143
  42.1 3.0 %shard_map.134 = (bf16[1024,1024]{1,0:T(8,128)(2,1)}, bf16[2,8,64,256]{3,2,1,0:T(8,128)(2,1)S(1)}, bf16[2,8,64,256]{3,2,1,0:T(8,128)(2,1)S(1)}) custom-call(s32[2]{0:T(128)S(1)} %add_xor_fusion.pick, s32[1]{0:T(128)} %bitcast.half, bf16[1024,1024]{1,0:T(8,128)(2,1)S(1)} %shard_map.130.refs_0_, bf16[1024,1024]{1,0:T(8,128)(2,1)S(1)} %copy-done, ...), custom_call_target="tpu_custom_call" | custom-call | flops 1207959552 | bytes 6291456 | tf_op jit(solution)/shard_map/pallas_call | solution.py:196
  49.9 3.0 %shard_map.135 = (bf16[1024,1024]{1,0:T(8,128)(2,1)}, bf16[2,8,64,256]{3,2,1,0:T(8,128)(2,1)S(1)}, bf16[2,8,64,256]{3,2,1,0:T(8,128)(2,1)S(1)}) custom-call(s32[2]{0:T(128)S(1)} %fusion.29.pick, s32[1]{0:T(128)} %bitcast.half, bf16[1024,1024]{1,0:T(8,128)(2,1)S(1)} %shard_map.130.refs_0_, ...), custom_call_target="tpu_custom_call", output_to_operand_aliasing={{0}: (7, {})} | custom-call | flops 1207959552 | bytes 6291456 | tf_op jit(solution)/shard_map/pallas_call | solution.py:196
  55.8 4.5 %collective-permute-done.16 = bf16[2,4,64,256]{3,2,0,1:T(8,128)(2,1)S(1)} collective-permute-done((bf16[2,4,64,256]{3,2,0,1:T(8,128)(2,1)S(1)}, bf16[2,4,64,256]{3,2,0,1:T(8,128)(2,1)S(1)}, u32[]{:S(2)}, u32[]{:S(2)}) %collective-permute-start.16) | collective-permute-done | bytes 262176 | tf_op jit(solution)/shard_map/ppermute | solution.py:308
  61.1 2.1 %collective-permute-start.14 = (bf16[1,4,64,256]{3,2,0,1:T(8,128)(2,1)S(1)}, bf16[1,4,64,256]{3,2,0,1:T(8,128)(2,1)S(1)}, u32[]{:S(2)}, u32[]{:S(2)}) collective-permute-start(bf16[1,4,64,256]{3,2,0,1:T(8,128)(2,1)S(1)} %slice.99), channel_id=1, source_target_pairs={{0,1},{1,0},{2,3},{3,2},{4,5},{5,4},{6,7},{7,6},{8,9},{9,8},{10,11... | collective-permute-start | bytes 393224 | tf_op jit(solution)/shard_map/ppermute | solution.py:308
  63.2 2.2 %collective-permute-done.17 = bf16[1,4,64,256]{3,2,0,1:T(8,128)(2,1)S(1)} collective-permute-done((bf16[1,4,64,256]{3,2,0,1:T(8,128)(2,1)S(1)}, bf16[1,4,64,256]{3,2,0,1:T(8,128)(2,1)S(1)}, u32[]{:S(2)}, u32[]{:S(2)}) %collective-permute-start.17) | collective-permute-done | bytes 131104 | tf_op jit(solution)/shard_map/ppermute | solution.py:308
  69.0 2.9 %collective-permute-done.18 = bf16[2,2,64,256]{3,2,0,1:T(8,128)(2,1)S(1)} collective-permute-done((bf16[2,2,64,256]{3,2,0,1:T(8,128)(2,1)S(1)}, bf16[2,2,64,256]{3,2,0,1:T(8,128)(2,1)S(1)}, u32[]{:S(2)}, u32[]{:S(2)}) %collective-permute-start.18) | collective-permute-done | bytes 131104 | tf_op jit(solution)/shard_map/ppermute | solution.py:308
  71.9 1.9 %collective-permute-start.19 = (bf16[2,64,256]{2,1,0:T(8,128)(2,1)S(1)}, bf16[2,64,256]{2,1,0:T(8,128)(2,1)S(1)}, u32[]{:S(2)}, u32[]{:S(2)}) collective-permute-start(bf16[2,64,256]{2,1,0:T(8,128)(2,1)S(1)} %fusion.19), channel_id=1, source_target_pairs={{0,4},{1,5},{2,6},{3,7},{4,0},{5,1},{6,2},{7,3},{8,12},{9,13},{10,... | collective-permute-start | bytes 196616 | tf_op jit(solution)/shard_map/ppermute | solution.py:308
  73.8 4.2 %collective-permute-done.19.came_ref = bf16[2,64,256]{2,1,0:T(8,128)(2,1)S(1)} collective-permute-done((bf16[2,64,256]{2,1,0:T(8,128)(2,1)S(1)}, bf16[2,64,256]{2,1,0:T(8,128)(2,1)S(1)}, u32[]{:S(2)}, u32[]{:S(2)}) %collective-permute-start.19) | collective-permute-done | bytes 65568 | tf_op jit(solution)/shard_map/ppermute | solution.py:308
  79.3 6.6 %collective-permute-done.22 = bf16[2,1,64,256]{3,2,1,0:T(8,128)(2,1)} collective-permute-done((bf16[2,1,64,256]{3,2,1,0:T(8,128)(2,1)S(1)}, bf16[2,1,64,256]{3,2,1,0:T(8,128)(2,1)}, u32[]{:S(2)}, u32[]{:S(2)}) %collective-permute-start.22) | collective-permute-done | bytes 65568 | tf_op jit(solution)/shard_map/ppermute | solution.py:308
  89.3 2.5 %collective-permute-done.23 = bf16[2,2,64,256]{3,2,1,0:T(8,128)(2,1)S(1)} collective-permute-done((bf16[2,2,64,256]{3,2,1,0:T(8,128)(2,1)S(1)}, bf16[2,2,64,256]{3,2,1,0:T(8,128)(2,1)S(1)}, u32[]{:S(2)}, u32[]{:S(2)}) %collective-permute-start.23) | collective-permute-done | bytes 131104 | tf_op jit(solution)/shard_map/ppermute | solution.py:308
  97.9 1.8 %collective-permute-start.28 = (bf16[2,4,64,256]{3,2,1,0:T(8,128)(2,1)S(1)}, bf16[2,4,64,256]{3,2,1,0:T(8,128)(2,1)S(1)}, u32[]{:S(2)}, u32[]{:S(2)}) collective-permute-start(bf16[2,4,64,256]{3,2,1,0:T(8,128)(2,1)S(1)} %pad_maximum_fusion.6), channel_id=1, source_target_pairs={{0,1},{1,0},{2,3},{3,2},{4,5},{5,4},{6,7},{7,6},{8,9},{9,8},{10,11... | collective-permute-start | bytes 786440 | tf_op jit(solution)/shard_map/ppermute | solution.py:308
  103.2 3.2 %collective-permute-done.28 = bf16[2,4,64,256]{3,2,1,0:T(8,128)(2,1)S(1)} collective-permute-done((bf16[2,4,64,256]{3,2,1,0:T(8,128)(2,1)S(1)}, bf16[2,4,64,256]{3,2,1,0:T(8,128)(2,1)S(1)}, u32[]{:S(2)}, u32[]{:S(2)}) %collective-permute-start.28) | collective-permute-done | bytes 262176 | tf_op jit(solution)/shard_map/ppermute | solution.py:308
  106.5 1.7 %collective-permute-done.25 = bf16[1,8,64,256]{3,2,1,0:T(8,128)(2,1)S(1)} collective-permute-done((bf16[1,8,64,256]{3,2,1,0:T(8,128)(2,1)S(1)}, bf16[1,8,64,256]{3,2,1,0:T(8,128)(2,1)S(1)}, u32[]{:S(2)}, u32[]{:S(2)}) %collective-permute-start.25) | collective-permute-done | bytes 262176 | tf_op jit(solution)/shard_map/ppermute | solution.py:308
  112.3 3.5 %collective-permute-done.5.oth_ref = bf16[4,128,128]{2,1,0:T(8,128)(2,1)S(1)} collective-permute-done((bf16[4,128,128]{2,1,0:T(8,128)(2,1)S(1)}, bf16[4,128,128]{2,1,0:T(8,128)(2,1)S(1)}, u32[]{:S(2)}, u32[]{:S(2)}) %collective-permute-start.5) | collective-permute-done | bytes 131104 | tf_op jit(solution)/shard_map/ppermute | solution.py:308
  115.7 6.9 %shard_map.129 = bf16[1024,1024]{1,0:T(8,128)(2,1)} custom-call(s32[1]{0:T(128)} %bitcast.half, bf16[1024,1024]{1,0:T(8,128)(2,1)S(1)} %copy-done.4, bf16[1024,1024]{1,0:T(8,128)(2,1)S(1)} %copy-done.6, bf16[1024,1024]{1,0:T(8,128)(2,1)S(1)} %copy-done, bf16[4,128,128]{2,1,0:T(8,128)(2,1)S(1)} %get-tuple-element.31.own_ref, ...), custom_call_target="tpu_custom_call" | custom-call | flops 1610612736 | bytes 8388608 | tf_op jit(solution)/shard_map/pallas_call | solution.py:116
  122.6 2.5 %shard_map.137 = (f32[128,1024]{1,0:T(8,128)}, f32[128,1024]{1,0:T(8,128)}, f32[128,1024]{1,0:T(8,128)}) custom-call(s32[4]{0:T(128)S(1)} %pad_add_fusion.pick, bf16[4,128,256]{2,1,0:T(8,128)(2,1)S(1)} %pad_maximum_fusion.3.grad_ref, f32[128,1024]{1,0:T(8,128)S(1)} %copy-done.11, f32[128,1024]{1,0:T(8,128)S(1)} %copy-done.12, f32[128,1024]{1,0:T(8,128)S(1)} %copy-done.14), custom_call_target="tpu_custom_call" | custom-call | flops 262144 | bytes 3407872 | tf_op jit(solution)/shard_map/pallas_call | solution.py:257
  (125 shorter events, 49.9 us)
Async XLA Ops:
  5.4 6.5 %collective-permute-start.6 = (bf16[4,128,128]{2,1,0:T(8,128)(2,1)S(1)}, bf16[4,128,128]{2,1,0:T(8,128)(2,1)S(1)}, u32[]{:S(2)}, u32[]{:S(2)}) collective-permute-start(bf16[4,128,128]{2,1,0:T(8,128)(2,1)S(1)} %shard_map.132), channel_id=1, source_target_pairs={{0,1},{1,0},{2,3},{3,2},{4,5},{5,4},{6,7},{7,6},{8,9},{9,8},{10,11... | collective-permute-start | bytes 393224 | tf_op jit(solution)/shard_map/ppermute | solution.py:308
  12.0 5.0 %collective-permute-start.7 = (bf16[4,128,128]{2,1,0:T(8,128)(2,1)S(1)}, bf16[4,128,128]{2,1,0:T(8,128)(2,1)S(1)}, u32[]{:S(2)}, u32[]{:S(2)}) collective-permute-start(bf16[4,128,128]{2,1,0:T(8,128)(2,1)S(1)} %fusion.17), channel_id=1, source_target_pairs={{0,2},{1,3},{2,0},{3,1},{4,6},{5,7},{6,4},{7,5},{8,10},{9,11},{10,... | collective-permute-start | bytes 393224 | tf_op jit(solution)/shard_map/ppermute | solution.py:308
  17.1 7.3 %collective-permute-start.8 = (bf16[4,128,128]{2,1,0:T(8,128)(2,1)S(1)}, bf16[4,128,128]{2,1,0:T(8,128)(2,1)S(1)}, u32[]{:S(2)}, u32[]{:S(2)}) collective-permute-start(bf16[4,128,128]{2,1,0:T(8,128)(2,1)S(1)} %fusion.31), channel_id=1, source_target_pairs={{0,4},{1,5},{2,6},{3,7},{4,0},{5,1},{6,2},{7,3},{8,12},{9,13},{10,... | collective-permute-start | bytes 393224 | tf_op jit(solution)/shard_map/ppermute | solution.py:308
  26.0 10.7 %collective-permute-start.10 = (bf16[4,128,128]{2,1,0:T(8,128)(2,1)S(1)}, bf16[4,128,128]{2,1,0:T(8,128)(2,1)S(1)}, u32[]{:S(2)}, u32[]{:S(2)}) collective-permute-start(bf16[4,128,128]{2,1,0:T(8,128)(2,1)S(1)} %fusion.11), channel_id=1, source_target_pairs={{0,16},{8,24},{16,0},{24,8},{1,17},{9,25},{17,1},{25,9},{2,18},{10... | collective-permute-start | bytes 393224 | tf_op jit(solution)/shard_map/ppermute | solution.py:308
  36.8 5.3 %collective-permute-start.11 = (bf16[4,128,128]{2,1,0:T(8,128)(2,1)S(1)}, bf16[4,128,128]{2,1,0:T(8,128)(2,1)S(1)}, u32[]{:S(2)}, u32[]{:S(2)}) collective-permute-start(bf16[4,128,128]{2,1,0:T(8,128)(2,1)S(1)} %get-tuple-element.28), channel_id=1, source_target_pairs={{0,1},{1,0},{2,3},{3,2},{4,5},{5,4},{6,7},{7,6},{8,9},{9,8},{10,11... | collective-permute-start | bytes 393224 | tf_op jit(solution)/shard_map/ppermute | solution.py:308
  45.2 7.7 %collective-permute-start.15 = (bf16[2,8,64,256]{3,2,0,1:T(8,128)(2,1)S(1)}, bf16[2,8,64,256]{3,2,0,1:T(8,128)(2,1)S(1)}, u32[]{:S(2)}, u32[]{:S(2)}) collective-permute-start(bf16[2,8,64,256]{3,2,0,1:T(8,128)(2,1)S(1)} %copy.19), channel_id=1, source_target_pairs={{0,8},{8,0},{16,24},{24,16},{1,9},{9,1},{17,25},{25,17},{2,10},{10... | collective-permute-start | bytes 1572872 | tf_op jit(solution)/shard_map/ppermute | solution.py:308
  45.3 8.3 %collective-permute-start.12 = (bf16[2,8,64,256]{3,2,0,1:T(8,128)(2,1)S(1)}, bf16[2,8,64,256]{3,2,0,1:T(8,128)(2,1)S(1)}, u32[]{:S(2)}, u32[]{:S(2)}) collective-permute-start(bf16[2,8,64,256]{3,2,0,1:T(8,128)(2,1)S(1)} %copy.17), channel_id=1, source_target_pairs={{0,8},{8,0},{16,24},{24,16},{1,9},{9,1},{17,25},{25,17},{2,10},{10... | collective-permute-start | bytes 1572872 | tf_op jit(solution)/shard_map/ppermute | solution.py:308
  48.3 18.6 %collective-permute-start = (bf16[4,128,128]{2,1,0:T(8,128)(2,1)S(1)}, bf16[4,128,128]{2,1,0:T(8,128)(2,1)S(1)}, u32[]{:S(2)}, u32[]{:S(2)}) collective-permute-start(bf16[4,128,128]{2,1,0:T(8,128)(2,1)S(1)} %shard_map.128), channel_id=1, source_target_pairs={{0,1},{1,0},{2,3},{3,2},{4,5},{5,4},{6,7},{7,6},{8,9},{9,8},{10,11... | collective-permute-start | bytes 393224 | tf_op jit(solution)/shard_map/ppermute | solution.py:308
  53.1 7.2 %collective-permute-start.16 = (bf16[2,4,64,256]{3,2,0,1:T(8,128)(2,1)S(1)}, bf16[2,4,64,256]{3,2,0,1:T(8,128)(2,1)S(1)}, u32[]{:S(2)}, u32[]{:S(2)}) collective-permute-start(bf16[2,4,64,256]{3,2,0,1:T(8,128)(2,1)S(1)} %slice.96), channel_id=1, source_target_pairs={{0,1},{1,0},{2,3},{3,2},{4,5},{5,4},{6,7},{7,6},{8,9},{9,8},{10,11... | collective-permute-start | bytes 786440 | tf_op jit(solution)/shard_map/ppermute | solution.py:308
  53.9 7.1 %collective-permute-start.13 = (bf16[1,8,64,256]{3,2,0,1:T(8,128)(2,1)S(1)}, bf16[1,8,64,256]{3,2,0,1:T(8,128)(2,1)S(1)}, u32[]{:S(2)}, u32[]{:S(2)}) collective-permute-start(bf16[1,8,64,256]{3,2,0,1:T(8,128)(2,1)S(1)} %slice.97), channel_id=1, source_target_pairs={{0,16},{8,24},{16,0},{24,8},{1,17},{9,25},{17,1},{25,9},{2,18},{10... | collective-permute-start | bytes 786440 | tf_op jit(solution)/shard_map/ppermute | solution.py:308
  66.2 5.7 %collective-permute-start.18 = (bf16[2,2,64,256]{3,2,0,1:T(8,128)(2,1)S(1)}, bf16[2,2,64,256]{3,2,0,1:T(8,128)(2,1)S(1)}, u32[]{:S(2)}, u32[]{:S(2)}) collective-permute-start(bf16[2,2,64,256]{3,2,0,1:T(8,128)(2,1)S(1)} %fusion.14), channel_id=1, source_target_pairs={{0,2},{1,3},{2,0},{3,1},{4,6},{5,7},{6,4},{7,5},{8,10},{9,11},{10,... | collective-permute-start | bytes 393224 | tf_op jit(solution)/shard_map/ppermute | solution.py:308
  67.6 19.2 %collective-permute-start.1 = (bf16[4,128,128]{2,1,0:T(8,128)(2,1)}, bf16[4,128,128]{2,1,0:T(8,128)(2,1)}, u32[]{:S(2)}, u32[]{:S(2)}) collective-permute-start(bf16[4,128,128]{2,1,0:T(8,128)(2,1)} %fusion.15), channel_id=1, source_target_pairs={{0,2},{1,3},{2,0},{3,1},{4,6},{5,7},{6,4},{7,5},{8,10},{9,11},{10,... | collective-permute-start | bytes 393224 | tf_op jit(solution)/shard_map/ppermute | solution.py:308
  71.9 6.1 %collective-permute-start.19 = (bf16[2,64,256]{2,1,0:T(8,128)(2,1)S(1)}, bf16[2,64,256]{2,1,0:T(8,128)(2,1)S(1)}, u32[]{:S(2)}, u32[]{:S(2)}) collective-permute-start(bf16[2,64,256]{2,1,0:T(8,128)(2,1)S(1)} %fusion.19), channel_id=1, source_target_pairs={{0,4},{1,5},{2,6},{3,7},{4,0},{5,1},{6,2},{7,3},{8,12},{9,13},{10,... | collective-permute-start | bytes 196616 | tf_op jit(solution)/shard_map/ppermute | solution.py:308
  78.2 7.7 %collective-permute-start.22 = (bf16[2,1,64,256]{3,2,1,0:T(8,128)(2,1)S(1)}, bf16[2,1,64,256]{3,2,1,0:T(8,128)(2,1)}, u32[]{:S(2)}, u32[]{:S(2)}) collective-permute-start(bf16[2,1,64,256]{3,2,1,0:T(8,128)(2,1)S(1)} %bitcast.11), channel_id=1, source_target_pairs={{0,4},{1,5},{2,6},{3,7},{4,0},{5,1},{6,2},{7,3},{8,12},{9,13},{10,... | collective-permute-start | bytes 196616 | tf_op jit(solution)/shard_map/ppermute | solution.py:308
  87.8 7.7 %collective-permute-start.2 = (bf16[4,128,128]{2,1,0:T(8,128)(2,1)S(1)}, bf16[4,128,128]{2,1,0:T(8,128)(2,1)S(1)}, u32[]{:S(2)}, u32[]{:S(2)}) collective-permute-start(bf16[4,128,128]{2,1,0:T(8,128)(2,1)S(1)} %fusion.30), channel_id=1, source_target_pairs={{0,4},{1,5},{2,6},{3,7},{4,0},{5,1},{6,2},{7,3},{8,12},{9,13},{10,... | collective-permute-start | bytes 393224 | tf_op jit(solution)/shard_map/ppermute | solution.py:308
  92.7 5.2 %collective-permute-start.27 = (bf16[1,4,64,256]{3,2,1,0:T(8,128)(2,1)S(1)}, bf16[1,4,64,256]{3,2,1,0:T(8,128)(2,1)S(1)}, u32[]{:S(2)}, u32[]{:S(2)}) collective-permute-start(bf16[1,4,64,256]{3,2,1,0:T(8,128)(2,1)S(1)} %get-tuple-element.32), channel_id=1, source_target_pairs={{0,16},{8,24},{16,0},{24,8},{1,17},{9,25},{17,1},{25,9},{2,18},{10... | collective-permute-start | bytes 393224 | tf_op jit(solution)/shard_map/ppermute | solution.py:308
  94.2 5.5 %collective-permute-start.24 = (bf16[1,4,64,256]{3,2,1,0:T(8,128)(2,1)S(1)}, bf16[1,4,64,256]{3,2,1,0:T(8,128)(2,1)S(1)}, u32[]{:S(2)}, u32[]{:S(2)}) collective-permute-start(bf16[1,4,64,256]{3,2,1,0:T(8,128)(2,1)S(1)} %get-tuple-element.33), channel_id=1, source_target_pairs={{0,1},{1,0},{2,3},{3,2},{4,5},{5,4},{6,7},{7,6},{8,9},{9,8},{10,11... | collective-permute-start | bytes 393224 | tf_op jit(solution)/shard_map/ppermute | solution.py:308
  96.7 6.4 %collective-permute-start.20 = (bf16[1,128,256]{2,1,0:T(8,128)(2,1)S(1)}, bf16[1,128,256]{2,1,0:T(8,128)(2,1)S(1)}, u32[]{:S(2)}, u32[]{:S(2)}) collective-permute-start(bf16[1,128,256]{2,1,0:T(8,128)(2,1)S(1)} %bitcast.8), channel_id=1, source_target_pairs={{0,16},{8,24},{16,0},{24,8},{1,17},{9,25},{17,1},{25,9},{2,18},{10... | collective-permute-start | bytes 196616 | tf_op jit(solution)/shard_map/ppermute | solution.py:308
  97.9 8.4 %collective-permute-start.28 = (bf16[2,4,64,256]{3,2,1,0:T(8,128)(2,1)S(1)}, bf16[2,4,64,256]{3,2,1,0:T(8,128)(2,1)S(1)}, u32[]{:S(2)}, u32[]{:S(2)}) collective-permute-start(bf16[2,4,64,256]{3,2,1,0:T(8,128)(2,1)S(1)} %pad_maximum_fusion.6), channel_id=1, source_target_pairs={{0,1},{1,0},{2,3},{3,2},{4,5},{5,4},{6,7},{7,6},{8,9},{9,8},{10,11... | collective-permute-start | bytes 786440 | tf_op jit(solution)/shard_map/ppermute | solution.py:308
  99.7 8.5 %collective-permute-start.25 = (bf16[1,8,64,256]{3,2,1,0:T(8,128)(2,1)S(1)}, bf16[1,8,64,256]{3,2,1,0:T(8,128)(2,1)S(1)}, u32[]{:S(2)}, u32[]{:S(2)}) collective-permute-start(bf16[1,8,64,256]{3,2,1,0:T(8,128)(2,1)S(1)} %pad_maximum_fusion.5), channel_id=1, source_target_pairs={{0,16},{8,24},{16,0},{24,8},{1,17},{9,25},{17,1},{25,9},{2,18},{10... | collective-permute-start | bytes 786440 | tf_op jit(solution)/shard_map/ppermute | solution.py:308
  101.9 7.7 %collective-permute-start.4 = (bf16[4,128,128]{2,1,0:T(8,128)(2,1)S(1)}, bf16[4,128,128]{2,1,0:T(8,128)(2,1)S(1)}, u32[]{:S(2)}, u32[]{:S(2)}) collective-permute-start(bf16[4,128,128]{2,1,0:T(8,128)(2,1)S(1)} %fusion.5), channel_id=1, source_target_pairs={{0,16},{8,24},{16,0},{24,8},{1,17},{9,25},{17,1},{25,9},{2,18},{10... | collective-permute-start | bytes 393224 | tf_op jit(solution)/shard_map/ppermute | solution.py:308
  103.1 9.1 %collective-permute-start.21 = (bf16[2,128,256]{2,1,0:T(8,128)(2,1)S(1)}, bf16[2,128,256]{2,1,0:T(8,128)(2,1)S(1)}, u32[]{:S(2)}, u32[]{:S(2)}) collective-permute-start(bf16[2,128,256]{2,1,0:T(8,128)(2,1)S(1)} %pad_maximum_fusion.7), channel_id=1, source_target_pairs={{0,8},{8,0},{16,24},{24,16},{1,9},{9,1},{17,25},{25,17},{2,10},{10... | collective-permute-start | bytes 393224 | tf_op jit(solution)/shard_map/ppermute | solution.py:308
  106.4 20.3 %collective-permute-start.29 = (bf16[2,8,64,256]{3,2,1,0:T(8,128)(2,1)S(1)}, bf16[2,8,64,256]{3,2,1,0:T(8,128)(2,1)S(1)}, u32[]{:S(2)}, u32[]{:S(2)}) collective-permute-start(bf16[2,8,64,256]{3,2,1,0:T(8,128)(2,1)S(1)} %pad_maximum_fusion.1.refs_1_), channel_id=1, source_target_pairs={{0,8},{8,0},{16,24},{24,16},{1,9},{9,1},{17,25},{25,17},{2,10},{10... | collective-permute-start | bytes 1572872 | tf_op jit(solution)/shard_map/ppermute | solution.py:308
  108.3 18.5 %collective-permute-start.26 = (bf16[2,8,64,256]{3,2,1,0:T(8,128)(2,1)S(1)}, bf16[2,8,64,256]{3,2,1,0:T(8,128)(2,1)S(1)}, u32[]{:S(2)}, u32[]{:S(2)}) collective-permute-start(bf16[2,8,64,256]{3,2,1,0:T(8,128)(2,1)S(1)} %pad_maximum_fusion.refs_0_), channel_id=1, source_target_pairs={{0,8},{8,0},{16,24},{24,16},{1,9},{9,1},{17,25},{25,17},{2,10},{10... | collective-permute-start | bytes 1572872 | tf_op jit(solution)/shard_map/ppermute | solution.py:308
  (23 other events, 182.8 us)

commit v2 on v0

v2 whole, which is shorter than its diff:
```python
import functools
import math

import jax
import jax.numpy as jnp
from jax import lax
from jax.experimental import pallas as pl
from jax.experimental.pallas import tpu as pltpu
from jax.sharding import PartitionSpec as P

HD = 128
SUB = 256
PAIR = 2 * HD
VMEM = 16 * 1024 * 1024
F32 = jnp.float32
BF16 = jnp.bfloat16
WHOLE = pl.BlockSpec(memory_space=pltpu.VMEM)
HBM = pl.BlockSpec(memory_space=pltpu.HBM)


def mm(a, b, contract):
    return lax.dot_general(a, b, ((contract[:1], contract[1:]), ((), ())), preferred_element_type=F32)


def far(x):
    return pltpu.with_memory_space_constraint(x, pltpu.HBM)


def call(body, args, specs, outs, macs=0, moved=0, scratch=(), aliases=None):
    args = [far(a) if spec is HBM else a for a, spec in zip(args, specs)]
    return pl.pallas_call(
        body,
        in_specs=specs,
        out_specs=[WHOLE if near else HBM for _, _, near in outs],
        out_shape=[(jax.ShapeDtypeStruct if near else pltpu.HBM)(shape, dtype) for shape, dtype, near in outs],
        scratch_shapes=list(scratch),
        input_output_aliases=aliases or {},
        compiler_params=pltpu.CompilerParams(vmem_limit_bytes=VMEM),
        cost_estimate=pl.CostEstimate(flops=2 * macs, bytes_accessed=moved, transcendentals=0),
    )(*args)


def dma(n):
    return pltpu.SemaphoreType.DMA((n,))


def tie(x, *after):
    return lax.optimization_barrier((x, *after))[0] if after else x


class Here:
    def __init__(self, n_outer, n_inner):
        self.i_bits, self.o_bits = (n_inner - 1).bit_length(), (n_outer - 1).bit_length()
        self.n_outer, self.n_inner = n_outer, n_inner

    def group(self, k):
        return lax.axis_index("outer") ^ k

    def block(self, p):
        return lax.axis_index("inner") ^ reversed_bits(p, self.i_bits)

    def position(self, block):
        return reversed_bits(lax.axis_index("inner") ^ block, self.i_bits)

    def bit(self, axis, b):
        return (lax.axis_index(axis) >> b) & 1

    def y(self):
        return self.bit("inner", 0)


def states_body(at, a_hbm, b_hbm, out_ref, a_buf, b_buf, a_sem, b_sem):
    chunks, rows, cols = a_buf.shape
    at = pl.multiple_of((1 - at.y()) * cols, cols)
    copies = []
    for c in range(chunks):
        here = (pl.ds(c * rows, rows), pl.ds(at, cols))
        pair = (
            pltpu.make_async_copy(a_hbm.at[here], a_buf.at[c], a_sem.at[c]),
            pltpu.make_async_copy(b_hbm.at[here], b_buf.at[c], b_sem.at[c]),
        )
        for copy in pair:
            copy.start()
        copies.append(pair)
    sums = [None] * (cols // HD)
    for c in range(chunks):
        for copy in copies[c]:
            copy.wait()
        for j in range(cols // HD):
            here = slice(j * HD, (j + 1) * HD)
            term = mm(a_buf[c, :, here], b_buf[c, :, here], (0, 0))
            sums[j] = term if c == 0 else sums[j] + term
    for j in range(cols // HD):
        out_ref[j] = sums[j].astype(out_ref.dtype)


def states(a, b, at, dtype):
    rows, width = a.shape
    cols = width // 2
    chunks = rows // SUB
    buf = pltpu.VMEM((chunks, SUB, cols), BF16)
    return call(
        functools.partial(states_body, at),
        [a, b],
        [HBM, HBM],
        [((cols // HD, HD, HD), dtype, True)],
        rows * cols * HD,
        4 * rows * cols,
        [buf, buf, dma(chunks), dma(chunks)],
    )[0]


def sums_of(a_ref, b_ref, at, cols, blocks, wait):
    sums = [None] * (cols // HD)
    for b in blocks:
        wait(b)
        for j in range(cols // HD):
            here = (pl.ds(b * SUB, SUB), pl.ds(pl.multiple_of(at * cols + j * HD, HD), HD))
            term = mm(a_ref[here], b_ref[here], (0, 0))
            sums[j] = term if sums[j] is None else sums[j] + term
    return sums


def load_body(n_load, at, *refs):
    sources, out_ref, loads, sem = refs[:n_load], refs[n_load], refs[n_load + 1 : -1], refs[-1]
    rows, width = sources[0].shape
    blocks = rows // SUB
    copies = []
    for b in range(blocks):
        copies.append([])
        for n in range(n_load):
            here = pl.ds(b * SUB, SUB)
            copy = pltpu.make_async_copy(sources[n].at[here, :], loads[n].at[here, :], sem.at[n_load * b + n])
            copy.start()
            copies[b].append(copy)

    def wait(b):
        for copy in copies[b]:
            copy.wait()

    for j, total in enumerate(sums_of(loads[0], loads[1], at.y(), width // 2, range(blocks), wait)):
        out_ref[j] = total


def load(sources, at):
    rows, width = sources[0].shape
    n = len(sources)
    return call(
        functools.partial(load_body, n, at),
        sources,
        [HBM] * n,
        [((width // 2 // HD, HD, HD), F32, True)] + [((rows, width), BF16, True)] * n,
        rows * width // 2 * HD,
        4 * n * rows * width,
        [dma(n * (rows // SUB))],
    )


def both_states_body(at, a_ref, b_hbm, sent_ref, own_ref, b_ref, sem):
    rows, width = a_ref.shape
    blocks = rows // SUB
    copies = []
    for b in range(blocks):
        here = pl.ds(b * SUB, SUB)
        copies.append(pltpu.make_async_copy(b_hbm.at[here, :], b_ref.at[here, :], sem.at[b]))
        copies[b].start()
    for side, ref in ((1 - at.y(), sent_ref), (at.y(), own_ref)):
        wait = (lambda b: copies[b].wait()) if ref is sent_ref else (lambda b: None)
        for j, total in enumerate(sums_of(a_ref, b_ref, side, width // 2, range(blocks), wait)):
            ref[j] = total.astype(ref.dtype)


def both_states(a, b, at):
    rows, width = a.shape
    shape = (width // 2 // HD, HD, HD)
    return call(
        functools.partial(both_states_body, at),
        [a, b],
        [WHOLE, HBM],
        [(shape, BF16, True), (shape, F32, True)],
        rows * width * HD,
        2 * rows * width,
        [pltpu.VMEM((rows, width), BF16), dma(rows // SUB)],
    )


def key_inside_body(scale, picks, here_at, g_ref, q_ref, v_ref, out_ref):
    n = len(picks)
    rows, cols = out_ref.shape[0], out_ref.shape[1] // n
    later = lax.broadcasted_iota(jnp.int32, (SUB, SUB), 1) >= lax.broadcasted_iota(jnp.int32, (SUB, SUB), 0)
    for s in range(n):
        for j in range(cols // HD):
            at = pl.ds(pl.multiple_of(here_at.group(picks[s]) * cols + j * HD, HD), HD)
            to = s * cols + j * HD
            state = None
            for b in reversed(range(rows // SUB)):
                here = (pl.ds(b * SUB, SUB), at)
                g, q, v = g_ref[here], q_ref[here], v_ref[here]
                scores = jnp.where(later, mm(v, g, (1, 1)), 0.0).astype(BF16)
                total = mm(scores, q, (1, 0))
                if state is not None:
                    total = total + mm(v, state.astype(BF16), (1, 0))
                out_ref[b * SUB : (b + 1) * SUB, to : to + HD] = total * scale
                if b:
                    term = mm(g, q, (0, 0))
                    state = term if state is None else state + term


def key_inside(g, q, v, at, picks, scale, cols):
    rows = g.shape[0]
    n = len(picks)
    return call(
        functools.partial(key_inside_body, scale, picks, at),
        [g, q, v],
        [WHOLE] * 3,
        [((rows, n * cols), F32, True)],
        rows * n * cols * (2 * SUB + 2 * HD),
        10 * rows * n * cols,
    )[0]


def head_of(ref_own, ref_oth, other, at):
    return jnp.where(other, ref_oth[at], ref_own[at])


def query_body(scale, first, count, at, g_ref, k_ref, v_ref, own_ref, oth_ref, *refs):
    out_hbm, buf, sem = refs[-3:]
    rows = g_ref.shape[0]
    heads_half = own_ref.shape[0]
    earlier = lax.broadcasted_iota(jnp.int32, (SUB, SUB), 0) >= lax.broadcasted_iota(jnp.int32, (SUB, SUB), 1)
    copies = []
    for n in range(count):
        for j in range(2):
            head = (first + n) * 2 + j
            cols = slice(head * HD, (head + 1) * HD)
            other = jnp.int32(head // heads_half) != at.y()
            state = head_of(own_ref, oth_ref, other, head % heads_half).astype(F32)
            for b in range(rows // SUB):
                here = slice(b * SUB, (b + 1) * SUB)
                g, k, v = g_ref[here, cols], k_ref[here, cols], v_ref[here, cols]
                scores = jnp.where(earlier, mm(g, v, (1, 1)), 0.0).astype(BF16)
                total = mm(scores, k, (1, 0)) + mm(g, state.astype(BF16), (1, 0))
                buf[n, here, j * HD : (j + 1) * HD] = (total * scale).astype(BF16)
                if b + 1 < rows // SUB:
                    state = state + mm(v, k, (0, 0))
        copy = pltpu.make_async_copy(buf.at[n], out_hbm.at[:, pl.ds((first + n) * PAIR, PAIR)], sem.at[n])
        copy.start()
        copies.append(copy)
    for copy in copies:
        copy.wait()


def query_side(g, k, v, own, oth, at, scale, first, count, before):
    rows, width = g.shape
    more = [] if before is None else [before]
    return call(
        functools.partial(query_body, scale, first, count, at),
        [g, k, v, own, oth] + more,
        [WHOLE] * 5 + [HBM] * len(more),
        [((rows, width), BF16, False)],
        rows * count * PAIR * (2 * SUB + 2 * HD),
        8 * rows * count * PAIR,
        [pltpu.VMEM((count, rows, PAIR), BF16), dma(count)],
        {5: 0} if more else None,
    )[0]


def turned_body(here_at, in_hbm, out_ref, buf, sem):
    size = out_ref.shape[0] // here_at.n_inner
    cols = max(size, HD)
    copies = []
    for n in range(out_ref.shape[0] // cols):
        copy = pltpu.make_async_copy(in_hbm.at[:, pl.ds(n * cols, cols)], buf.at[n], sem.at[n])
        copy.start()
        copies.append(copy)
    for n, copy in enumerate(copies):
        copy.wait()
        turned = buf[n].T
        for j in range(cols // size):
            at = pl.multiple_of(here_at.position(n * (cols // size) + j) * size, size)
            out_ref[pl.ds(at, size), :] = turned[j * size : (j + 1) * size, :]


def turned_inputs(inputs, at):
    rows, width = inputs.shape
    cols = max(width // at.n_inner, HD)
    return call(
        functools.partial(turned_body, at),
        [inputs],
        [HBM],
        [((width, rows), BF16, True)],
        0,
        4 * rows * width,
        [pltpu.VMEM((width // cols, rows, cols), BF16), dma(width // cols)],
    )[0]


def key_product_body(scale, grad_scale, n_inner, picks, here_at, *refs):
    inside_ref, v_ref, own_ref, oth_ref, turned_ref = refs[:5]
    key_hbm, p_ref, q_ref, buf, sem = refs[-5:]
    n = len(picks)
    heads_half = own_ref.shape[0]
    cols = inside_ref.shape[1] // n
    heads = cols // HD
    copies = []
    for s in range(n):
        group = here_at.group(picks[s])
        for j in range(heads):
            here = slice(s * cols + j * HD, s * cols + (j + 1) * HD)
            head = group * heads + j
            other = (head // heads_half) != here_at.y()
            state = head_of(own_ref, oth_ref, other, lax.rem(head, heads_half))
            part = mm(v_ref[:, pl.ds(pl.multiple_of(head * HD, HD), HD)], state, (1, 0))
            buf[s, :, j * HD : (j + 1) * HD] = (inside_ref[:, here] + part * scale).astype(BF16)
        at = pl.ds(pl.multiple_of(group * cols, cols), cols)
        copy = pltpu.make_async_copy(buf.at[s], key_hbm.at[:, at], sem.at[s])
        copy.start()
        copies.append(copy)
    for s in range(n):
        product = (mm(turned_ref[...], buf[s], (1, 0)) * grad_scale).astype(BF16)
        size = product.shape[0] // n_inner
        for r in range(n_inner):
            p_ref[s, r] = product[r * size : r * size + size // 2]
            q_ref[s, r] = product[r * size + size // 2 : (r + 1) * size]
    for copy in copies:
        copy.wait()


def key_product(inside, v, own, oth, turned, picks, at, scale, grad_scale, n_inner, before):
    n = len(picks)
    rows, width = v.shape
    cols = inside.shape[1] // n
    d = turned.shape[0]
    piece = ((n, n_inner, d // n_inner // 2, cols), BF16, True)
    more = [] if before is None else [before]
    return call(
        functools.partial(key_product_body, scale, grad_scale, n_inner, picks, at),
        [inside, v, own, oth, turned] + more,
        [WHOLE] * 5 + [HBM] * len(more),
        [((rows, width), BF16, False), piece, piece],
        n * cols * rows * (d + HD),
        2 * rows * (d + 4 * n * cols),
        [pltpu.VMEM((n, rows, cols), BF16), dma(n)],
        {5: 0} if more else None,
    )


def adam(grad, master, moment1, moment2):
    new_moment1 = 0.9 * moment1 + 0.1 * grad
    new_moment2 = 0.95 * moment2 + 0.05 * grad * grad
    new_master = master - 0.01 * (new_moment1 / (jnp.sqrt(new_moment2) + 1e-08) + 0.1 * master)
    return new_master, new_moment1, new_moment2


def adam_own_body(at, keep_ref, came_ref, master_ref, m1_ref, m2_ref, grad_ref, weight_ref):
    _, _, part, size = keep_ref.shape
    cols = pl.ds(pl.multiple_of(at.group(0) * size, size), size)
    for j in range(2):
        here = slice(j * part, (j + 1) * part)
        grad = (keep_ref[j, 0] + came_ref[j, 0].astype(F32)).astype(BF16)
        grad_ref[here, :] = grad
        new_master, _, _ = adam(grad.astype(F32), master_ref[here, cols], m1_ref[here, cols], m2_ref[here, cols])
        weight_ref[j, 0] = new_master.astype(BF16)


def adam_own(keep, came, master, moment1, moment2, at):
    _, _, part, cols = keep.shape
    return call(
        functools.partial(adam_own_body, at),
        [keep, came, master, moment1, moment2],
        [WHOLE] * 5,
        [((2 * part, cols), BF16, True), (keep.shape, BF16, True)],
        2 * part * cols,
        48 * part * cols,
    )


def adam_all_body(picks, at, *refs):
    n = len(picks)
    grads, (master_ref, m1_ref, m2_ref) = refs[:n], refs[n : n + 3]
    outs, bufs, sem = refs[n + 3 : n + 6], refs[n + 6 : n + 9], refs[n + 9]
    size = grads[0].shape[1]
    copies = []
    for s in range(n):
        cols = pl.ds(pl.multiple_of(at.group(picks[s]) * size, size), size)
        new = adam(grads[s][...].astype(F32), master_ref[:, cols], m1_ref[:, cols], m2_ref[:, cols])
        for i in range(3):
            bufs[i][s] = new[i]
            copy = pltpu.make_async_copy(bufs[i].at[s], outs[i].at[:, cols], sem.at[s * 3 + i])
            copy.start()
            copies.append(copy)
    for copy in copies:
        copy.wait()


def adam_all(grads, master, moment1, moment2, at, picks):
    n = len(grads)
    rows, cols = grads[0].shape
    return call(
        functools.partial(adam_all_body, picks, at),
        [*grads, master, moment1, moment2],
        [WHOLE] * (n + 3),
        [(master.shape, F32, False)] * 3,
        n * rows * cols,
        26 * n * rows * cols,
        [pltpu.VMEM((n, rows, cols), F32)] * 3 + [dma(3 * n)],
    )


def assemble_body(kinds, at, *refs):
    n = len(kinds)
    pieces, bufs = refs[:n], refs[-n - 1 : -1]
    out_hbm, sem = refs[-n - 2], refs[-1]
    copies = []
    for i, (which, groups, start, count) in enumerate(kinds):
        size = pieces[i].shape[-1]
        for s, k in enumerate(groups):
            cols = pl.ds(pl.multiple_of(at.group(k) * size, size), size)
            for r in range(count):
                block = at.block(start + r)
                if which:
                    bufs[i][s, block // 2] = pieces[i][s, r]
                else:
                    bufs[i][s, block // 2, block % 2] = pieces[i][s, r]
            if which:
                goal = out_hbm.at[:, at.block(start) % 2, which, :, cols]
            else:
                goal = out_hbm.at[:, :, which, :, cols]
            copy = pltpu.make_async_copy(bufs[i].at[s], goal, sem.at[2 * i + s])
            copy.start()
            copies.append(copy)
    for copy in copies:
        copy.wait()


def assemble(pieces, at, before, width):
    n_inner = at.n_inner
    part, cols = pieces[0][0].shape[2:]
    kinds = [kind for _, kind in pieces]
    bufs = [
        pltpu.VMEM((len(groups), n_inner // 2) + (() if which else (2,)) + (part, cols), BF16)
        for which, groups, _, _ in kinds
    ]
    more = [] if before is None else [before]
    return call(
        functools.partial(assemble_body, kinds, at),
        [array for array, _ in pieces] + more,
        [WHOLE] * len(pieces) + [HBM] * len(more),
        [((n_inner // 2, 2, 2, part, width), BF16, False)],
        0,
        4 * sum(array.size for array, _ in pieces),
        bufs + [dma(2 * len(pieces))],
        {len(pieces): 0} if more else None,
    )[0]


def swap(x, axis, bit):
    n = lax.axis_size(axis)
    return lax.ppermute(x, axis, [(i, i ^ (1 << bit)) for i in range(n)])


def reversed_bits(value, n_bits):
    out = 0
    for b in range(n_bits):
        out = out | (((value >> b) & 1) << (n_bits - 1 - b))
    return out


def step_body(level, side, at, total_ref, got_ref, *refs):
    total_out, send_out, outside_out = refs[-3:]
    got = got_ref[...].astype(F32)
    total = total_ref[...] + got
    total_out[...] = total
    send_out[...] = total.astype(BF16)
    if level is None:
        outside_out[...] = jnp.zeros_like(got)
    else:
        outside_out[...] = refs[0][...] + jnp.where(at.bit(*level) == side, got, 0.0)


def step(level, side, at, total, got, *outside):
    outs = [(total.shape, F32, True), (total.shape, BF16, True), (total.shape, F32, True)]
    body = functools.partial(step_body, level, side, at)
    return call(body, [total, got, *outside], [WHOLE] * (2 + len(outside)), outs)


def last_body(level, side, at, outside_ref, got_ref, own_ref, came_ref, give_out, out):
    outside = outside_ref[...] + jnp.where(at.bit(*level) == side, got_ref[...].astype(F32), 0.0)
    mine = at.y() == side
    give_out[...] = (outside + jnp.where(mine, 0.0, own_ref[...])).astype(BF16)
    out[...] = (outside + jnp.where(mine, came_ref[...].astype(F32), 0.0)).astype(BF16)


def last(level, side, at, outside, got, own, came):
    outs = [(own.shape, BF16, True)] * 2
    return call(functools.partial(last_body, level, side, at), [outside, got, own, came], [WHOLE] * 4, outs)


def scan_states(own, sent, reverse, at):
    side = 0 if reverse else 1
    came = swap(sent, "inner", 0)
    after = yield came
    own = own()
    total, send, outside = step(None, side, at, own, came)
    levels = [("inner", b) for b in range(1, at.i_bits)] + [("outer", b) for b in range(at.o_bits)]
    for n, level in enumerate(levels):
        got = swap(tie(send, *after), *level)
        after = yield got
        if n + 1 < len(levels):
            total, send, outside = step(level, side, at, total, got, outside)
    give, kept = last(levels[-1], side, at, outside, got, own, came)
    back = swap(tie(give, *after), "inner", 0)
    yield kept, back


def fold(keep, got, axis):
    size = keep.shape[axis] // 2
    low, high = [
        lax.slice_in_dim(keep, at, at + size, axis=axis).astype(F32)
        + lax.slice_in_dim(got, at, at + size, axis=axis).astype(F32)
        for at in (0, size)
    ]
    return high.astype(BF16), low


def merge(p_keep, p_got, q_keep, q_got):
    (p_send, p), (q_send, q) = fold(p_keep, p_got, 1), fold(q_keep, q_got, 1)
    return jnp.concatenate([p_send, q_send], 0), jnp.concatenate([p, q], 0)


def join_body(axis, a_ref, b_ref, out):
    size = a_ref.shape[axis]
    for side, ref in enumerate((a_ref, b_ref)):
        at = tuple(pl.ds(side * size, size) if a == axis else slice(None) for a in range(len(ref.shape)))
        out[at] = ref[...]


def join(a, b, axis):
    shape = tuple(2 * s if i == axis else s for i, s in enumerate(a.shape))
    return call(functools.partial(join_body, axis), [a, b], [WHOLE] * 2, [(shape, BF16, True)])[0]


def split_body(a_ref, b_ref, p_out, q_out):
    n = a_ref.shape[1]
    for i, out in enumerate((p_out, q_out)):
        out[:, :n] = a_ref[i : i + 1]
        out[:, n:] = b_ref[i : i + 1]


def split(a, b):
    _, n, part, cols = a.shape
    return call(split_body, [a, b], [WHOLE] * 2, [((1, 2 * n, part, cols), BF16, True)] * 2)


def local(inputs, queries, keys, values, out_grad, master, moment1, moment2):
    rows_here, width = queries.shape
    d = inputs.shape[1]
    n_outer = lax.axis_size("outer")
    n_inner = lax.axis_size("inner")
    at = Here(n_outer, n_inner)
    i_bits = at.i_bits
    assert n_outer == 4 and i_bits >= 2
    total_tokens = rows_here * n_outer * n_inner
    att_scale = 1.0 / math.sqrt(HD * total_tokens)
    grad_scale = 1.0 / math.sqrt(total_tokens)
    cols = width // n_outer
    near, far_ = tuple(range(0, n_outer, 2)), tuple(range(1, n_outer, 2))

    qg_sent = states(out_grad, queries, at, BF16)
    loaded = []

    def own_states():
        loaded.extend(load([out_grad, queries, values], at))
        return loaded[0]

    qg = scan_states(own_states, qg_sent, True, at)
    next(qg)
    qg.send([])
    g, q, v = loaded[1:]
    inside_far = key_inside(g, q, v, at, far_, att_scale, cols)
    done = [inside_far]
    turned = inside_near = None
    for _ in range(2, i_bits):
        qg.send(done)
        done = []
        if turned is None:
            inside_near = key_inside(tie(g, inside_far), q, v, at, near, att_scale, cols)
            turned = turned_inputs(tie(inputs, inside_far), at)
            done = [inside_near, turned]
    qg.send(done)
    qg.send([])
    kv_sent, kv_own = both_states(tie(v, inside_near, turned), keys, at)
    qg_mine, qg_other = qg.send([kv_own])
    kv = scan_states(lambda: kv_own, kv_sent, False, at)
    kv_got = next(kv)
    kv_stages = i_bits + 2

    def kv_next(*after):
        nonlocal kv_stages, kv_got
        if kv_stages:
            kv_stages -= 1
            kv_got = kv.send(list(after))
        return kv_got

    ends = (at, att_scale, grad_scale, n_inner)
    key_grad, p_far, q_far = key_product(inside_far, v, qg_mine, qg_other, turned, far_, *ends, None)
    p_got, q_got = swap(p_far, "outer", 0), swap(q_far, "outer", 0)
    key_grad, p, q = key_product(inside_near, v, qg_mine, qg_other, turned, near, *ends, key_grad)

    p_send, p = fold(p, p_got, 0)
    q_send, q = fold(q, q_got, 1)
    p_got, q_got = swap(p_send, "outer", 1), swap(q_send, "inner", 0)
    kv_next(p_send, q_send)
    p_send, p = fold(p, p_got, 1)
    q_send, q = fold(q, q_got, 0)
    p_got, q_got = swap(p_send, "inner", 0), swap(q_send, "outer", 1)
    kv_next(p_send, q_send)
    send, keep = merge(p, p_got, q, q_got)
    for b in range(1, i_bits):
        got = swap(send, "inner", b)
        if b + 1 < i_bits:
            send, keep = fold(keep, got, 1)
            kv_next(send)
    while kv_stages > 1:
        kv_next(send)
    grad, weight = adam_own(keep, got, master, moment1, moment2, at)
    kv_mine, kv_other = kv_next(weight)

    query_grad = None
    pair = 0

    def query_next(count, after):
        nonlocal query_grad, pair
        if pair < width // PAIR:
            args = (tie(kv_mine, after), kv_other, at, att_scale, pair, min(count, width // PAIR - pair))
            query_grad = query_side(out_grad, keys, values, *args, query_grad)
            pair += count
        return query_grad

    for b in reversed(range(1, i_bits)):
        got = swap(weight, "inner", b)
        if b == i_bits - 1:
            grad_x = swap(grad, "outer", 1)
        if b > 1:
            weight = join(weight, got, 1)
    p, q = split(weight, got)
    p_got, q_got = swap(p, "inner", 0), swap(q, "outer", 1)
    grads = [grad, swap(grad, "outer", 0), grad_x, swap(grad_x, "outer", 0)]
    p, q = join(p, p_got, 1), join(q, q_got, 0)
    p_last, q_last = swap(p, "outer", 1), swap(q, "inner", 0)
    p_core, q_core = swap(p, "outer", 0), swap(q, "outer", 0)
    query_next(2, p)
    query_next(2, p)
    new_master, new_moment1, new_moment2 = adam_all(
        [tie(grads[0], p, q)] + grads[1:], master, moment1, moment2, at, (0, 1, 2, 3)
    )
    n = n_inner // 2
    weights = assemble(
        [(p, (0, (0,), 0, 2 * n)), (q, (1, (0, 2), 0, n)), (p_core, (0, (1,), 0, 2 * n)), (q_core, (1, (1, 3), 0, n))],
        at, None, width,
    )
    done = [weights, query_grad, new_master]
    p_core, q_core = swap(tie(p_last, *done), "outer", 0), swap(tie(q_last, *done), "outer", 0)
    weights = assemble([(p_last, (0, (2,), 0, 2 * n)), (q_last, (1, (0, 2), n, n))], at, weights, width)
    weights = assemble([(p_core, (0, (3,), 0, 2 * n)), (q_core, (1, (1, 3), n, n))], at, weights, width)
    return (query_grad, key_grad, new_master, new_moment1, new_moment2, weights.reshape(d, width))


def solution(mesh):
    tokens = P(("outer", "inner"), None)
    rows = P("inner", None)
    return jax.shard_map(
        local,
        mesh=mesh,
        in_specs=(tokens,) * 5 + (rows,) * 3,
        out_specs=(tokens, tokens, rows, rows, rows, P()),
        check_vma=False,
    )
```

time: 511 us -> 101 us (0.20)
  waiting for transfers between devices: 305 us -> 31.7 us
  other arithmetic: 86.5 us -> 0.64 us
  local copies, waits for them, and re-layouts: 62.8 us -> 0.03 us
  matrix products: 36.4 us -> 0 us
  starting transfers between devices: 0.38 us -> 36.1 us
  Pallas kernels: 0 us -> 31.6 us
  between operations: 14.1 us -> 1.13 us
    all_gather x3 -> x0, waiting for transfers between devices: 200 us -> none  [the longest x2 200 us: entering(): everything = lax.all_gather(array, axis)]
    reduce_scatter x1 -> x0, waiting for transfers between devices: 81.3 us -> none  [local(): lax.psum_scatter(product * grad_scale, 'inner', scatter_dimension=0, tile...]
    select_n x64 -> x0, other arithmetic: 78.7 us -> none  [turn(): return jnp.where(reached, new, before)]
    dot_general x17 -> x0, matrix products: 36.4 us -> none  [the longest x2 8.45 us: local(): jnp.einsum('thv,shv->hts', block_gradient, value_block_rows, preferred_el...]
    unnamed x71 -> x12, local copies, waits for them, and re-layouts: 36.2 us -> 0.03 us
    ppermute x0 -> x33, starting transfers between devices: none -> 36.1 us  [swap(): return lax.ppermute(x, axis, [(i, i ^ 1 << bit) for i in range(n)])]
    ppermute x0 -> x33, waiting for transfers between devices: none -> 31.7 us  [swap(): return lax.ppermute(x, axis, [(i, i ^ 1 << bit) for i in range(n)])]
    pallas_call x0 -> x29, Pallas kernels: none -> 31.6 us  [call(): pl.pallas_call(body, in_specs=specs, out_specs=[WHOLE if near else HBM fo...]
  transfers between devices with their start and end apart: 5 -> 33, of which waited for: 4 -> 18; matrix products, arithmetic and copies ran while one was open for 21% -> 1% of each run, Pallas kernels for 0% -> 25%
where the time goes in v2:
time: 101 us
  starting transfers between devices  36.1 us (36%)
  waiting for transfers between devices  31.7 us (31%)
  Pallas kernels  31.6 us (31%)
  between operations  1.13 us (1%)
    ppermute x33, starting transfers between devices, swap(): return lax.ppermute(x, axis, [(i, i ^ 1 << bit) for i in range(n)])  36.1 us
    ppermute x33, waiting for transfers between devices, swap(): return lax.ppermute(x, axis, [(i, i ^ 1 << bit) for i in range(n)])  31.7 us
    pallas_call x29, Pallas kernels, call(): pl.pallas_call(body, in_specs=specs, out_specs=[WHOLE if near else HBM fo...  31.6 us
  transfers between devices with their start and end apart: 33, of which 18 were waited for; matrix products, arithmetic and copies ran while one was open for 1% of the time, Pallas kernels for 25%

profile of v2, /device:TPU:0, one launch (start us, length us, event | category | flops | bytes accessed | tf_op | source)
XLA Modules:
  0.0 101.2 jit_solution(7721008356977665048)
XLA Ops:
  0.6 2.2 %shard_map.133 = bf16[4,128,128]{2,1,0:T(8,128)(2,1)S(1)} custom-call(bf16[1024,1024]{1,0:T(8,128)(2,1)} %g_ref.3, bf16[1024,1024]{1,0:T(8,128)(2,1)} %b_hbm.3), custom_call_target="tpu_custom_call" | custom-call | flops 134217728 | bytes 2097152 | tf_op jit(solution)/shard_map/pallas_call | solution.py:31
  2.8 3.0 %collective-permute-start.1 = (bf16[4,128,128]{2,1,0:T(8,128)(2,1)S(1)}, bf16[4,128,128]{2,1,0:T(8,128)(2,1)S(1)}, u32[]{:S(2)}, u32[]{:S(2)}) collective-permute-start(bf16[4,128,128]{2,1,0:T(8,128)(2,1)S(1)} %shard_map.133), channel_id=1, source_target_pairs={{0,1},{1,0},{2,3},{3,2},{4,5},{5,4},{6,7},{7,6},{8,9},{9,8},{10,11... | collective-permute-start | bytes 393224 | tf_op jit(solution)/shard_map/ppermute | solution.py:459
  5.8 3.3 %shard_map.127 = (f32[4,128,128]{2,1,0:T(8,128)S(1)}, bf16[1024,1024]{1,0:T(8,128)(2,1)S(1)}, bf16[1024,1024]{1,0:T(8,128)(2,1)S(1)}, bf16[1024,1024]{1,0:T(8,128)(2,1)S(1)}) custom-call(bf16[1024,1024]{1,0:T(8,128)(2,1)} %g_ref.3, bf16[1024,1024]{1,0:T(8,128)(2,1)} %b_hbm.3, bf16[1024,1024]{1,0:T(8,128)(2,1)} %v_ref.3), custom_call_target="tpu_custom_call" | custom-call | flops 134217728 | bytes 12582912 | tf_op jit(solution)/shard_map/pallas_call | solution.py:31
  9.4 1.9 %collective-permute-start.2 = (bf16[4,128,128]{2,1,0:T(8,128)(2,1)S(1)}, bf16[4,128,128]{2,1,0:T(8,128)(2,1)S(1)}, u32[]{:S(2)}, u32[]{:S(2)}) collective-permute-start(bf16[4,128,128]{2,1,0:T(8,128)(2,1)S(1)} %get-tuple-element.78), channel_id=1, source_target_pairs={{0,2},{1,3},{2,0},{3,1},{4,6},{5,7},{6,4},{7,5},{8,10},{9,11},{10,... | collective-permute-start | bytes 393224 | tf_op jit(solution)/shard_map/ppermute | solution.py:459
  11.3 2.0 %shard_map.128.refs_0_ = f32[1024,512]{1,0:T(8,128)S(1)} custom-call(bf16[1024,1024]{1,0:T(8,128)(2,1)S(1)} %get-tuple-element.69.g_ref, bf16[1024,1024]{1,0:T(8,128)(2,1)S(1)} %get-tuple-element.68.q_ref, bf16[1024,1024]{1,0:T(8,128)(2,1)S(1)} %get-tuple-element.71.v_ref.a_ref.refs_1_), custom_call_target="tpu_custom_call" | custom-call | flops 805306368 | bytes 5242880 | tf_op jit(solution)/shard_map/pallas_call | solution.py:31
  14.5 2.9 %collective-permute-start.3 = (bf16[4,128,128]{2,1,0:T(8,128)(2,1)S(1)}, bf16[4,128,128]{2,1,0:T(8,128)(2,1)S(1)}, u32[]{:S(2)}, u32[]{:S(2)}) collective-permute-start(bf16[4,128,128]{2,1,0:T(8,128)(2,1)S(1)} %get-tuple-element.82), channel_id=1, source_target_pairs={{0,4},{1,5},{2,6},{3,7},{4,0},{5,1},{6,2},{7,3},{8,12},{9,13},{10,... | collective-permute-start | bytes 393224 | tf_op jit(solution)/shard_map/ppermute | solution.py:459
  17.4 2.0 %shard_map.130.refs_4_ = bf16[1024,1024]{1,0:T(8,128)(2,1)S(1)} custom-call(bf16[1024,1024]{1,0:T(8,128)(2,1)} %in_hbm), custom_call_target="tpu_custom_call" | custom-call | bytes 4194304 | tf_op jit(solution)/shard_map/pallas_call | solution.py:31
  19.4 2.0 %shard_map.129.refs_0_ = f32[1024,512]{1,0:T(8,128)S(1)} custom-call(bf16[1024,1024]{1,0:T(8,128)(2,1)S(1)} %get-tuple-element.69.g_ref, bf16[1024,1024]{1,0:T(8,128)(2,1)S(1)} %get-tuple-element.68.q_ref, bf16[1024,1024]{1,0:T(8,128)(2,1)S(1)} %get-tuple-element.71.v_ref.a_ref.refs_1_), custom_call_target="tpu_custom_call" | custom-call | flops 805306368 | bytes 5242880 | tf_op jit(solution)/shard_map/pallas_call | solution.py:31
  25.8 2.9 %shard_map.131 = (bf16[4,128,128]{2,1,0:T(8,128)(2,1)S(1)}, f32[4,128,128]{2,1,0:T(8,128)S(1)}) custom-call(bf16[1024,1024]{1,0:T(8,128)(2,1)S(1)} %get-tuple-element.71.v_ref.a_ref.refs_1_, bf16[1024,1024]{1,0:T(8,128)(2,1)} %k_ref.3), custom_call_target="tpu_custom_call" | custom-call | flops 268435456 | bytes 2097152 | tf_op jit(solution)/shard_map/pallas_call | solution.py:31
  29.7 1.8 %collective-permute-start.6 = (bf16[4,128,128]{2,1,0:T(8,128)(2,1)S(1)}, bf16[4,128,128]{2,1,0:T(8,128)(2,1)S(1)}, u32[]{:S(2)}, u32[]{:S(2)}) collective-permute-start(bf16[4,128,128]{2,1,0:T(8,128)(2,1)S(1)} %get-tuple-element.92), channel_id=1, source_target_pairs={{0,1},{1,0},{2,3},{3,2},{4,5},{5,4},{6,7},{7,6},{8,9},{9,8},{10,11... | collective-permute-start | bytes 393224 | tf_op jit(solution)/shard_map/ppermute | solution.py:459
  31.5 3.3 %collective-permute-done.6.refs_3_ = bf16[4,128,128]{2,1,0:T(8,128)(2,1)S(1)} collective-permute-done((bf16[4,128,128]{2,1,0:T(8,128)(2,1)S(1)}, bf16[4,128,128]{2,1,0:T(8,128)(2,1)S(1)}, u32[]{:S(2)}, u32[]{:S(2)}) %collective-permute-start.6) | collective-permute-done | bytes 131104 | tf_op jit(solution)/shard_map/ppermute | solution.py:459
  34.8 2.3 %shard_map.139 = (bf16[1024,1024]{1,0:T(8,128)(2,1)}, bf16[2,8,64,256]{3,2,1,0:T(8,128)(2,1)S(1)}, bf16[2,8,64,256]{3,2,1,0:T(8,128)(2,1)S(1)}) custom-call(f32[1024,512]{1,0:T(8,128)S(1)} %shard_map.128.refs_0_, bf16[1024,1024]{1,0:T(8,128)(2,1)S(1)} %get-tuple-element.71.v_ref.a_ref.refs_1_, bf16[4,128,128]{2,1,0:T(8,128)(2,1)S(1)} %get-tuple-element.90.refs_2_, ...), custom_call_target="tpu_custom_call" | custom-call | flops 1207959552 | bytes 6291456 | tf_op jit(solution)/shard_map/pallas_call | solution.py:31
  39.4 2.3 %shard_map.140 = (bf16[1024,1024]{1,0:T(8,128)(2,1)}, bf16[2,8,64,256]{3,2,1,0:T(8,128)(2,1)S(1)}, bf16[2,8,64,256]{3,2,1,0:T(8,128)(2,1)S(1)}) custom-call(f32[1024,512]{1,0:T(8,128)S(1)} %shard_map.129.refs_0_, bf16[1024,1024]{1,0:T(8,128)(2,1)S(1)} %get-tuple-element.71.v_ref.a_ref.refs_1_, ...), custom_call_target="tpu_custom_call", output_to_operand_aliasing={{0}: (5, {})} | custom-call | flops 1207959552 | bytes 6291456 | tf_op jit(solution)/shard_map/pallas_call | solution.py:31
  45.1 4.8 %collective-permute-done.10 = bf16[1,8,64,256]{3,2,1,0:T(8,128)(2,1)S(1)} collective-permute-done((bf16[1,8,64,256]{3,2,1,0:T(8,128)(2,1)S(1)}, bf16[1,8,64,256]{3,2,1,0:T(8,128)(2,1)S(1)}, u32[]{:S(2)}, u32[]{:S(2)}) %collective-permute-start.10) | collective-permute-done | bytes 262176 | tf_op jit(solution)/shard_map/ppermute | solution.py:459
  52.4 2.8 %collective-permute-done.13 = bf16[1,4,64,256]{3,2,1,0:T(8,128)(2,1)S(1)} collective-permute-done((bf16[1,4,64,256]{3,2,1,0:T(8,128)(2,1)S(1)}, bf16[1,4,64,256]{3,2,1,0:T(8,128)(2,1)S(1)}, u32[]{:S(2)}, u32[]{:S(2)}) %collective-permute-start.13) | collective-permute-done | bytes 131104 | tf_op jit(solution)/shard_map/ppermute | solution.py:459
  57.5 3.2 %collective-permute-start.12 = (bf16[4,128,128]{2,1,0:T(8,128)(2,1)S(1)}, bf16[4,128,128]{2,1,0:T(8,128)(2,1)S(1)}, u32[]{:S(2)}, u32[]{:S(2)}) collective-permute-start(bf16[4,128,128]{2,1,0:T(8,128)(2,1)S(1)} %get-tuple-element.102), channel_id=1, source_target_pairs={{0,4},{1,5},{2,6},{3,7},{4,0},{5,1},{6,2},{7,3},{8,12},{9,13},{10,... | collective-permute-start | bytes 393224 | tf_op jit(solution)/shard_map/ppermute | solution.py:459
  61.6 2.0 %collective-permute-start.18 = (bf16[2,1,64,256]{3,2,1,0:T(8,128)(2,1)S(1)}, bf16[2,1,64,256]{3,2,1,0:T(8,128)(2,1)S(1)}, u32[]{:S(2)}, u32[]{:S(2)}) collective-permute-start(bf16[2,1,64,256]{3,2,1,0:T(8,128)(2,1)S(1)} %get-tuple-element.135), channel_id=1, source_target_pairs={{0,4},{1,5},{2,6},{3,7},{4,0},{5,1},{6,2},{7,3},{8,12},{9,13},{10,... | collective-permute-start | bytes 196616 | tf_op jit(solution)/shard_map/ppermute | solution.py:459
  63.6 3.4 %collective-permute-done.18.came_ref = bf16[2,1,64,256]{3,2,1,0:T(8,128)(2,1)S(1)} collective-permute-done((bf16[2,1,64,256]{3,2,1,0:T(8,128)(2,1)S(1)}, bf16[2,1,64,256]{3,2,1,0:T(8,128)(2,1)S(1)}, u32[]{:S(2)}, u32[]{:S(2)}) %collective-permute-start.18) | collective-permute-done | bytes 65568 | tf_op jit(solution)/shard_map/ppermute | solution.py:459
  67.2 1.9 %collective-permute-start.19 = (bf16[2,1,64,256]{3,2,1,0:T(8,128)(2,1)S(1)}, bf16[2,1,64,256]{3,2,1,0:T(8,128)(2,1)S(1)}, u32[]{:S(2)}, u32[]{:S(2)}) collective-permute-start(bf16[2,1,64,256]{3,2,1,0:T(8,128)(2,1)S(1)} %get-tuple-element.112.a_ref), channel_id=1, source_target_pairs={{0,4},{1,5},{2,6},{3,7},{4,0},{5,1},{6,2},{7,3},{8,12},{9,13},{10,... | collective-permute-start | bytes 196616 | tf_op jit(solution)/shard_map/ppermute | solution.py:459
  69.3 3.2 %collective-permute-done.19.b_ref = bf16[2,1,64,256]{3,2,1,0:T(8,128)(2,1)S(1)} collective-permute-done((bf16[2,1,64,256]{3,2,1,0:T(8,128)(2,1)S(1)}, bf16[2,1,64,256]{3,2,1,0:T(8,128)(2,1)S(1)}, u32[]{:S(2)}, u32[]{:S(2)}) %collective-permute-start.19) | collective-permute-done | bytes 65568 | tf_op jit(solution)/shard_map/ppermute | solution.py:459
  72.5 1.9 %collective-permute-start.20 = (bf16[2,2,64,256]{3,2,1,0:T(8,128)(2,1)S(1)}, bf16[2,2,64,256]{3,2,1,0:T(8,128)(2,1)S(1)}, u32[]{:S(2)}, u32[]{:S(2)}) collective-permute-start(bf16[2,2,64,256]{3,2,1,0:T(8,128)(2,1)S(1)} %shard_map.146.a_ref), channel_id=1, source_target_pairs={{0,2},{1,3},{2,0},{3,1},{4,6},{5,7},{6,4},{7,5},{8,10},{9,11},{10,... | collective-permute-start | bytes 393224 | tf_op jit(solution)/shard_map/ppermute | solution.py:459
  80.6 3.8 %collective-permute-done.25.refs_2_ = bf16[128,256]{1,0:T(8,128)(2,1)S(1)} collective-permute-done((bf16[128,256]{1,0:T(8,128)(2,1)S(1)}, bf16[128,256]{1,0:T(8,128)(2,1)S(1)}, u32[]{:S(2)}, u32[]{:S(2)}) %collective-permute-start.25) | collective-permute-done | bytes 65568 | tf_op jit(solution)/shard_map/ppermute | solution.py:459
  90.8 3.1 %shard_map.149.refs_0_ = bf16[1024,1024]{1,0:T(8,128)(2,1)} custom-call(bf16[1024,1024]{1,0:T(8,128)(2,1)S(1)} %copy-done, bf16[1024,1024]{1,0:T(8,128)(2,1)S(1)} %copy-done.2, bf16[1024,1024]{1,0:T(8,128)(2,1)S(1)} %copy-done.1, bf16[4,128,128]{2,1,0:T(8,128)(2,1)S(1)} %get-tuple-element.114.own_ref, bf16[4,128,128]{2,1,0:T(8,128)(2,1)S(1)} %collective-permute-done.22.oth_ref), custom_call_target="tpu_custom_call" | custom-call | flops 805306368 | bytes 4194304 | tf_op jit(solution)/shard_map/pallas_call | solution.py:31
  93.9 3.1 %shard_map.150 = bf16[1024,1024]{1,0:T(8,128)(2,1)} custom-call(bf16[1024,1024]{1,0:T(8,128)(2,1)S(1)} %copy-done, bf16[1024,1024]{1,0:T(8,128)(2,1)S(1)} %copy-done.2, bf16[1024,1024]{1,0:T(8,128)(2,1)S(1)} %copy-done.1, bf16[4,128,128]{2,1,0:T(8,128)(2,1)S(1)} %get-tuple-element.114.own_ref, ...), custom_call_target="tpu_custom_call", output_to_operand_aliasing={{}: (5, {})} | custom-call | flops 805306368 | bytes 4194304 | tf_op jit(solution)/shard_map/pallas_call | solution.py:31
  (91 shorter events, 35.1 us)
Async XLA Ops:
  2.8 6.5 %collective-permute-start.1 = (bf16[4,128,128]{2,1,0:T(8,128)(2,1)S(1)}, bf16[4,128,128]{2,1,0:T(8,128)(2,1)S(1)}, u32[]{:S(2)}, u32[]{:S(2)}) collective-permute-start(bf16[4,128,128]{2,1,0:T(8,128)(2,1)S(1)} %shard_map.133), channel_id=1, source_target_pairs={{0,1},{1,0},{2,3},{3,2},{4,5},{5,4},{6,7},{7,6},{8,9},{9,8},{10,11... | collective-permute-start | bytes 393224 | tf_op jit(solution)/shard_map/ppermute | solution.py:459
  9.4 5.0 %collective-permute-start.2 = (bf16[4,128,128]{2,1,0:T(8,128)(2,1)S(1)}, bf16[4,128,128]{2,1,0:T(8,128)(2,1)S(1)}, u32[]{:S(2)}, u32[]{:S(2)}) collective-permute-start(bf16[4,128,128]{2,1,0:T(8,128)(2,1)S(1)} %get-tuple-element.78), channel_id=1, source_target_pairs={{0,2},{1,3},{2,0},{3,1},{4,6},{5,7},{6,4},{7,5},{8,10},{9,11},{10,... | collective-permute-start | bytes 393224 | tf_op jit(solution)/shard_map/ppermute | solution.py:459
  14.5 7.4 %collective-permute-start.3 = (bf16[4,128,128]{2,1,0:T(8,128)(2,1)S(1)}, bf16[4,128,128]{2,1,0:T(8,128)(2,1)S(1)}, u32[]{:S(2)}, u32[]{:S(2)}) collective-permute-start(bf16[4,128,128]{2,1,0:T(8,128)(2,1)S(1)} %get-tuple-element.82), channel_id=1, source_target_pairs={{0,4},{1,5},{2,6},{3,7},{4,0},{5,1},{6,2},{7,3},{8,12},{9,13},{10,... | collective-permute-start | bytes 393224 | tf_op jit(solution)/shard_map/ppermute | solution.py:459
  24.1 5.5 %collective-permute-start.5 = (bf16[4,128,128]{2,1,0:T(8,128)(2,1)S(1)}, bf16[4,128,128]{2,1,0:T(8,128)(2,1)S(1)}, u32[]{:S(2)}, u32[]{:S(2)}) collective-permute-start(bf16[4,128,128]{2,1,0:T(8,128)(2,1)S(1)} %get-tuple-element.89), channel_id=1, source_target_pairs={{0,16},{8,24},{16,0},{24,8},{1,17},{9,25},{17,1},{25,9},{2,18},{10... | collective-permute-start | bytes 393224 | tf_op jit(solution)/shard_map/ppermute | solution.py:459
  29.7 5.0 %collective-permute-start.6 = (bf16[4,128,128]{2,1,0:T(8,128)(2,1)S(1)}, bf16[4,128,128]{2,1,0:T(8,128)(2,1)S(1)}, u32[]{:S(2)}, u32[]{:S(2)}) collective-permute-start(bf16[4,128,128]{2,1,0:T(8,128)(2,1)S(1)} %get-tuple-element.92), channel_id=1, source_target_pairs={{0,1},{1,0},{2,3},{3,2},{4,5},{5,4},{6,7},{7,6},{8,9},{9,8},{10,11... | collective-permute-start | bytes 393224 | tf_op jit(solution)/shard_map/ppermute | solution.py:459
  37.2 6.2 %collective-permute-start.8 = (bf16[2,8,64,256]{3,2,1,0:T(8,128)(2,1)S(1)}, bf16[2,8,64,256]{3,2,1,0:T(8,128)(2,1)S(1)}, u32[]{:S(2)}, u32[]{:S(2)}) collective-permute-start(bf16[2,8,64,256]{3,2,1,0:T(8,128)(2,1)S(1)} %get-tuple-element.97), channel_id=1, source_target_pairs={{0,8},{8,0},{16,24},{24,16},{1,9},{9,1},{17,25},{25,17},{2,10},{10... | collective-permute-start | bytes 1572872 | tf_op jit(solution)/shard_map/ppermute | solution.py:459
  37.7 6.4 %collective-permute-start = (bf16[4,128,128]{2,1,0:T(8,128)(2,1)S(1)}, bf16[4,128,128]{2,1,0:T(8,128)(2,1)S(1)}, u32[]{:S(2)}, u32[]{:S(2)}) collective-permute-start(bf16[4,128,128]{2,1,0:T(8,128)(2,1)S(1)} %get-tuple-element.73), channel_id=1, source_target_pairs={{0,1},{1,0},{2,3},{3,2},{4,5},{5,4},{6,7},{7,6},{8,9},{9,8},{10,11... | collective-permute-start | bytes 393224 | tf_op jit(solution)/shard_map/ppermute | solution.py:459
  41.8 8.1 %collective-permute-start.10 = (bf16[1,8,64,256]{3,2,1,0:T(8,128)(2,1)S(1)}, bf16[1,8,64,256]{3,2,1,0:T(8,128)(2,1)S(1)}, u32[]{:S(2)}, u32[]{:S(2)}) collective-permute-start(bf16[1,8,64,256]{3,2,1,0:T(8,128)(2,1)S(1)} %get-tuple-element.129), channel_id=1, source_target_pairs={{0,16},{8,24},{16,0},{24,8},{1,17},{9,25},{17,1},{25,9},{2,18},{10... | collective-permute-start | bytes 786440 | tf_op jit(solution)/shard_map/ppermute | solution.py:459
  43.5 7.8 %collective-permute-start.11 = (bf16[2,4,64,256]{3,2,1,0:T(8,128)(2,1)S(1)}, bf16[2,4,64,256]{3,2,1,0:T(8,128)(2,1)S(1)}, u32[]{:S(2)}, u32[]{:S(2)}) collective-permute-start(bf16[2,4,64,256]{3,2,1,0:T(8,128)(2,1)S(1)} %get-tuple-element.127), channel_id=1, source_target_pairs={{0,1},{1,0},{2,3},{3,2},{4,5},{5,4},{6,7},{7,6},{8,9},{9,8},{10,11... | collective-permute-start | bytes 786440 | tf_op jit(solution)/shard_map/ppermute | solution.py:459
  44.1 13.3 %collective-permute-start.9 = (bf16[4,128,128]{2,1,0:T(8,128)(2,1)S(1)}, bf16[4,128,128]{2,1,0:T(8,128)(2,1)S(1)}, u32[]{:S(2)}, u32[]{:S(2)}) collective-permute-start(bf16[4,128,128]{2,1,0:T(8,128)(2,1)S(1)} %get-tuple-element.98), channel_id=1, source_target_pairs={{0,2},{1,3},{2,0},{3,1},{4,6},{5,7},{6,4},{7,5},{8,10},{9,11},{10,... | collective-permute-start | bytes 393224 | tf_op jit(solution)/shard_map/ppermute | solution.py:459
  56.5 5.1 %collective-permute-start.15 = (bf16[2,2,64,256]{3,2,1,0:T(8,128)(2,1)S(1)}, bf16[2,2,64,256]{3,2,1,0:T(8,128)(2,1)S(1)}, u32[]{:S(2)}, u32[]{:S(2)}) collective-permute-start(bf16[2,2,64,256]{3,2,1,0:T(8,128)(2,1)S(1)} %pad_maximum_fusion.1), channel_id=1, source_target_pairs={{0,2},{1,3},{2,0},{3,1},{4,6},{5,7},{6,4},{7,5},{8,10},{9,11},{10,... | collective-permute-start | bytes 393224 | tf_op jit(solution)/shard_map/ppermute | solution.py:459
  57.5 11.6 %collective-permute-start.12 = (bf16[4,128,128]{2,1,0:T(8,128)(2,1)S(1)}, bf16[4,128,128]{2,1,0:T(8,128)(2,1)S(1)}, u32[]{:S(2)}, u32[]{:S(2)}) collective-permute-start(bf16[4,128,128]{2,1,0:T(8,128)(2,1)S(1)} %get-tuple-element.102), channel_id=1, source_target_pairs={{0,4},{1,5},{2,6},{3,7},{4,0},{5,1},{6,2},{7,3},{8,12},{9,13},{10,... | collective-permute-start | bytes 393224 | tf_op jit(solution)/shard_map/ppermute | solution.py:459
  61.6 5.5 %collective-permute-start.18 = (bf16[2,1,64,256]{3,2,1,0:T(8,128)(2,1)S(1)}, bf16[2,1,64,256]{3,2,1,0:T(8,128)(2,1)S(1)}, u32[]{:S(2)}, u32[]{:S(2)}) collective-permute-start(bf16[2,1,64,256]{3,2,1,0:T(8,128)(2,1)S(1)} %get-tuple-element.135), channel_id=1, source_target_pairs={{0,4},{1,5},{2,6},{3,7},{4,0},{5,1},{6,2},{7,3},{8,12},{9,13},{10,... | collective-permute-start | bytes 196616 | tf_op jit(solution)/shard_map/ppermute | solution.py:459
  67.2 5.2 %collective-permute-start.19 = (bf16[2,1,64,256]{3,2,1,0:T(8,128)(2,1)S(1)}, bf16[2,1,64,256]{3,2,1,0:T(8,128)(2,1)S(1)}, u32[]{:S(2)}, u32[]{:S(2)}) collective-permute-start(bf16[2,1,64,256]{3,2,1,0:T(8,128)(2,1)S(1)} %get-tuple-element.112.a_ref), channel_id=1, source_target_pairs={{0,4},{1,5},{2,6},{3,7},{4,0},{5,1},{6,2},{7,3},{8,12},{9,13},{10,... | collective-permute-start | bytes 196616 | tf_op jit(solution)/shard_map/ppermute | solution.py:459
  69.2 5.2 %collective-permute-start.16 = (bf16[4,128,128]{2,1,0:T(8,128)(2,1)S(1)}, bf16[4,128,128]{2,1,0:T(8,128)(2,1)S(1)}, u32[]{:S(2)}, u32[]{:S(2)}) collective-permute-start(bf16[4,128,128]{2,1,0:T(8,128)(2,1)S(1)} %get-tuple-element.106), channel_id=1, source_target_pairs={{0,8},{8,0},{16,24},{24,16},{1,9},{9,1},{17,25},{25,17},{2,10},{10... | collective-permute-start | bytes 393224 | tf_op jit(solution)/shard_map/ppermute | solution.py:459
  75.1 9.2 %collective-permute-start.17 = (bf16[4,128,128]{2,1,0:T(8,128)(2,1)S(1)}, bf16[4,128,128]{2,1,0:T(8,128)(2,1)S(1)}, u32[]{:S(2)}, u32[]{:S(2)}) collective-permute-start(bf16[4,128,128]{2,1,0:T(8,128)(2,1)S(1)} %get-tuple-element.110), channel_id=1, source_target_pairs={{0,16},{8,24},{16,0},{24,8},{1,17},{9,25},{17,1},{25,9},{2,18},{10... | collective-permute-start | bytes 393224 | tf_op jit(solution)/shard_map/ppermute | solution.py:459
  77.5 7.7 %collective-permute-start.23 = (bf16[1,4,64,256]{3,2,1,0:T(8,128)(2,1)S(1)}, bf16[1,4,64,256]{3,2,1,0:T(8,128)(2,1)S(1)}, u32[]{:S(2)}, u32[]{:S(2)}) collective-permute-start(bf16[1,4,64,256]{3,2,1,0:T(8,128)(2,1)S(1)} %get-tuple-element.119.a_ref), channel_id=1, source_target_pairs={{0,16},{8,24},{16,0},{24,8},{1,17},{9,25},{17,1},{25,9},{2,18},{10... | collective-permute-start | bytes 393224 | tf_op jit(solution)/shard_map/ppermute | solution.py:459
  78.8 6.8 %collective-permute-start.21 = (bf16[1,4,64,256]{3,2,1,0:T(8,128)(2,1)S(1)}, bf16[1,4,64,256]{3,2,1,0:T(8,128)(2,1)S(1)}, u32[]{:S(2)}, u32[]{:S(2)}) collective-permute-start(bf16[1,4,64,256]{3,2,1,0:T(8,128)(2,1)S(1)} %get-tuple-element.113.a_ref), channel_id=1, source_target_pairs={{0,1},{1,0},{2,3},{3,2},{4,5},{5,4},{6,7},{7,6},{8,9},{9,8},{10,11... | collective-permute-start | bytes 393224 | tf_op jit(solution)/shard_map/ppermute | solution.py:459
  80.6 5.4 %collective-permute-start.24 = (bf16[128,256]{1,0:T(8,128)(2,1)S(1)}, bf16[128,256]{1,0:T(8,128)(2,1)S(1)}, u32[]{:S(2)}, u32[]{:S(2)}) collective-permute-start(bf16[128,256]{1,0:T(8,128)(2,1)S(1)} %get-tuple-element.120.refs_0_), channel_id=1, source_target_pairs={{0,8},{8,0},{16,24},{24,16},{1,9},{9,1},{17,25},{25,17},{2,10},{10... | collective-permute-start | bytes 196616 | tf_op jit(solution)/shard_map/ppermute | solution.py:459
  84.4 6.4 %collective-permute-start.22 = (bf16[4,128,128]{2,1,0:T(8,128)(2,1)S(1)}, bf16[4,128,128]{2,1,0:T(8,128)(2,1)S(1)}, u32[]{:S(2)}, u32[]{:S(2)}) collective-permute-start(bf16[4,128,128]{2,1,0:T(8,128)(2,1)S(1)} %get-tuple-element.116), channel_id=1, source_target_pairs={{0,1},{1,0},{2,3},{3,2},{4,5},{5,4},{6,7},{7,6},{8,9},{9,8},{10,11... | collective-permute-start | bytes 393224 | tf_op jit(solution)/shard_map/ppermute | solution.py:459
  85.3 11.7 %collective-permute-start.29 = (bf16[2,4,64,256]{3,2,1,0:T(8,128)(2,1)S(1)}, bf16[2,4,64,256]{3,2,1,0:T(8,128)(2,1)S(1)}, u32[]{:S(2)}, u32[]{:S(2)}) collective-permute-start(bf16[2,4,64,256]{3,2,1,0:T(8,128)(2,1)S(1)} %shard_map.151.refs_1_), channel_id=1, source_target_pairs={{0,8},{8,0},{16,24},{24,16},{1,9},{9,1},{17,25},{25,17},{2,10},{10... | collective-permute-start | bytes 786440 | tf_op jit(solution)/shard_map/ppermute | solution.py:459
  85.6 11.4 %collective-permute-start.28 = (bf16[1,8,64,256]{3,2,1,0:T(8,128)(2,1)S(1)}, bf16[1,8,64,256]{3,2,1,0:T(8,128)(2,1)S(1)}, u32[]{:S(2)}, u32[]{:S(2)}) collective-permute-start(bf16[1,8,64,256]{3,2,1,0:T(8,128)(2,1)S(1)} %shard_map.148.refs_0_), channel_id=1, source_target_pairs={{0,8},{8,0},{16,24},{24,16},{1,9},{9,1},{17,25},{25,17},{2,10},{10... | collective-permute-start | bytes 786440 | tf_op jit(solution)/shard_map/ppermute | solution.py:459
  85.9 12.2 %collective-permute-start.31 = (bf16[2,4,64,256]{3,2,1,0:T(8,128)(2,1)S(1)}, bf16[2,4,64,256]{3,2,1,0:T(8,128)(2,1)S(1)}, u32[]{:S(2)}, u32[]{:S(2)}) collective-permute-start(bf16[2,4,64,256]{3,2,1,0:T(8,128)(2,1)S(1)} %shard_map.151.refs_1_), channel_id=1, source_target_pairs={{0,1},{1,0},{2,3},{3,2},{4,5},{5,4},{6,7},{7,6},{8,9},{9,8},{10,11... | collective-permute-start | bytes 786440 | tf_op jit(solution)/shard_map/ppermute | solution.py:459
  87.2 10.9 %collective-permute-start.27 = (bf16[1,8,64,256]{3,2,1,0:T(8,128)(2,1)S(1)}, bf16[1,8,64,256]{3,2,1,0:T(8,128)(2,1)S(1)}, u32[]{:S(2)}, u32[]{:S(2)}) collective-permute-start(bf16[1,8,64,256]{3,2,1,0:T(8,128)(2,1)S(1)} %shard_map.148.refs_0_), channel_id=1, source_target_pairs={{0,16},{8,24},{16,0},{24,8},{1,17},{9,25},{17,1},{25,9},{2,18},{10... | collective-permute-start | bytes 786440 | tf_op jit(solution)/shard_map/ppermute | solution.py:459
  (15 other events, 138.4 us)

commit v3 on v2

--- a/solution.py
+++ b/solution.py
@@ -177,91 +177,125 @@
         functools.partial(both_states_body, at),
         [a, b],
         [WHOLE, HBM],
-        [(shape, BF16, True), (shape, F32, True)],
+        [(shape, BF16, True), (shape, F32, True), ((rows, width), BF16, True)],
         rows * width * HD,
         2 * rows * width,
-        [pltpu.VMEM((rows, width), BF16), dma(rows // SUB)],
-    )
-
-
-def key_inside_body(scale, picks, here_at, g_ref, q_ref, v_ref, out_ref):
-    n = len(picks)
-    rows, cols = out_ref.shape[0], out_ref.shape[1] // n
+        [dma(rows // SUB)],
+    )
+
+
+def key_inside_body(scale, other, at, g_ref, q_ref, v_ref, out_ref):
+    rows, cols = out_ref.shape
     later = lax.broadcasted_iota(jnp.int32, (SUB, SUB), 1) >= lax.broadcasted_iota(jnp.int32, (SUB, SUB), 0)
-    for s in range(n):
-        for j in range(cols // HD):
-            at = pl.ds(pl.multiple_of(here_at.group(picks[s]) * cols + j * HD, HD), HD)
-            to = s * cols + j * HD
-            state = None
-            for b in reversed(range(rows // SUB)):
-                here = (pl.ds(b * SUB, SUB), at)
-                g, q, v = g_ref[here], q_ref[here], v_ref[here]
-                scores = jnp.where(later, mm(v, g, (1, 1)), 0.0).astype(BF16)
-                total = mm(scores, q, (1, 0))
-                if state is not None:
-                    total = total + mm(v, state.astype(BF16), (1, 0))
-                out_ref[b * SUB : (b + 1) * SUB, to : to + HD] = total * scale
-                if b:
-                    term = mm(g, q, (0, 0))
-                    state = term if state is None else state + term
-
-
-def key_inside(g, q, v, at, picks, scale, cols):
-    rows = g.shape[0]
-    n = len(picks)
-    return call(
-        functools.partial(key_inside_body, scale, picks, at),
+    for to in range(0, cols, HD):
+        from_ = pl.ds(pl.multiple_of((at.y() ^ other) * cols + to, HD), HD)
+        state = None
+        for b in reversed(range(rows // SUB)):
+            here = (pl.ds(b * SUB, SUB), from_)
+            g, q, v = g_ref[here], q_ref[here], v_ref[here]
+            scores = jnp.where(later, mm(v, g, (1, 1)), 0.0).astype(BF16)
+            total = mm(scores, q, (1, 0))
+            if state is not None:
+                total = total + mm(v, state.astype(BF16), (1, 0))
+            out_ref[b * SUB : (b + 1) * SUB, to : to + HD] = total * scale
+            if b:
+                term = mm(g, q, (0, 0))
+                state = term if state is None else state + term
+
+
+def query_inside_body(scale, other, at, kinds, g_ref, k_ref, v_ref, *refs):
+    pieces = refs[: len(kinds)]
+    if kinds:
+        out_ref, key_hbm, sem = refs[len(kinds) :]
+    else:
+        (out_ref,) = refs
+    rows, cols = out_ref.shape
+    copies = []
+    for i, (piece, (piece_other, core)) in enumerate(zip(pieces, kinds)):
+        size = piece.shape[1]
+        group = (at.y() ^ piece_other) * 2 + (at.bit("outer", 0) ^ core)
+        to = pl.ds(pl.multiple_of(group * size, size), size)
+        copies.append(pltpu.make_async_copy(piece, key_hbm.at[:, to], sem.at[i]))
+        copies[i].start()
+    earlier = lax.broadcasted_iota(jnp.int32, (SUB, SUB), 0) >= lax.broadcasted_iota(jnp.int32, (SUB, SUB), 1)
+    for to in range(0, cols, HD):
+        from_ = pl.ds(pl.multiple_of((at.y() ^ other) * cols + to, HD), HD)
+        state = None
+        for b in range(rows // SUB):
+            here = (pl.ds(b * SUB, SUB), from_)
+            g, k, v = g_ref[here], k_ref[here], v_ref[here]
+            scores = jnp.where(earlier, mm(g, v, (1, 1)), 0.0).astype(BF16)
+            total = mm(scores, k, (1, 0))
+            if state is not None:
+                total = total + mm(g, state.astype(BF16), (1, 0))
+            out_ref[b * SUB : (b + 1) * SUB, to : to + HD] = total * scale
+            if b + 1 < rows // SUB:
+                term = mm(v, k, (0, 0))
+                state = term if state is None else state + term
+    for copy in copies:
+        copy.wait()
+
+
+def key_inside(g, q, v, at, other, scale):
+    rows, width = g.shape
+    cols = width // 2
+    return call(
+        functools.partial(key_inside_body, scale, other, at),
         [g, q, v],
         [WHOLE] * 3,
-        [((rows, n * cols), F32, True)],
-        rows * n * cols * (2 * SUB + 2 * HD),
-        10 * rows * n * cols,
+        [((rows, cols), F32, True)],
+        rows * cols * (2 * SUB + 2 * HD),
+        10 * rows * cols,
     )[0]
 
 
-def head_of(ref_own, ref_oth, other, at):
-    return jnp.where(other, ref_oth[at], ref_own[at])
-
-
-def query_body(scale, first, count, at, g_ref, k_ref, v_ref, own_ref, oth_ref, *refs):
-    out_hbm, buf, sem = refs[-3:]
-    rows = g_ref.shape[0]
-    heads_half = own_ref.shape[0]
-    earlier = lax.broadcasted_iota(jnp.int32, (SUB, SUB), 0) >= lax.broadcasted_iota(jnp.int32, (SUB, SUB), 1)
+def query_inside(g, k, v, at, other, scale, pieces=()):
+    rows, width = g.shape
+    cols = width // 2
+    kinds = [kind for _, kind in pieces]
+    outs = [((rows, cols), F32, True)] + [((rows, width), BF16, False)] * bool(pieces)
+    return call(
+        functools.partial(query_inside_body, scale, other, at, kinds),
+        [g, k, v] + [piece for piece, _ in pieces],
+        [WHOLE] * (3 + len(pieces)),
+        outs,
+        rows * cols * (2 * SUB + 2 * HD),
+        10 * rows * cols,
+        [dma(len(pieces))] if pieces else [],
+    )
+
+
+def query_body(scale, at, g_ref, in_own, in_oth, own_ref, oth_ref, out_hbm, buf, sem):
+    n, rows, cols = buf.shape
     copies = []
-    for n in range(count):
-        for j in range(2):
-            head = (first + n) * 2 + j
-            cols = slice(head * HD, (head + 1) * HD)
-            other = jnp.int32(head // heads_half) != at.y()
-            state = head_of(own_ref, oth_ref, other, head % heads_half).astype(F32)
-            for b in range(rows // SUB):
-                here = slice(b * SUB, (b + 1) * SUB)
-                g, k, v = g_ref[here, cols], k_ref[here, cols], v_ref[here, cols]
-                scores = jnp.where(earlier, mm(g, v, (1, 1)), 0.0).astype(BF16)
-                total = mm(scores, k, (1, 0)) + mm(g, state.astype(BF16), (1, 0))
-                buf[n, here, j * HD : (j + 1) * HD] = (total * scale).astype(BF16)
-                if b + 1 < rows // SUB:
-                    state = state + mm(v, k, (0, 0))
-        copy = pltpu.make_async_copy(buf.at[n], out_hbm.at[:, pl.ds((first + n) * PAIR, PAIR)], sem.at[n])
-        copy.start()
-        copies.append(copy)
+    for other, (in_ref, state_ref) in enumerate(((in_own, own_ref), (in_oth, oth_ref))):
+        half = at.y() ^ other
+        for p in range(n // 2):
+            i = other * (n // 2) + p
+            for j in range(cols // HD):
+                head = p * (cols // HD) + j
+                from_ = pl.multiple_of((half * (n // 2) + p) * cols + j * HD, HD)
+                part = mm(g_ref[:, pl.ds(from_, HD)], state_ref[head], (1, 0))
+                total = in_ref[:, head * HD : (head + 1) * HD] + part * scale
+                buf[i, :, j * HD : (j + 1) * HD] = total.astype(BF16)
+            to = pl.ds(pl.multiple_of((half * (n // 2) + p) * cols, cols), cols)
+            copies.append(pltpu.make_async_copy(buf.at[i], out_hbm.at[:, to], sem.at[i]))
+            copies[i].start()
     for copy in copies:
         copy.wait()
 
 
-def query_side(g, k, v, own, oth, at, scale, first, count, before):
+def query_side(g, in_own, in_oth, own, oth, at, scale):
     rows, width = g.shape
-    more = [] if before is None else [before]
-    return call(
-        functools.partial(query_body, scale, first, count, at),
-        [g, k, v, own, oth] + more,
-        [WHOLE] * 5 + [HBM] * len(more),
+    n = width // PAIR
+    return call(
+        functools.partial(query_body, scale, at),
+        [g, in_own, in_oth, own, oth],
+        [WHOLE] * 5,
         [((rows, width), BF16, False)],
-        rows * count * PAIR * (2 * SUB + 2 * HD),
-        8 * rows * count * PAIR,
-        [pltpu.VMEM((count, rows, PAIR), BF16), dma(count)],
-        {5: 0} if more else None,
+        rows * width * HD,
+        8 * rows * width,
+        [pltpu.VMEM((n, rows, PAIR), BF16), dma(n)],
     )[0]
 
 
@@ -295,53 +329,64 @@
     )[0]
 
 
-def key_product_body(scale, grad_scale, n_inner, picks, here_at, *refs):
-    inside_ref, v_ref, own_ref, oth_ref, turned_ref = refs[:5]
-    key_hbm, p_ref, q_ref, buf, sem = refs[-5:]
-    n = len(picks)
-    heads_half = own_ref.shape[0]
-    cols = inside_ref.shape[1] // n
+def key_product_body(scale, grad_scale, at, other, cores, inside_ref, v_ref, state_ref, turned_ref, *refs):
+    n = len(cores)
+    cols = refs[0].shape[1]
     heads = cols // HD
-    copies = []
-    for s in range(n):
-        group = here_at.group(picks[s])
+    half = at.y() ^ other
+    for s, core in enumerate(cores):
+        key_ref, out = refs[s], refs[n + s]
+        place = at.bit("outer", 0) ^ core
         for j in range(heads):
-            here = slice(s * cols + j * HD, s * cols + (j + 1) * HD)
-            head = group * heads + j
-            other = (head // heads_half) != here_at.y()
-            state = head_of(own_ref, oth_ref, other, lax.rem(head, heads_half))
-            part = mm(v_ref[:, pl.ds(pl.multiple_of(head * HD, HD), HD)], state, (1, 0))
-            buf[s, :, j * HD : (j + 1) * HD] = (inside_ref[:, here] + part * scale).astype(BF16)
-        at = pl.ds(pl.multiple_of(group * cols, cols), cols)
-        copy = pltpu.make_async_copy(buf.at[s], key_hbm.at[:, at], sem.at[s])
-        copy.start()
-        copies.append(copy)
-    for s in range(n):
-        product = (mm(turned_ref[...], buf[s], (1, 0)) * grad_scale).astype(BF16)
-        size = product.shape[0] // n_inner
-        for r in range(n_inner):
-            p_ref[s, r] = product[r * size : r * size + size // 2]
-            q_ref[s, r] = product[r * size + size // 2 : (r + 1) * size]
-    for copy in copies:
-        copy.wait()
-
-
-def key_product(inside, v, own, oth, turned, picks, at, scale, grad_scale, n_inner, before):
-    n = len(picks)
+            head = place * heads + j
+            here = pl.ds(pl.multiple_of(head * HD, HD), HD)
+            from_ = pl.ds(pl.multiple_of((half * 2 * heads + head) * HD, HD), HD)
+            part = mm(v_ref[:, from_], state_ref[head], (1, 0))
+            key_ref[:, j * HD : (j + 1) * HD] = (inside_ref[:, here] + part * scale).astype(BF16)
+        product = (mm(turned_ref[...], key_ref[...], (1, 0)) * grad_scale).astype(BF16)
+        size = product.shape[0] // at.n_inner
+        for r in range(at.n_inner):
+            for i in range(2):
+                out[i, r] = product[r * size + i * (size // 2) : r * size + (i + 1) * (size // 2)]
+
+
+def key_product(inside, v, states, turned, at, other, cores, scale, grad_scale):
+    n = len(cores)
     rows, width = v.shape
-    cols = inside.shape[1] // n
+    cols = width // at.n_outer
     d = turned.shape[0]
-    piece = ((n, n_inner, d // n_inner // 2, cols), BF16, True)
-    more = [] if before is None else [before]
-    return call(
-        functools.partial(key_product_body, scale, grad_scale, n_inner, picks, at),
-        [inside, v, own, oth, turned] + more,
-        [WHOLE] * 5 + [HBM] * len(more),
-        [((rows, width), BF16, False), piece, piece],
+    piece = ((2, at.n_inner, d // at.n_inner // 2, cols), BF16, True)
+    return call(
+        functools.partial(key_product_body, scale, grad_scale, at, other, cores),
+        [inside, v, states, turned],
+        [WHOLE] * 4,
+        [((rows, cols), BF16, True)] * n + [piece] * n,
         n * cols * rows * (d + HD),
         2 * rows * (d + 4 * n * cols),
-        [pltpu.VMEM((n, rows, cols), BF16), dma(n)],
-        {5: 0} if more else None,
+    )
+
+
+def cores_body(at, *refs):
+    (n_own, n_oth, g_own, g_oth), (p_send, p_keep, q_send, q_keep) = refs[:4], refs[4:]
+    far_own = at.bit("outer", 1) ^ at.y()
+    p_own = n_own[0].astype(F32) + g_own[0].astype(F32)
+    p_oth = n_oth[0].astype(F32) + g_oth[0].astype(F32)
+    p_send[0] = jnp.where(far_own == 1, p_own, p_oth).astype(BF16)
+    p_keep[0] = jnp.where(far_own == 1, p_oth, p_own)
+    n = n_own.shape[1] // 2
+    for side, near, got in ((far_own, n_own, g_own), (1 - far_own, n_oth, g_oth)):
+        q_keep[side] = near[1, :n].astype(F32) + got[1, :n].astype(F32)
+        q_send[side] = (near[1, n:].astype(F32) + got[1, n:].astype(F32)).astype(BF16)
+
+
+def cores(at, near_own, near_oth, got_own, got_oth):
+    _, n, part, cols = near_own.shape
+    one, two = (1, n, part, cols), (2, n // 2, part, cols)
+    return call(
+        functools.partial(cores_body, at),
+        [near_own, near_oth, got_own, got_oth],
+        [WHOLE] * 4,
+        [(one, BF16, True), (one, F32, True), (two, BF16, True), (two, F32, True)],
     )
 
 
@@ -352,24 +397,26 @@
     return new_master, new_moment1, new_moment2
 
 
-def adam_own_body(at, keep_ref, came_ref, master_ref, m1_ref, m2_ref, grad_ref, weight_ref):
-    _, _, part, size = keep_ref.shape
+def adam_own_body(at, n, *refs):
+    sums, (master_ref, m1_ref, m2_ref, grad_ref, weight_ref) = refs[:n], refs[n:]
+    _, _, part, size = sums[0].shape
     cols = pl.ds(pl.multiple_of(at.group(0) * size, size), size)
     for j in range(2):
         here = slice(j * part, (j + 1) * part)
-        grad = (keep_ref[j, 0] + came_ref[j, 0].astype(F32)).astype(BF16)
+        grad = sum(ref[j, 0].astype(F32) for ref in sums).astype(BF16)
         grad_ref[here, :] = grad
         new_master, _, _ = adam(grad.astype(F32), master_ref[here, cols], m1_ref[here, cols], m2_ref[here, cols])
         weight_ref[j, 0] = new_master.astype(BF16)
 
 
-def adam_own(keep, came, master, moment1, moment2, at):
-    _, _, part, cols = keep.shape
-    return call(
-        functools.partial(adam_own_body, at),
-        [keep, came, master, moment1, moment2],
-        [WHOLE] * 5,
-        [((2 * part, cols), BF16, True), (keep.shape, BF16, True)],
+def adam_own(sums, master, moment1, moment2, at):
+    shape = sums[0].shape
+    _, _, part, cols = shape
+    return call(
+        functools.partial(adam_own_body, at, len(sums)),
+        [*sums, master, moment1, moment2],
+        [WHOLE] * (len(sums) + 3),
+        [((2 * part, cols), BF16, True), (shape, BF16, True)],
         2 * part * cols,
         48 * part * cols,
     )
@@ -466,22 +513,24 @@
     return out
 
 
-def step_body(level, side, at, total_ref, got_ref, *refs):
-    total_out, send_out, outside_out = refs[-3:]
+def step_body(level, side, at, more, total_ref, got_ref, *refs):
+    send_out, outside_out = refs[-2:]
     got = got_ref[...].astype(F32)
     total = total_ref[...] + got
-    total_out[...] = total
     send_out[...] = total.astype(BF16)
+    if more:
+        refs[-3][...] = total
     if level is None:
         outside_out[...] = jnp.zeros_like(got)
     else:
         outside_out[...] = refs[0][...] + jnp.where(at.bit(*level) == side, got, 0.0)
 
 
-def step(level, side, at, total, got, *outside):
-    outs = [(total.shape, F32, True), (total.shape, BF16, True), (total.shape, F32, True)]
-    body = functools.partial(step_body, level, side, at)
-    return call(body, [total, got, *outside], [WHOLE] * (2 + len(outside)), outs)
+def step(level, side, at, total, got, *outside, more=True):
+    outs = [(total.shape, F32, True)] * more + [(total.shape, BF16, True), (total.shape, F32, True)]
+    body = functools.partial(step_body, level, side, at, more)
+    results = call(body, [total, got, *outside], [WHOLE] * (2 + len(outside)), outs)
+    return results if more else [None, *results]
 
 
 def last_body(level, side, at, outside_ref, got_ref, own_ref, came_ref, give_out, out):
@@ -501,15 +550,17 @@
     came = swap(sent, "inner", 0)
     after = yield came
     own = own()
+    came = tie(came, *after)
     total, send, outside = step(None, side, at, own, came)
     levels = [("inner", b) for b in range(1, at.i_bits)] + [("outer", b) for b in range(at.o_bits)]
     for n, level in enumerate(levels):
-        got = swap(tie(send, *after), *level)
+        got = swap(send, *level)
         after = yield got
+        got = tie(got, *after)
         if n + 1 < len(levels):
-            total, send, outside = step(level, side, at, total, got, outside)
+            total, send, outside = step(level, side, at, total, got, outside, more=n + 2 < len(levels))
     give, kept = last(levels[-1], side, at, outside, got, own, came)
-    back = swap(tie(give, *after), "inner", 0)
+    back = swap(give, "inner", 0)
     yield kept, back
 
 
@@ -523,33 +574,68 @@
     return high.astype(BF16), low
 
 
-def merge(p_keep, p_got, q_keep, q_got):
-    (p_send, p), (q_send, q) = fold(p_keep, p_got, 1), fold(q_keep, q_got, 1)
-    return jnp.concatenate([p_send, q_send], 0), jnp.concatenate([p, q], 0)
-
-
-def join_body(axis, a_ref, b_ref, out):
-    size = a_ref.shape[axis]
-    for side, ref in enumerate((a_ref, b_ref)):
+def fan_body(n_keep, ways, *refs):
+    outs = refs[len(refs) - ways :]
+    if n_keep == 2:
+        rows = [(refs[0], refs[1]), (refs[2], refs[3])]
+        totals = [sum(ref[0].astype(F32) for ref in pair) for pair in rows]
+    else:
+        totals = [sum(ref[i].astype(F32) for ref in refs[: len(refs) - ways]) for i in range(2)]
+    size = outs[0].shape[1]
+    for i, total in enumerate(totals):
+        for j, out in enumerate(outs):
+            out[i] = total[j * size : (j + 1) * size].astype(out.dtype)
+
+
+def fan(n_keep, ways, *arrays):
+    _, n, part, cols = arrays[0].shape
+    shape = (2, n // ways, part, cols)
+    outs = [(shape, F32 if j == 0 else BF16, True) for j in range(ways)]
+    return call(functools.partial(fan_body, n_keep, ways), list(arrays), [WHOLE] * len(arrays), outs)
+
+
+def swap_all(xs, masks):
+    n = lax.axis_size("inner")
+    return [lax.ppermute(x, "inner", [(i, i ^ mask) for i in range(n)]) for x, mask in zip(xs, masks)]
+
+
+def bit_groups(i_bits):
+    groups = []
+    for b in range(1, i_bits, 2):
+        if b + 1 < i_bits:
+            groups.append([((i >> 1) << b) | ((i & 1) << (b + 1)) for i in range(1, 4)])
+        else:
+            groups.append([1 << b])
+    return groups
+
+
+def join_body(axis, *refs):
+    out = refs[-1]
+    size = refs[0].shape[axis]
+    for side, ref in enumerate(refs[:-1]):
         at = tuple(pl.ds(side * size, size) if a == axis else slice(None) for a in range(len(ref.shape)))
         out[at] = ref[...]
 
 
-def join(a, b, axis):
-    shape = tuple(2 * s if i == axis else s for i, s in enumerate(a.shape))
-    return call(functools.partial(join_body, axis), [a, b], [WHOLE] * 2, [(shape, BF16, True)])[0]
-
-
-def split_body(a_ref, b_ref, p_out, q_out):
-    n = a_ref.shape[1]
-    for i, out in enumerate((p_out, q_out)):
-        out[:, :n] = a_ref[i : i + 1]
-        out[:, n:] = b_ref[i : i + 1]
-
-
-def split(a, b):
-    _, n, part, cols = a.shape
-    return call(split_body, [a, b], [WHOLE] * 2, [((1, 2 * n, part, cols), BF16, True)] * 2)
+def join(axis, *arrays):
+    shape = tuple(len(arrays) * s if i == axis else s for i, s in enumerate(arrays[0].shape))
+    body = functools.partial(join_body, axis)
+    return call(body, list(arrays), [WHOLE] * len(arrays), [(shape, BF16, True)])[0]
+
+
+def split_body(*refs):
+    outs = refs[-2:]
+    for j, ref in enumerate(refs[:-2]):
+        n = ref.shape[1]
+        for i, out in enumerate(outs):
+            out[:, j * n : (j + 1) * n] = ref[i : i + 1]
+
+
+def split(*arrays):
+    _, n, part, cols = arrays[0].shape
+    return call(
+        split_body, list(arrays), [WHOLE] * len(arrays), [((1, len(arrays) * n, part, cols), BF16, True)] * 2
+    )
 
 
 def local(inputs, queries, keys, values, out_grad, master, moment1, moment2):
@@ -563,8 +649,6 @@
     total_tokens = rows_here * n_outer * n_inner
     att_scale = 1.0 / math.sqrt(HD * total_tokens)
     grad_scale = 1.0 / math.sqrt(total_tokens)
-    cols = width // n_outer
-    near, far_ = tuple(range(0, n_outer, 2)), tuple(range(1, n_outer, 2))
 
     qg_sent = states(out_grad, queries, at, BF16)
     loaded = []
@@ -577,23 +661,23 @@
     next(qg)
     qg.send([])
     g, q, v = loaded[1:]
-    inside_far = key_inside(g, q, v, at, far_, att_scale, cols)
-    done = [inside_far]
-    turned = inside_near = None
+    kv_sent, kv_own, k = both_states(v, keys, at)
+    done = [kv_own]
+    turned = None
     for _ in range(2, i_bits):
         qg.send(done)
         done = []
         if turned is None:
-            inside_near = key_inside(tie(g, inside_far), q, v, at, near, att_scale, cols)
-            turned = turned_inputs(tie(inputs, inside_far), at)
-            done = [inside_near, turned]
+            in_own = key_inside(tie(g, kv_own), q, v, at, 0, att_scale)
+            turned = turned_inputs(tie(inputs, kv_own), at)
+            done = [in_own, turned]
     qg.send(done)
     qg.send([])
-    kv_sent, kv_own = both_states(tie(v, inside_near, turned), keys, at)
-    qg_mine, qg_other = qg.send([kv_own])
+    in_oth = key_inside(tie(g, in_own, turned), q, v, at, 1, att_scale)
     kv = scan_states(lambda: kv_own, kv_sent, False, at)
     kv_got = next(kv)
     kv_stages = i_bits + 2
+    qg_own, qg_oth = qg.send([in_oth])
 
     def kv_next(*after):
         nonlocal kv_stages, kv_got
@@ -602,55 +686,50 @@
             kv_got = kv.send(list(after))
         return kv_got
 
-    ends = (at, att_scale, grad_scale, n_inner)
-    key_grad, p_far, q_far = key_product(inside_far, v, qg_mine, qg_other, turned, far_, *ends, None)
-    p_got, q_got = swap(p_far, "outer", 0), swap(q_far, "outer", 0)
-    key_grad, p, q = key_product(inside_near, v, qg_mine, qg_other, turned, near, *ends, key_grad)
-
-    p_send, p = fold(p, p_got, 0)
-    q_send, q = fold(q, q_got, 1)
+    ends = (att_scale, grad_scale)
+    in_own = tie(in_own, kv_got)
+    far_key, near_key, far_own, near_own = key_product(in_own, v, qg_own, turned, at, 0, (1, 0), *ends)
+    keys_own = [(far_key, (0, 1)), (near_key, (0, 0))]
+    got_own = swap(far_own, "outer", 0)
+    far_key, far_oth = key_product(in_oth, v, qg_oth, turned, at, 1, (1,), *ends)
+    got_oth = swap(far_oth, "outer", 0)
+    near_key, near_oth = key_product(in_oth, v, qg_oth, turned, at, 1, (0,), *ends)
+    pieces = keys_own + [(far_key, (1, 1)), (near_key, (1, 0))]
+
+    p_send, p, q_send, q = cores(at, near_own, near_oth, got_own, got_oth)
     p_got, q_got = swap(p_send, "outer", 1), swap(q_send, "inner", 0)
+    query_own, key_grad = query_inside(tie(g, p_send), k, v, at, 0, att_scale, pieces)
     kv_next(p_send, q_send)
     p_send, p = fold(p, p_got, 1)
     q_send, q = fold(q, q_got, 0)
+    p_send, q_send = tie(p_send, query_own), tie(q_send, query_own)
     p_got, q_got = swap(p_send, "inner", 0), swap(q_send, "outer", 1)
+    (query_oth,) = query_inside(tie(g, p_send, q_send), k, v, at, 1, att_scale)
     kv_next(p_send, q_send)
-    send, keep = merge(p, p_got, q, q_got)
-    for b in range(1, i_bits):
-        got = swap(send, "inner", b)
-        if b + 1 < i_bits:
-            send, keep = fold(keep, got, 1)
-            kv_next(send)
+    groups = bit_groups(i_bits)
+    keep, *sends = fan(2, 1 + len(groups[0]), p, p_got, q, q_got)
+    sends[0] = tie(sends[0], query_oth)
+    came = swap_all(sends, groups[0])
+    for masks in groups[1:]:
+        keep, *sends = fan(1, 1 + len(masks), keep, *came)
+        came = swap_all(sends, masks)
+    grad, weight = adam_own([keep, *came], master, moment1, moment2, at)
     while kv_stages > 1:
-        kv_next(send)
-    grad, weight = adam_own(keep, got, master, moment1, moment2, at)
-    kv_mine, kv_other = kv_next(weight)
-
-    query_grad = None
-    pair = 0
-
-    def query_next(count, after):
-        nonlocal query_grad, pair
-        if pair < width // PAIR:
-            args = (tie(kv_mine, after), kv_other, at, att_scale, pair, min(count, width // PAIR - pair))
-            query_grad = query_side(out_grad, keys, values, *args, query_grad)
-            pair += count
-        return query_grad
-
-    for b in reversed(range(1, i_bits)):
-        got = swap(weight, "inner", b)
-        if b == i_bits - 1:
-            grad_x = swap(grad, "outer", 1)
-        if b > 1:
-            weight = join(weight, got, 1)
-    p, q = split(weight, got)
+        kv_now = kv_next(weight)
+
+    grad_x = swap(grad, "outer", 1)
+    for masks in reversed(groups[1:]):
+        weight = join(1, weight, *swap_all([weight] * len(masks), masks))
+    p, q = split(weight, *swap_all([weight] * len(groups[0]), groups[0]))
+    p, q = tie(p, grad_x), tie(q, grad_x)
+    kv_own, kv_oth = kv_next(p, q)
     p_got, q_got = swap(p, "inner", 0), swap(q, "outer", 1)
     grads = [grad, swap(grad, "outer", 0), grad_x, swap(grad_x, "outer", 0)]
-    p, q = join(p, p_got, 1), join(q, q_got, 0)
+    p, q = join(1, p, p_got), join(0, q, q_got)
+    p, q = tie(p, kv_oth), tie(q, kv_oth)
     p_last, q_last = swap(p, "outer", 1), swap(q, "inner", 0)
     p_core, q_core = swap(p, "outer", 0), swap(q, "outer", 0)
-    query_next(2, p)
-    query_next(2, p)
+    query_grad = query_side(tie(g, p, q), query_own, query_oth, kv_own, kv_oth, at, att_scale)
     new_master, new_moment1, new_moment2 = adam_all(
         [tie(grads[0], p, q)] + grads[1:], master, moment1, moment2, at, (0, 1, 2, 3)
     )

time: 101 us -> 94.8 us (0.939)
  waiting for transfers between devices: 31.7 us -> 24.1 us
  starting transfers between devices: 36.1 us -> 38.5 us
    ppermute x33 -> x29, waiting for transfers between devices: 31.7 us -> 16.6 us  [swap(): return lax.ppermute(x, axis, [(i, i ^ 1 << bit) for i in range(n)])]
    ppermute x0 -> x6, starting transfers between devices: none -> 9.56 us  [swap_all(): lax.ppermute(x, 'inner', [(i, i ^ mask) for i in range(n)])]
    ppermute x0 -> x6, waiting for transfers between devices: none -> 7.54 us  [swap_all(): lax.ppermute(x, 'inner', [(i, i ^ mask) for i in range(n)])]
    ppermute x33 -> x29, starting transfers between devices: 36.1 us -> 28.9 us  [swap(): return lax.ppermute(x, axis, [(i, i ^ 1 << bit) for i in range(n)])]
    pallas_call x29 -> x32, Pallas kernels: 31.6 us -> 30.7 us  [call(): pl.pallas_call(body, in_specs=specs, out_specs=[WHOLE if near else HBM fo...]
  transfers between devices with their start and end apart: 33 -> 35, of which waited for: 18 -> 21; matrix products, arithmetic and copies ran while one was open for 1% -> 0% of each run, Pallas kernels for 25% -> 28%
where the time goes in v3:
time: 94.8 us; the launch traced here: 94.6 us
  starting transfers between devices  38.5 us (41%)
  Pallas kernels  30.7 us (32%)
  waiting for transfers between devices  24.1 us (25%)
  between operations  1.12 us (1%)
    pallas_call x32, Pallas kernels, call(): pl.pallas_call(body, in_specs=specs, out_specs=[WHOLE if near else HBM fo...  30.7 us
    ppermute x29, starting transfers between devices, swap(): return lax.ppermute(x, axis, [(i, i ^ 1 << bit) for i in range(n)])  28.9 us
    ppermute x29, waiting for transfers between devices, swap(): return lax.ppermute(x, axis, [(i, i ^ 1 << bit) for i in range(n)])  16.6 us
    ppermute x6, starting transfers between devices, swap_all(): lax.ppermute(x, 'inner', [(i, i ^ mask) for i in range(n)])  9.56 us
    ppermute x6, waiting for transfers between devices, swap_all(): lax.ppermute(x, 'inner', [(i, i ^ mask) for i in range(n)])  7.54 us
  transfers between devices with their start and end apart: 35, of which 21 were waited for; matrix products, arithmetic and copies ran while one was open for 0% of the time, Pallas kernels for 28%

profile of v3, /device:TPU:0, one launch (start us, length us, event | category | flops | bytes accessed | tf_op | source)
XLA Modules:
  0.0 94.6 jit_solution(8051879313302874649)
XLA Ops:
  0.6 2.2 %shard_map.130 = bf16[4,128,128]{2,1,0:T(8,128)(2,1)S(1)} custom-call(bf16[1024,1024]{1,0:T(8,128)(2,1)} %a_hbm.1, bf16[1024,1024]{1,0:T(8,128)(2,1)} %b_hbm.3), custom_call_target="tpu_custom_call" | custom-call | flops 134217728 | bytes 2097152 | tf_op jit(solution)/shard_map/pallas_call | solution.py:31
  2.8 3.0 %collective-permute-start.1 = (bf16[4,128,128]{2,1,0:T(8,128)(2,1)S(1)}, bf16[4,128,128]{2,1,0:T(8,128)(2,1)S(1)}, u32[]{:S(2)}, u32[]{:S(2)}) collective-permute-start(bf16[4,128,128]{2,1,0:T(8,128)(2,1)S(1)} %shard_map.130), channel_id=1, source_target_pairs={{0,1},{1,0},{2,3},{3,2},{4,5},{5,4},{6,7},{7,6},{8,9},{9,8},{10,11... | collective-permute-start | bytes 393224 | tf_op jit(solution)/shard_map/ppermute | solution.py:506
  5.8 3.3 %shard_map.127 = (f32[4,128,128]{2,1,0:T(8,128)S(1)}, bf16[1024,1024]{1,0:T(8,128)(2,1)S(1)}, bf16[1024,1024]{1,0:T(8,128)(2,1)S(1)}, bf16[1024,1024]{1,0:T(8,128)(2,1)S(1)}) custom-call(bf16[1024,1024]{1,0:T(8,128)(2,1)} %a_hbm.1, bf16[1024,1024]{1,0:T(8,128)(2,1)} %b_hbm.3, bf16[1024,1024]{1,0:T(8,128)(2,1)} %refs_2_.1), custom_call_target="tpu_custom_call" | custom-call | flops 134217728 | bytes 12582912 | tf_op jit(solution)/shard_map/pallas_call | solution.py:31
  9.4 1.9 %collective-permute-start.2 = (bf16[4,128,128]{2,1,0:T(8,128)(2,1)S(1)}, bf16[4,128,128]{2,1,0:T(8,128)(2,1)S(1)}, u32[]{:S(2)}, u32[]{:S(2)}) collective-permute-start(bf16[4,128,128]{2,1,0:T(8,128)(2,1)S(1)} %get-tuple-element.98), channel_id=1, source_target_pairs={{0,2},{1,3},{2,0},{3,1},{4,6},{5,7},{6,4},{7,5},{8,10},{9,11},{10,... | collective-permute-start | bytes 393224 | tf_op jit(solution)/shard_map/ppermute | solution.py:506
  11.2 2.9 %shard_map.128 = (bf16[4,128,128]{2,1,0:T(8,128)(2,1)S(1)}, f32[4,128,128]{2,1,0:T(8,128)S(1)}, bf16[1024,1024]{1,0:T(8,128)(2,1)S(1)}) custom-call(bf16[1024,1024]{1,0:T(8,128)(2,1)S(1)} %get-tuple-element.90.a_ref.v_ref, bf16[1024,1024]{1,0:T(8,128)(2,1)} %b_hbm.2), custom_call_target="tpu_custom_call" | custom-call | flops 268435456 | bytes 2097152 | tf_op jit(solution)/shard_map/pallas_call | solution.py:31
  14.5 2.9 %collective-permute-start.3 = (bf16[4,128,128]{2,1,0:T(8,128)(2,1)S(1)}, bf16[4,128,128]{2,1,0:T(8,128)(2,1)S(1)}, u32[]{:S(2)}, u32[]{:S(2)}) collective-permute-start(bf16[4,128,128]{2,1,0:T(8,128)(2,1)S(1)} %get-tuple-element.102), channel_id=1, source_target_pairs={{0,4},{1,5},{2,6},{3,7},{4,0},{5,1},{6,2},{7,3},{8,12},{9,13},{10,... | collective-permute-start | bytes 393224 | tf_op jit(solution)/shard_map/ppermute | solution.py:506
  17.3 2.0 %shard_map.133.turned_ref = bf16[1024,1024]{1,0:T(8,128)(2,1)S(1)} custom-call(bf16[1024,1024]{1,0:T(8,128)(2,1)} %in_hbm), custom_call_target="tpu_custom_call" | custom-call | bytes 4194304 | tf_op jit(solution)/shard_map/pallas_call | solution.py:31
  19.4 2.0 %shard_map.129.inside_ref = f32[1024,512]{1,0:T(8,128)S(1)} custom-call(bf16[1024,1024]{1,0:T(8,128)(2,1)S(1)} %get-tuple-element.163.g_ref, bf16[1024,1024]{1,0:T(8,128)(2,1)S(1)} %get-tuple-element.93.q_ref, bf16[1024,1024]{1,0:T(8,128)(2,1)S(1)} %get-tuple-element.90.a_ref.v_ref), custom_call_target="tpu_custom_call" | custom-call | flops 805306368 | bytes 5242880 | tf_op jit(solution)/shard_map/pallas_call | solution.py:31
  23.8 1.6 %collective-permute-start.5 = (bf16[4,128,128]{2,1,0:T(8,128)(2,1)S(1)}, bf16[4,128,128]{2,1,0:T(8,128)(2,1)S(1)}, u32[]{:S(2)}, u32[]{:S(2)}) collective-permute-start(bf16[4,128,128]{2,1,0:T(8,128)(2,1)S(1)} %get-tuple-element.110), channel_id=1, source_target_pairs={{0,16},{8,24},{16,0},{24,8},{1,17},{9,25},{17,1},{25,9},{2,18},{10... | collective-permute-start | bytes 393224 | tf_op jit(solution)/shard_map/ppermute | solution.py:506
  26.7 2.0 %shard_map.136.inside_ref = f32[1024,512]{1,0:T(8,128)S(1)} custom-call(bf16[1024,1024]{1,0:T(8,128)(2,1)S(1)} %get-tuple-element.163.g_ref, bf16[1024,1024]{1,0:T(8,128)(2,1)S(1)} %get-tuple-element.93.q_ref, bf16[1024,1024]{1,0:T(8,128)(2,1)S(1)} %get-tuple-element.90.a_ref.v_ref), custom_call_target="tpu_custom_call" | custom-call | flops 805306368 | bytes 5242880 | tf_op jit(solution)/shard_map/pallas_call | solution.py:31
  30.9 1.7 %shard_map.138 = (bf16[1024,256]{1,0:T(8,128)(2,1)S(1)}, bf16[1024,256]{1,0:T(8,128)(2,1)S(1)}, bf16[2,8,64,256]{3,2,1,0:T(8,128)(2,1)S(1)}, bf16[2,8,64,256]{3,2,1,0:T(8,128)(2,1)S(1)}) custom-call(f32[1024,512]{1,0:T(8,128)S(1)} %shard_map.129.inside_ref, bf16[1024,1024]{1,0:T(8,128)(2,1)S(1)} %get-tuple-element.90.a_ref.v_ref, ...), custom_call_target="tpu_custom_call" | custom-call | flops 1207959552 | bytes 6291456 | tf_op jit(solution)/shard_map/pallas_call | solution.py:31
  32.8 1.8 %collective-permute-done.6.state_ref = bf16[4,128,128]{2,1,0:T(8,128)(2,1)S(1)} collective-permute-done((bf16[4,128,128]{2,1,0:T(8,128)(2,1)S(1)}, bf16[4,128,128]{2,1,0:T(8,128)(2,1)S(1)}, u32[]{:S(2)}, u32[]{:S(2)}) %collective-permute-start.6) | collective-permute-done | bytes 131104 | tf_op jit(solution)/shard_map/ppermute | solution.py:506
  38.0 1.6 %collective-permute-start.9 = (bf16[1,8,64,256]{3,2,1,0:T(8,128)(2,1)S(1)}, bf16[1,8,64,256]{3,2,1,0:T(8,128)(2,1)S(1)}, u32[]{:S(2)}, u32[]{:S(2)}) collective-permute-start(bf16[1,8,64,256]{3,2,1,0:T(8,128)(2,1)S(1)} %get-tuple-element.120), channel_id=1, source_target_pairs={{0,16},{8,24},{16,0},{24,8},{1,17},{9,25},{17,1},{25,9},{2,18},{10... | collective-permute-start | bytes 786440 | tf_op jit(solution)/shard_map/ppermute | solution.py:506
  41.9 3.2 %shard_map.142 = (f32[1024,512]{1,0:T(8,128)S(1)}, bf16[1024,1024]{1,0:T(8,128)(2,1)}) custom-call(bf16[1024,1024]{1,0:T(8,128)(2,1)S(1)} %get-tuple-element.163.g_ref, bf16[1024,1024]{1,0:T(8,128)(2,1)S(1)} %get-tuple-element.122.k_ref, bf16[1024,1024]{1,0:T(8,128)(2,1)S(1)} %get-tuple-element.90.a_ref.v_ref, ...), custom_call_target="tpu_custom_call" | custom-call | flops 805306368 | bytes 5242880 | tf_op jit(solution)/shard_map/pallas_call | solution.py:31
  48.0 1.6 %collective-permute-start.12 = (bf16[1,4,64,256]{3,2,1,0:T(8,128)(2,1)S(1)}, bf16[1,4,64,256]{3,2,1,0:T(8,128)(2,1)S(1)}, u32[]{:S(2)}, u32[]{:S(2)}) collective-permute-start(bf16[1,4,64,256]{3,2,1,0:T(8,128)(2,1)S(1)} %get-tuple-element.131), channel_id=1, source_target_pairs={{0,16},{8,24},{16,0},{24,8},{1,17},{9,25},{17,1},{25,9},{2,18},{10... | collective-permute-start | bytes 393224 | tf_op jit(solution)/shard_map/ppermute | solution.py:506
  50.9 2.1 %shard_map.144.in_oth = f32[1024,512]{1,0:T(8,128)S(1)} custom-call(bf16[1024,1024]{1,0:T(8,128)(2,1)S(1)} %get-tuple-element.163.g_ref, bf16[1024,1024]{1,0:T(8,128)(2,1)S(1)} %get-tuple-element.122.k_ref, bf16[1024,1024]{1,0:T(8,128)(2,1)S(1)} %get-tuple-element.90.a_ref.v_ref), custom_call_target="tpu_custom_call" | custom-call | flops 805306368 | bytes 5242880 | tf_op jit(solution)/shard_map/pallas_call | solution.py:31
  53.1 1.8 %collective-permute-start.13 = (bf16[2,1,64,256]{3,2,1,0:T(8,128)(2,1)S(1)}, bf16[2,1,64,256]{3,2,1,0:T(8,128)(2,1)S(1)}, u32[]{:S(2)}, u32[]{:S(2)}) collective-permute-start(bf16[2,1,64,256]{3,2,1,0:T(8,128)(2,1)S(1)} %get-tuple-element.135), channel_id=1, source_target_pairs={{0,4},{1,5},{2,6},{3,7},{4,0},{5,1},{6,2},{7,3},{8,12},{9,13},{10,... | collective-permute-start | bytes 196616 | tf_op jit(solution)/shard_map/ppermute | solution.py:599
  54.8 2.3 %collective-permute-start.14 = (bf16[2,1,64,256]{3,2,1,0:T(8,128)(2,1)S(1)}, bf16[2,1,64,256]{3,2,1,0:T(8,128)(2,1)S(1)}, u32[]{:S(2)}, u32[]{:S(2)}) collective-permute-start(bf16[2,1,64,256]{3,2,1,0:T(8,128)(2,1)S(1)} %get-tuple-element.136), channel_id=1, source_target_pairs={{0,2},{1,3},{2,0},{3,1},{4,6},{5,7},{6,4},{7,5},{8,10},{9,11},{10,... | collective-permute-start | bytes 196616 | tf_op jit(solution)/shard_map/ppermute | solution.py:599
  58.2 3.6 %collective-permute-done.13.refs_1_ = bf16[2,1,64,256]{3,2,1,0:T(8,128)(2,1)S(1)} collective-permute-done((bf16[2,1,64,256]{3,2,1,0:T(8,128)(2,1)S(1)}, bf16[2,1,64,256]{3,2,1,0:T(8,128)(2,1)S(1)}, u32[]{:S(2)}, u32[]{:S(2)}) %collective-permute-start.13) | collective-permute-done | bytes 65568 | tf_op jit(solution)/shard_map/ppermute | solution.py:599
  64.9 1.5 %collective-permute-start.24 = (bf16[4,128,128]{2,1,0:T(8,128)(2,1)S(1)}, bf16[4,128,128]{2,1,0:T(8,128)(2,1)S(1)}, u32[]{:S(2)}, u32[]{:S(2)}) collective-permute-start(bf16[4,128,128]{2,1,0:T(8,128)(2,1)S(1)} %get-tuple-element.156), channel_id=1, source_target_pairs={{0,16},{8,24},{16,0},{24,8},{1,17},{9,25},{17,1},{25,9},{2,18},{10... | collective-permute-start | bytes 393224 | tf_op jit(solution)/shard_map/ppermute | solution.py:506
  67.8 3.0 %collective-permute-start.18 = (bf16[2,1,64,256]{3,2,1,0:T(8,128)(2,1)S(1)}, bf16[2,1,64,256]{3,2,1,0:T(8,128)(2,1)S(1)}, u32[]{:S(2)}, u32[]{:S(2)}) collective-permute-start(bf16[2,1,64,256]{3,2,1,0:T(8,128)(2,1)S(1)} %get-tuple-element.138.refs_0_), channel_id=1, source_target_pairs={{0,6},{1,7},{2,4},{3,5},{4,2},{5,3},{6,0},{7,1},{8,14},{9,15},{10,... | collective-permute-start | bytes 196616 | tf_op jit(solution)/shard_map/ppermute | solution.py:599
  77.8 2.2 %collective-permute-done.20.refs_1_ = bf16[1,4,64,256]{3,2,1,0:T(8,128)(2,1)S(1)} collective-permute-done((bf16[1,4,64,256]{3,2,1,0:T(8,128)(2,1)S(1)}, bf16[1,4,64,256]{3,2,1,0:T(8,128)(2,1)S(1)}, u32[]{:S(2)}, u32[]{:S(2)}) %collective-permute-start.20) | collective-permute-done | bytes 131104 | tf_op jit(solution)/shard_map/ppermute | solution.py:506
  83.2 1.5 %collective-permute-start.33 = (bf16[2,4,64,256]{3,2,1,0:T(8,128)(2,1)S(1)}, bf16[2,4,64,256]{3,2,1,0:T(8,128)(2,1)S(1)}, u32[]{:S(2)}, u32[]{:S(2)}) collective-permute-start(bf16[2,4,64,256]{3,2,1,0:T(8,128)(2,1)S(1)} %shard_map.153.refs_1_), channel_id=1, source_target_pairs={{0,1},{1,0},{2,3},{3,2},{4,5},{5,4},{6,7},{7,6},{8,9},{9,8},{10,11... | collective-permute-start | bytes 786440 | tf_op jit(solution)/shard_map/ppermute | solution.py:506
  88.6 1.8 %shard_map.154 = bf16[1024,1024]{1,0:T(8,128)(2,1)} custom-call(bf16[1024,1024]{1,0:T(8,128)(2,1)S(1)} %get-tuple-element.163.g_ref, f32[1024,512]{1,0:T(8,128)S(1)} %get-tuple-element.127.in_own, f32[1024,512]{1,0:T(8,128)S(1)} %shard_map.144.in_oth, bf16[4,128,128]{2,1,0:T(8,128)(2,1)S(1)} %get-tuple-element.164.own_ref, ...), custom_call_target="tpu_custom_call" | custom-call | flops 268435456 | bytes 8388608 | tf_op jit(solution)/shard_map/pallas_call | solution.py:31
  (86 shorter events, 40.2 us)
Async XLA Ops:
  2.8 6.5 %collective-permute-start.1 = (bf16[4,128,128]{2,1,0:T(8,128)(2,1)S(1)}, bf16[4,128,128]{2,1,0:T(8,128)(2,1)S(1)}, u32[]{:S(2)}, u32[]{:S(2)}) collective-permute-start(bf16[4,128,128]{2,1,0:T(8,128)(2,1)S(1)} %shard_map.130), channel_id=1, source_target_pairs={{0,1},{1,0},{2,3},{3,2},{4,5},{5,4},{6,7},{7,6},{8,9},{9,8},{10,11... | collective-permute-start | bytes 393224 | tf_op jit(solution)/shard_map/ppermute | solution.py:506
  9.4 5.0 %collective-permute-start.2 = (bf16[4,128,128]{2,1,0:T(8,128)(2,1)S(1)}, bf16[4,128,128]{2,1,0:T(8,128)(2,1)S(1)}, u32[]{:S(2)}, u32[]{:S(2)}) collective-permute-start(bf16[4,128,128]{2,1,0:T(8,128)(2,1)S(1)} %get-tuple-element.98), channel_id=1, source_target_pairs={{0,2},{1,3},{2,0},{3,1},{4,6},{5,7},{6,4},{7,5},{8,10},{9,11},{10,... | collective-permute-start | bytes 393224 | tf_op jit(solution)/shard_map/ppermute | solution.py:506
  14.5 7.8 %collective-permute-start.3 = (bf16[4,128,128]{2,1,0:T(8,128)(2,1)S(1)}, bf16[4,128,128]{2,1,0:T(8,128)(2,1)S(1)}, u32[]{:S(2)}, u32[]{:S(2)}) collective-permute-start(bf16[4,128,128]{2,1,0:T(8,128)(2,1)S(1)} %get-tuple-element.102), channel_id=1, source_target_pairs={{0,4},{1,5},{2,6},{3,7},{4,0},{5,1},{6,2},{7,3},{8,12},{9,13},{10,... | collective-permute-start | bytes 393224 | tf_op jit(solution)/shard_map/ppermute | solution.py:506
  23.8 5.6 %collective-permute-start.5 = (bf16[4,128,128]{2,1,0:T(8,128)(2,1)S(1)}, bf16[4,128,128]{2,1,0:T(8,128)(2,1)S(1)}, u32[]{:S(2)}, u32[]{:S(2)}) collective-permute-start(bf16[4,128,128]{2,1,0:T(8,128)(2,1)S(1)} %get-tuple-element.110), channel_id=1, source_target_pairs={{0,16},{8,24},{16,0},{24,8},{1,17},{9,25},{17,1},{25,9},{2,18},{10... | collective-permute-start | bytes 393224 | tf_op jit(solution)/shard_map/ppermute | solution.py:506
  25.4 5.6 %collective-permute-start = (bf16[4,128,128]{2,1,0:T(8,128)(2,1)S(1)}, bf16[4,128,128]{2,1,0:T(8,128)(2,1)S(1)}, u32[]{:S(2)}, u32[]{:S(2)}) collective-permute-start(bf16[4,128,128]{2,1,0:T(8,128)(2,1)S(1)} %get-tuple-element.94), channel_id=1, source_target_pairs={{0,1},{1,0},{2,3},{3,2},{4,5},{5,4},{6,7},{7,6},{8,9},{9,8},{10,11... | collective-permute-start | bytes 393224 | tf_op jit(solution)/shard_map/ppermute | solution.py:506
  29.5 5.0 %collective-permute-start.6 = (bf16[4,128,128]{2,1,0:T(8,128)(2,1)S(1)}, bf16[4,128,128]{2,1,0:T(8,128)(2,1)S(1)}, u32[]{:S(2)}, u32[]{:S(2)}) collective-permute-start(bf16[4,128,128]{2,1,0:T(8,128)(2,1)S(1)} %get-tuple-element.115), channel_id=1, source_target_pairs={{0,1},{1,0},{2,3},{3,2},{4,5},{5,4},{6,7},{7,6},{8,9},{9,8},{10,11... | collective-permute-start | bytes 393224 | tf_op jit(solution)/shard_map/ppermute | solution.py:506
  38.0 8.4 %collective-permute-start.9 = (bf16[1,8,64,256]{3,2,1,0:T(8,128)(2,1)S(1)}, bf16[1,8,64,256]{3,2,1,0:T(8,128)(2,1)S(1)}, u32[]{:S(2)}, u32[]{:S(2)}) collective-permute-start(bf16[1,8,64,256]{3,2,1,0:T(8,128)(2,1)S(1)} %get-tuple-element.120), channel_id=1, source_target_pairs={{0,16},{8,24},{16,0},{24,8},{1,17},{9,25},{17,1},{25,9},{2,18},{10... | collective-permute-start | bytes 786440 | tf_op jit(solution)/shard_map/ppermute | solution.py:506
  39.6 8.3 %collective-permute-start.11 = (bf16[2,4,64,256]{3,2,1,0:T(8,128)(2,1)S(1)}, bf16[2,4,64,256]{3,2,1,0:T(8,128)(2,1)S(1)}, u32[]{:S(2)}, u32[]{:S(2)}) collective-permute-start(bf16[2,4,64,256]{3,2,1,0:T(8,128)(2,1)S(1)} %get-tuple-element.130), channel_id=1, source_target_pairs={{0,1},{1,0},{2,3},{3,2},{4,5},{5,4},{6,7},{7,6},{8,9},{9,8},{10,11... | collective-permute-start | bytes 786440 | tf_op jit(solution)/shard_map/ppermute | solution.py:506
  41.0 8.6 %collective-permute-start.21 = (bf16[4,128,128]{2,1,0:T(8,128)(2,1)S(1)}, bf16[4,128,128]{2,1,0:T(8,128)(2,1)S(1)}, u32[]{:S(2)}, u32[]{:S(2)}) collective-permute-start(bf16[4,128,128]{2,1,0:T(8,128)(2,1)S(1)} %get-tuple-element.144), channel_id=1, source_target_pairs={{0,2},{1,3},{2,0},{3,1},{4,6},{5,7},{6,4},{7,5},{8,10},{9,11},{10,... | collective-permute-start | bytes 393224 | tf_op jit(solution)/shard_map/ppermute | solution.py:506
  46.5 6.5 %collective-permute-start.10 = (bf16[1,4,64,256]{3,2,1,0:T(8,128)(2,1)S(1)}, bf16[1,4,64,256]{3,2,1,0:T(8,128)(2,1)S(1)}, u32[]{:S(2)}, u32[]{:S(2)}) collective-permute-start(bf16[1,4,64,256]{3,2,1,0:T(8,128)(2,1)S(1)} %get-tuple-element.128), channel_id=1, source_target_pairs={{0,1},{1,0},{2,3},{3,2},{4,5},{5,4},{6,7},{7,6},{8,9},{9,8},{10,11... | collective-permute-start | bytes 393224 | tf_op jit(solution)/shard_map/ppermute | solution.py:506
  48.0 5.0 %collective-permute-start.12 = (bf16[1,4,64,256]{3,2,1,0:T(8,128)(2,1)S(1)}, bf16[1,4,64,256]{3,2,1,0:T(8,128)(2,1)S(1)}, u32[]{:S(2)}, u32[]{:S(2)}) collective-permute-start(bf16[1,4,64,256]{3,2,1,0:T(8,128)(2,1)S(1)} %get-tuple-element.131), channel_id=1, source_target_pairs={{0,16},{8,24},{16,0},{24,8},{1,17},{9,25},{17,1},{25,9},{2,18},{10... | collective-permute-start | bytes 393224 | tf_op jit(solution)/shard_map/ppermute | solution.py:506
  49.6 13.7 %collective-permute-start.22 = (bf16[4,128,128]{2,1,0:T(8,128)(2,1)S(1)}, bf16[4,128,128]{2,1,0:T(8,128)(2,1)S(1)}, u32[]{:S(2)}, u32[]{:S(2)}) collective-permute-start(bf16[4,128,128]{2,1,0:T(8,128)(2,1)S(1)} %get-tuple-element.148), channel_id=1, source_target_pairs={{0,4},{1,5},{2,6},{3,7},{4,0},{5,1},{6,2},{7,3},{8,12},{9,13},{10,... | collective-permute-start | bytes 393224 | tf_op jit(solution)/shard_map/ppermute | solution.py:506
  53.1 8.7 %collective-permute-start.13 = (bf16[2,1,64,256]{3,2,1,0:T(8,128)(2,1)S(1)}, bf16[2,1,64,256]{3,2,1,0:T(8,128)(2,1)S(1)}, u32[]{:S(2)}, u32[]{:S(2)}) collective-permute-start(bf16[2,1,64,256]{3,2,1,0:T(8,128)(2,1)S(1)} %get-tuple-element.135), channel_id=1, source_target_pairs={{0,4},{1,5},{2,6},{3,7},{4,0},{5,1},{6,2},{7,3},{8,12},{9,13},{10,... | collective-permute-start | bytes 196616 | tf_op jit(solution)/shard_map/ppermute | solution.py:599
  54.8 7.0 %collective-permute-start.14 = (bf16[2,1,64,256]{3,2,1,0:T(8,128)(2,1)S(1)}, bf16[2,1,64,256]{3,2,1,0:T(8,128)(2,1)S(1)}, u32[]{:S(2)}, u32[]{:S(2)}) collective-permute-start(bf16[2,1,64,256]{3,2,1,0:T(8,128)(2,1)S(1)} %get-tuple-element.136), channel_id=1, source_target_pairs={{0,2},{1,3},{2,0},{3,1},{4,6},{5,7},{6,4},{7,5},{8,10},{9,11},{10,... | collective-permute-start | bytes 196616 | tf_op jit(solution)/shard_map/ppermute | solution.py:599
  57.1 6.1 %collective-permute-start.15 = (bf16[2,1,64,256]{3,2,1,0:T(8,128)(2,1)S(1)}, bf16[2,1,64,256]{3,2,1,0:T(8,128)(2,1)S(1)}, u32[]{:S(2)}, u32[]{:S(2)}) collective-permute-start(bf16[2,1,64,256]{3,2,1,0:T(8,128)(2,1)S(1)} %get-tuple-element.137), channel_id=1, source_target_pairs={{0,6},{1,7},{2,4},{3,5},{4,2},{5,3},{6,0},{7,1},{8,14},{9,15},{10,... | collective-permute-start | bytes 196616 | tf_op jit(solution)/shard_map/ppermute | solution.py:599
  64.9 11.8 %collective-permute-start.24 = (bf16[4,128,128]{2,1,0:T(8,128)(2,1)S(1)}, bf16[4,128,128]{2,1,0:T(8,128)(2,1)S(1)}, u32[]{:S(2)}, u32[]{:S(2)}) collective-permute-start(bf16[4,128,128]{2,1,0:T(8,128)(2,1)S(1)} %get-tuple-element.156), channel_id=1, source_target_pairs={{0,16},{8,24},{16,0},{24,8},{1,17},{9,25},{17,1},{25,9},{2,18},{10... | collective-permute-start | bytes 393224 | tf_op jit(solution)/shard_map/ppermute | solution.py:506
  66.4 6.3 %collective-permute-start.16 = (bf16[2,1,64,256]{3,2,1,0:T(8,128)(2,1)S(1)}, bf16[2,1,64,256]{3,2,1,0:T(8,128)(2,1)S(1)}, u32[]{:S(2)}, u32[]{:S(2)}) collective-permute-start(bf16[2,1,64,256]{3,2,1,0:T(8,128)(2,1)S(1)} %get-tuple-element.138.refs_0_), channel_id=1, source_target_pairs={{0,4},{1,5},{2,6},{3,7},{4,0},{5,1},{6,2},{7,3},{8,12},{9,13},{10,... | collective-permute-start | bytes 196616 | tf_op jit(solution)/shard_map/ppermute | solution.py:599
  66.7 6.1 %collective-permute-start.17 = (bf16[2,1,64,256]{3,2,1,0:T(8,128)(2,1)S(1)}, bf16[2,1,64,256]{3,2,1,0:T(8,128)(2,1)S(1)}, u32[]{:S(2)}, u32[]{:S(2)}) collective-permute-start(bf16[2,1,64,256]{3,2,1,0:T(8,128)(2,1)S(1)} %get-tuple-element.138.refs_0_), channel_id=1, source_target_pairs={{0,2},{1,3},{2,0},{3,1},{4,6},{5,7},{6,4},{7,5},{8,10},{9,11},{10,... | collective-permute-start | bytes 196616 | tf_op jit(solution)/shard_map/ppermute | solution.py:599
  67.8 6.2 %collective-permute-start.18 = (bf16[2,1,64,256]{3,2,1,0:T(8,128)(2,1)S(1)}, bf16[2,1,64,256]{3,2,1,0:T(8,128)(2,1)S(1)}, u32[]{:S(2)}, u32[]{:S(2)}) collective-permute-start(bf16[2,1,64,256]{3,2,1,0:T(8,128)(2,1)S(1)} %get-tuple-element.138.refs_0_), channel_id=1, source_target_pairs={{0,6},{1,7},{2,4},{3,5},{4,2},{5,3},{6,0},{7,1},{8,14},{9,15},{10,... | collective-permute-start | bytes 196616 | tf_op jit(solution)/shard_map/ppermute | solution.py:599
  76.8 5.0 %collective-permute-start.25 = (bf16[4,128,128]{2,1,0:T(8,128)(2,1)S(1)}, bf16[4,128,128]{2,1,0:T(8,128)(2,1)S(1)}, u32[]{:S(2)}, u32[]{:S(2)}) collective-permute-start(bf16[4,128,128]{2,1,0:T(8,128)(2,1)S(1)} %get-tuple-element.160), channel_id=1, source_target_pairs={{0,1},{1,0},{2,3},{3,2},{4,5},{5,4},{6,7},{7,6},{8,9},{9,8},{10,11... | collective-permute-start | bytes 393224 | tf_op jit(solution)/shard_map/ppermute | solution.py:506
  81.8 8.6 %collective-permute-start.30 = (bf16[1,8,64,256]{3,2,1,0:T(8,128)(2,1)S(1)}, bf16[1,8,64,256]{3,2,1,0:T(8,128)(2,1)S(1)}, u32[]{:S(2)}, u32[]{:S(2)}) collective-permute-start(bf16[1,8,64,256]{3,2,1,0:T(8,128)(2,1)S(1)} %shard_map.147.refs_0_), channel_id=1, source_target_pairs={{0,8},{8,0},{16,24},{24,16},{1,9},{9,1},{17,25},{25,17},{2,10},{10... | collective-permute-start | bytes 786440 | tf_op jit(solution)/shard_map/ppermute | solution.py:506
  81.8 8.6 %collective-permute-start.31 = (bf16[2,4,64,256]{3,2,1,0:T(8,128)(2,1)S(1)}, bf16[2,4,64,256]{3,2,1,0:T(8,128)(2,1)S(1)}, u32[]{:S(2)}, u32[]{:S(2)}) collective-permute-start(bf16[2,4,64,256]{3,2,1,0:T(8,128)(2,1)S(1)} %shard_map.153.refs_1_), channel_id=1, source_target_pairs={{0,8},{8,0},{16,24},{24,16},{1,9},{9,1},{17,25},{25,17},{2,10},{10... | collective-permute-start | bytes 786440 | tf_op jit(solution)/shard_map/ppermute | solution.py:506
  82.3 9.2 %collective-permute-start.29 = (bf16[1,8,64,256]{3,2,1,0:T(8,128)(2,1)S(1)}, bf16[1,8,64,256]{3,2,1,0:T(8,128)(2,1)S(1)}, u32[]{:S(2)}, u32[]{:S(2)}) collective-permute-start(bf16[1,8,64,256]{3,2,1,0:T(8,128)(2,1)S(1)} %shard_map.147.refs_0_), channel_id=1, source_target_pairs={{0,16},{8,24},{16,0},{24,8},{1,17},{9,25},{17,1},{25,9},{2,18},{10... | collective-permute-start | bytes 786440 | tf_op jit(solution)/shard_map/ppermute | solution.py:506
  83.2 8.5 %collective-permute-start.33 = (bf16[2,4,64,256]{3,2,1,0:T(8,128)(2,1)S(1)}, bf16[2,4,64,256]{3,2,1,0:T(8,128)(2,1)S(1)}, u32[]{:S(2)}, u32[]{:S(2)}) collective-permute-start(bf16[2,4,64,256]{3,2,1,0:T(8,128)(2,1)S(1)} %shard_map.153.refs_1_), channel_id=1, source_target_pairs={{0,1},{1,0},{2,3},{3,2},{4,5},{5,4},{6,7},{7,6},{8,9},{9,8},{10,11... | collective-permute-start | bytes 786440 | tf_op jit(solution)/shard_map/ppermute | solution.py:506
  (14 other events, 69.8 us)

commit v4 on v3

--- a/solution.py
+++ b/solution.py
@@ -623,19 +623,40 @@
     return call(body, list(arrays), [WHOLE] * len(arrays), [(shape, BF16, True)])[0]
 
 
-def split_body(*refs):
-    outs = refs[-2:]
-    for j, ref in enumerate(refs[:-2]):
-        n = ref.shape[1]
-        for i, out in enumerate(outs):
-            out[:, j * n : (j + 1) * n] = ref[i : i + 1]
-
-
-def split(*arrays):
+def split_body(n_pieces, *refs):
+    pieces, grad_ref, (p_out, q_out) = refs[:n_pieces], refs[n_pieces], refs[n_pieces + 1 :]
+    for j, ref in enumerate(pieces):
+        n, part = ref.shape[1:3]
+        p_out[:, j * n : (j + 1) * n] = ref[0:1]
+        q_out[:, j * n : (j + 1) * n] = ref[1:2]
+    for i in range(2):
+        q_out[0, n_pieces * n + i] = grad_ref[i * part : (i + 1) * part]
+
+
+def split(grad, *arrays):
     _, n, part, cols = arrays[0].shape
-    return call(
-        split_body, list(arrays), [WHOLE] * len(arrays), [((1, len(arrays) * n, part, cols), BF16, True)] * 2
-    )
+    n_pieces = len(arrays)
+    shapes = [(1, n_pieces * n, part, cols), (1, n_pieces * n + 2, part, cols)]
+    return call(
+        functools.partial(split_body, n_pieces),
+        [*arrays, grad],
+        [WHOLE] * (n_pieces + 1),
+        [(shape, BF16, True) for shape in shapes],
+    )
+
+
+def rejoin_body(a_ref, b_ref, out, grad_out):
+    n, part = out.shape[1:3]
+    out[0:1] = a_ref[:, :n]
+    out[1:2] = b_ref[:, :n]
+    for i in range(2):
+        grad_out[i * part : (i + 1) * part] = b_ref[0, n + i]
+
+
+def rejoin(a, b):
+    _, n, part, cols = a.shape
+    outs = [((2, n - 2, part, cols), BF16, True), ((2 * part, cols), BF16, True)]
+    return call(rejoin_body, [a, b], [WHOLE] * 2, outs)
 
 
 def local(inputs, queries, keys, values, out_grad, master, moment1, moment2):
@@ -662,22 +683,22 @@
     qg.send([])
     g, q, v = loaded[1:]
     kv_sent, kv_own, k = both_states(v, keys, at)
+    kv = scan_states(lambda: kv_own, kv_sent, False, at)
+    kv_stages = i_bits + 2
     done = [kv_own]
-    turned = None
+    in_own = kv_got = None
     for _ in range(2, i_bits):
         qg.send(done)
         done = []
-        if turned is None:
+        if in_own is None:
             in_own = key_inside(tie(g, kv_own), q, v, at, 0, att_scale)
-            turned = turned_inputs(tie(inputs, kv_own), at)
-            done = [in_own, turned]
+            kv_got = next(kv)
+            done = [in_own] + [kv_got] * 1
     qg.send(done)
     qg.send([])
-    in_oth = key_inside(tie(g, in_own, turned), q, v, at, 1, att_scale)
-    kv = scan_states(lambda: kv_own, kv_sent, False, at)
-    kv_got = next(kv)
-    kv_stages = i_bits + 2
+    in_oth = key_inside(tie(g, in_own), q, v, at, 1, att_scale)
     qg_own, qg_oth = qg.send([in_oth])
+    turned = turned_inputs(tie(inputs, in_oth), at)
 
     def kv_next(*after):
         nonlocal kv_stages, kv_got
@@ -687,7 +708,7 @@
         return kv_got
 
     ends = (att_scale, grad_scale)
-    in_own = tie(in_own, kv_got)
+    in_own = tie(in_own, kv_next())
     far_key, near_key, far_own, near_own = key_product(in_own, v, qg_own, turned, at, 0, (1, 0), *ends)
     keys_own = [(far_key, (0, 1)), (near_key, (0, 0))]
     got_own = swap(far_own, "outer", 0)
@@ -698,37 +719,36 @@
 
     p_send, p, q_send, q = cores(at, near_own, near_oth, got_own, got_oth)
     p_got, q_got = swap(p_send, "outer", 1), swap(q_send, "inner", 0)
-    query_own, key_grad = query_inside(tie(g, p_send), k, v, at, 0, att_scale, pieces)
     kv_next(p_send, q_send)
     p_send, p = fold(p, p_got, 1)
     q_send, q = fold(q, q_got, 0)
-    p_send, q_send = tie(p_send, query_own), tie(q_send, query_own)
     p_got, q_got = swap(p_send, "inner", 0), swap(q_send, "outer", 1)
-    (query_oth,) = query_inside(tie(g, p_send, q_send), k, v, at, 1, att_scale)
-    kv_next(p_send, q_send)
+    query_own, key_grad = query_inside(tie(g, p_send, q_send), k, v, at, 0, att_scale, pieces)
+    kv_next(p_send, q_send, query_own)
     groups = bit_groups(i_bits)
     keep, *sends = fan(2, 1 + len(groups[0]), p, p_got, q, q_got)
-    sends[0] = tie(sends[0], query_oth)
+    sends[0] = tie(sends[0], query_own)
     came = swap_all(sends, groups[0])
+    (query_oth,) = query_inside(tie(g, *sends), k, v, at, 1, att_scale)
     for masks in groups[1:]:
         keep, *sends = fan(1, 1 + len(masks), keep, *came)
         came = swap_all(sends, masks)
+    while kv_stages > 1:
+        kv_next(query_oth)
     grad, weight = adam_own([keep, *came], master, moment1, moment2, at)
-    while kv_stages > 1:
-        kv_now = kv_next(weight)
-
-    grad_x = swap(grad, "outer", 1)
+    weight = tie(weight, query_oth)
+    kv_own, kv_oth = kv_next(weight)
+
     for masks in reversed(groups[1:]):
         weight = join(1, weight, *swap_all([weight] * len(masks), masks))
-    p, q = split(weight, *swap_all([weight] * len(groups[0]), groups[0]))
-    p, q = tie(p, grad_x), tie(q, grad_x)
-    kv_own, kv_oth = kv_next(p, q)
+    p, q = split(grad, weight, *swap_all([weight] * len(groups[0]), groups[0]))
     p_got, q_got = swap(p, "inner", 0), swap(q, "outer", 1)
-    grads = [grad, swap(grad, "outer", 0), grad_x, swap(grad_x, "outer", 0)]
-    p, q = join(1, p, p_got), join(0, q, q_got)
-    p, q = tie(p, kv_oth), tie(q, kv_oth)
+    p = join(1, p, p_got)
+    q, grad_x = rejoin(q, q_got)
+    p, q, kv_oth = lax.optimization_barrier((p, q, kv_oth))
     p_last, q_last = swap(p, "outer", 1), swap(q, "inner", 0)
     p_core, q_core = swap(p, "outer", 0), swap(q, "outer", 0)
+    grads = [grad, swap(grad, "outer", 0), grad_x, swap(grad_x, "outer", 0)]
     query_grad = query_side(tie(g, p, q), query_own, query_oth, kv_own, kv_oth, at, att_scale)
     new_master, new_moment1, new_moment2 = adam_all(
         [tie(grads[0], p, q)] + grads[1:], master, moment1, moment2, at, (0, 1, 2, 3)

time: 94.8 us -> 91.8 us (0.968)
  starting transfers between devices: 38.5 us -> 35 us
    ppermute x29 -> x28, starting transfers between devices: 28.9 us -> 26.1 us  [swap(): return lax.ppermute(x, axis, [(i, i ^ 1 << bit) for i in range(n)])]
    ppermute x29 -> x28, waiting for transfers between devices: 16.6 us -> 19 us  [swap(): return lax.ppermute(x, axis, [(i, i ^ 1 << bit) for i in range(n)])]
    ppermute x6, waiting for transfers between devices: 7.54 us -> 5.52 us  [swap_all(): lax.ppermute(x, 'inner', [(i, i ^ mask) for i in range(n)])]
  transfers between devices with their start and end apart: 35 -> 34, of which waited for: 21 -> 19; matrix products, arithmetic and copies ran while one was open for 0% -> 0% of each run, Pallas kernels for 28% -> 30%
where the time goes in v4:
time: 91.8 us; the launch traced here: 91.6 us
  starting transfers between devices  35 us (38%)
  Pallas kernels  30.8 us (34%)
  waiting for transfers between devices  24.5 us (27%)
  between operations  1.13 us (1%)
    pallas_call x32, Pallas kernels, call(): pl.pallas_call(body, in_specs=specs, out_specs=[WHOLE if near else HBM fo...  30.8 us
    ppermute x28, starting transfers between devices, swap(): return lax.ppermute(x, axis, [(i, i ^ 1 << bit) for i in range(n)])  26.1 us
    ppermute x28, waiting for transfers between devices, swap(): return lax.ppermute(x, axis, [(i, i ^ 1 << bit) for i in range(n)])  19 us
    ppermute x6, starting transfers between devices, swap_all(): lax.ppermute(x, 'inner', [(i, i ^ mask) for i in range(n)])  8.9 us
    ppermute x6, waiting for transfers between devices, swap_all(): lax.ppermute(x, 'inner', [(i, i ^ mask) for i in range(n)])  5.52 us
  transfers between devices with their start and end apart: 34, of which 19 were waited for; matrix products, arithmetic and copies ran while one was open for 0% of the time, Pallas kernels for 30%

profile of v4, /device:TPU:0, one launch (start us, length us, event | category | flops | bytes accessed | tf_op | source)
XLA Modules:
  0.0 91.6 jit_solution(6652739311067362361)
XLA Ops:
  0.6 2.2 %shard_map.131 = bf16[4,128,128]{2,1,0:T(8,128)(2,1)S(1)} custom-call(bf16[1024,1024]{1,0:T(8,128)(2,1)} %a_hbm.1, bf16[1024,1024]{1,0:T(8,128)(2,1)} %b_hbm.3), custom_call_target="tpu_custom_call" | custom-call | flops 134217728 | bytes 2097152 | tf_op jit(solution)/shard_map/pallas_call | solution.py:31
  2.8 3.0 %collective-permute-start.2 = (bf16[4,128,128]{2,1,0:T(8,128)(2,1)S(1)}, bf16[4,128,128]{2,1,0:T(8,128)(2,1)S(1)}, u32[]{:S(2)}, u32[]{:S(2)}) collective-permute-start(bf16[4,128,128]{2,1,0:T(8,128)(2,1)S(1)} %shard_map.131), channel_id=1, source_target_pairs={{0,1},{1,0},{2,3},{3,2},{4,5},{5,4},{6,7},{7,6},{8,9},{9,8},{10,11... | collective-permute-start | bytes 393224 | tf_op jit(solution)/shard_map/ppermute | solution.py:506
  5.8 3.3 %shard_map.127 = (f32[4,128,128]{2,1,0:T(8,128)S(1)}, bf16[1024,1024]{1,0:T(8,128)(2,1)S(1)}, bf16[1024,1024]{1,0:T(8,128)(2,1)S(1)}, bf16[1024,1024]{1,0:T(8,128)(2,1)S(1)}) custom-call(bf16[1024,1024]{1,0:T(8,128)(2,1)} %a_hbm.1, bf16[1024,1024]{1,0:T(8,128)(2,1)} %b_hbm.3, bf16[1024,1024]{1,0:T(8,128)(2,1)} %refs_2_.1), custom_call_target="tpu_custom_call" | custom-call | flops 134217728 | bytes 12582912 | tf_op jit(solution)/shard_map/pallas_call | solution.py:31
  9.4 1.9 %collective-permute-start.3 = (bf16[4,128,128]{2,1,0:T(8,128)(2,1)S(1)}, bf16[4,128,128]{2,1,0:T(8,128)(2,1)S(1)}, u32[]{:S(2)}, u32[]{:S(2)}) collective-permute-start(bf16[4,128,128]{2,1,0:T(8,128)(2,1)S(1)} %get-tuple-element.98), channel_id=1, source_target_pairs={{0,2},{1,3},{2,0},{3,1},{4,6},{5,7},{6,4},{7,5},{8,10},{9,11},{10,... | collective-permute-start | bytes 393224 | tf_op jit(solution)/shard_map/ppermute | solution.py:506
  11.2 2.9 %shard_map.128 = (bf16[4,128,128]{2,1,0:T(8,128)(2,1)S(1)}, f32[4,128,128]{2,1,0:T(8,128)S(1)}, bf16[1024,1024]{1,0:T(8,128)(2,1)S(1)}) custom-call(bf16[1024,1024]{1,0:T(8,128)(2,1)S(1)} %get-tuple-element.89.a_ref.v_ref, bf16[1024,1024]{1,0:T(8,128)(2,1)} %b_hbm.2), custom_call_target="tpu_custom_call" | custom-call | flops 268435456 | bytes 2097152 | tf_op jit(solution)/shard_map/pallas_call | solution.py:31
  14.2 1.6 %collective-permute-start = (bf16[4,128,128]{2,1,0:T(8,128)(2,1)S(1)}, bf16[4,128,128]{2,1,0:T(8,128)(2,1)S(1)}, u32[]{:S(2)}, u32[]{:S(2)}) collective-permute-start(bf16[4,128,128]{2,1,0:T(8,128)(2,1)S(1)} %get-tuple-element.93), channel_id=1, source_target_pairs={{0,1},{1,0},{2,3},{3,2},{4,5},{5,4},{6,7},{7,6},{8,9},{9,8},{10,11... | collective-permute-start | bytes 393224 | tf_op jit(solution)/shard_map/ppermute | solution.py:506
  15.8 2.7 %collective-permute-start.4 = (bf16[4,128,128]{2,1,0:T(8,128)(2,1)S(1)}, bf16[4,128,128]{2,1,0:T(8,128)(2,1)S(1)}, u32[]{:S(2)}, u32[]{:S(2)}) collective-permute-start(bf16[4,128,128]{2,1,0:T(8,128)(2,1)S(1)} %get-tuple-element.102), channel_id=1, source_target_pairs={{0,4},{1,5},{2,6},{3,7},{4,0},{5,1},{6,2},{7,3},{8,12},{9,13},{10,... | collective-permute-start | bytes 393224 | tf_op jit(solution)/shard_map/ppermute | solution.py:506
  18.5 2.0 %shard_map.129.inside_ref = f32[1024,512]{1,0:T(8,128)S(1)} custom-call(bf16[1024,1024]{1,0:T(8,128)(2,1)S(1)} %get-tuple-element.159.g_ref, bf16[1024,1024]{1,0:T(8,128)(2,1)S(1)} %get-tuple-element.92.q_ref, bf16[1024,1024]{1,0:T(8,128)(2,1)S(1)} %get-tuple-element.89.a_ref.v_ref), custom_call_target="tpu_custom_call" | custom-call | flops 805306368 | bytes 5242880 | tf_op jit(solution)/shard_map/pallas_call | solution.py:31
  20.5 2.8 %collective-permute-done.4.got_ref = bf16[4,128,128]{2,1,0:T(8,128)(2,1)S(1)} collective-permute-done((bf16[4,128,128]{2,1,0:T(8,128)(2,1)S(1)}, bf16[4,128,128]{2,1,0:T(8,128)(2,1)S(1)}, u32[]{:S(2)}, u32[]{:S(2)}) %collective-permute-start.4) | collective-permute-done | bytes 131104 | tf_op jit(solution)/shard_map/ppermute | solution.py:506
  24.8 1.6 %collective-permute-start.6 = (bf16[4,128,128]{2,1,0:T(8,128)(2,1)S(1)}, bf16[4,128,128]{2,1,0:T(8,128)(2,1)S(1)}, u32[]{:S(2)}, u32[]{:S(2)}) collective-permute-start(bf16[4,128,128]{2,1,0:T(8,128)(2,1)S(1)} %get-tuple-element.109), channel_id=1, source_target_pairs={{0,16},{8,24},{16,0},{24,8},{1,17},{9,25},{17,1},{25,9},{2,18},{10... | collective-permute-start | bytes 393224 | tf_op jit(solution)/shard_map/ppermute | solution.py:506
  26.5 2.0 %shard_map.136.inside_ref = f32[1024,512]{1,0:T(8,128)S(1)} custom-call(bf16[1024,1024]{1,0:T(8,128)(2,1)S(1)} %get-tuple-element.159.g_ref, bf16[1024,1024]{1,0:T(8,128)(2,1)S(1)} %get-tuple-element.92.q_ref, bf16[1024,1024]{1,0:T(8,128)(2,1)S(1)} %get-tuple-element.89.a_ref.v_ref), custom_call_target="tpu_custom_call" | custom-call | flops 805306368 | bytes 5242880 | tf_op jit(solution)/shard_map/pallas_call | solution.py:31
  28.5 1.9 %collective-permute-done.6.got_ref = bf16[4,128,128]{2,1,0:T(8,128)(2,1)S(1)} collective-permute-done((bf16[4,128,128]{2,1,0:T(8,128)(2,1)S(1)}, bf16[4,128,128]{2,1,0:T(8,128)(2,1)S(1)}, u32[]{:S(2)}, u32[]{:S(2)}) %collective-permute-start.6) | collective-permute-done | bytes 131104 | tf_op jit(solution)/shard_map/ppermute | solution.py:506
  31.4 2.0 %shard_map.138.turned_ref = bf16[1024,1024]{1,0:T(8,128)(2,1)S(1)} custom-call(bf16[1024,1024]{1,0:T(8,128)(2,1)} %in_hbm), custom_call_target="tpu_custom_call" | custom-call | bytes 4194304 | tf_op jit(solution)/shard_map/pallas_call | solution.py:31
  33.4 1.8 %shard_map.139 = (bf16[1024,256]{1,0:T(8,128)(2,1)S(1)}, bf16[1024,256]{1,0:T(8,128)(2,1)S(1)}, bf16[2,8,64,256]{3,2,1,0:T(8,128)(2,1)S(1)}, bf16[2,8,64,256]{3,2,1,0:T(8,128)(2,1)S(1)}) custom-call(f32[1024,512]{1,0:T(8,128)S(1)} %shard_map.129.inside_ref, bf16[1024,1024]{1,0:T(8,128)(2,1)S(1)} %get-tuple-element.89.a_ref.v_ref, ...), custom_call_target="tpu_custom_call" | custom-call | flops 1207959552 | bytes 6291456 | tf_op jit(solution)/shard_map/pallas_call | solution.py:31
  42.9 4.6 %collective-permute-done.12 = bf16[2,4,64,256]{3,2,1,0:T(8,128)(2,1)S(1)} collective-permute-done((bf16[2,4,64,256]{3,2,1,0:T(8,128)(2,1)S(1)}, bf16[2,4,64,256]{3,2,1,0:T(8,128)(2,1)S(1)}, u32[]{:S(2)}, u32[]{:S(2)}) %collective-permute-start.12) | collective-permute-done | bytes 262176 | tf_op jit(solution)/shard_map/ppermute | solution.py:506
  47.5 1.6 %collective-permute-start.13 = (bf16[1,4,64,256]{3,2,1,0:T(8,128)(2,1)S(1)}, bf16[1,4,64,256]{3,2,1,0:T(8,128)(2,1)S(1)}, u32[]{:S(2)}, u32[]{:S(2)}) collective-permute-start(bf16[1,4,64,256]{3,2,1,0:T(8,128)(2,1)S(1)} %get-tuple-element.170), channel_id=1, source_target_pairs={{0,16},{8,24},{16,0},{24,8},{1,17},{9,25},{17,1},{25,9},{2,18},{10... | collective-permute-start | bytes 393224 | tf_op jit(solution)/shard_map/ppermute | solution.py:506
  50.4 3.2 %shard_map.144 = (f32[1024,512]{1,0:T(8,128)S(1)}, bf16[1024,1024]{1,0:T(8,128)(2,1)}) custom-call(bf16[1024,1024]{1,0:T(8,128)(2,1)S(1)} %get-tuple-element.159.g_ref, bf16[1024,1024]{1,0:T(8,128)(2,1)S(1)} %get-tuple-element.126.k_ref, bf16[1024,1024]{1,0:T(8,128)(2,1)S(1)} %get-tuple-element.89.a_ref.v_ref, ...), custom_call_target="tpu_custom_call" | custom-call | flops 805306368 | bytes 5242880 | tf_op jit(solution)/shard_map/pallas_call | solution.py:31
  55.4 2.5 %collective-permute-start.15 = (bf16[2,1,64,256]{3,2,1,0:T(8,128)(2,1)S(1)}, bf16[2,1,64,256]{3,2,1,0:T(8,128)(2,1)S(1)}, u32[]{:S(2)}, u32[]{:S(2)}) collective-permute-start(bf16[2,1,64,256]{3,2,1,0:T(8,128)(2,1)S(1)} %get-tuple-element.133), channel_id=1, source_target_pairs={{0,2},{1,3},{2,0},{3,1},{4,6},{5,7},{6,4},{7,5},{8,10},{9,11},{10,... | collective-permute-start | bytes 196616 | tf_op jit(solution)/shard_map/ppermute | solution.py:599
  58.7 2.1 %shard_map.146.in_oth = f32[1024,512]{1,0:T(8,128)S(1)} custom-call(bf16[1024,1024]{1,0:T(8,128)(2,1)S(1)} %get-tuple-element.159.g_ref, bf16[1024,1024]{1,0:T(8,128)(2,1)S(1)} %get-tuple-element.126.k_ref, bf16[1024,1024]{1,0:T(8,128)(2,1)S(1)} %get-tuple-element.89.a_ref.v_ref), custom_call_target="tpu_custom_call" | custom-call | flops 805306368 | bytes 5242880 | tf_op jit(solution)/shard_map/pallas_call | solution.py:31
  61.7 2.3 %collective-permute-done.16.refs_3_ = bf16[2,1,64,256]{3,2,1,0:T(8,128)(2,1)S(1)} collective-permute-done((bf16[2,1,64,256]{3,2,1,0:T(8,128)(2,1)S(1)}, bf16[2,1,64,256]{3,2,1,0:T(8,128)(2,1)S(1)}, u32[]{:S(2)}, u32[]{:S(2)}) %collective-permute-start.16) | collective-permute-done | bytes 65568 | tf_op jit(solution)/shard_map/ppermute | solution.py:599
  65.7 3.0 %collective-permute-start.19 = (bf16[2,1,64,256]{3,2,1,0:T(8,128)(2,1)S(1)}, bf16[2,1,64,256]{3,2,1,0:T(8,128)(2,1)S(1)}, u32[]{:S(2)}, u32[]{:S(2)}) collective-permute-start(bf16[2,1,64,256]{3,2,1,0:T(8,128)(2,1)S(1)} %get-tuple-element.137.refs_0_), channel_id=1, source_target_pairs={{0,6},{1,7},{2,4},{3,5},{4,2},{5,3},{6,0},{7,1},{8,14},{9,15},{10,... | collective-permute-start | bytes 196616 | tf_op jit(solution)/shard_map/ppermute | solution.py:599
  68.6 1.9 %collective-permute-done.17.refs_1_ = bf16[2,1,64,256]{3,2,1,0:T(8,128)(2,1)S(1)} collective-permute-done((bf16[2,1,64,256]{3,2,1,0:T(8,128)(2,1)S(1)}, bf16[2,1,64,256]{3,2,1,0:T(8,128)(2,1)S(1)}, u32[]{:S(2)}, u32[]{:S(2)}) %collective-permute-start.17) | collective-permute-done | bytes 65568 | tf_op jit(solution)/shard_map/ppermute | solution.py:599
  75.1 2.8 %collective-permute-done.20.refs_1_ = bf16[1,4,64,256]{3,2,1,0:T(8,128)(2,1)S(1)} collective-permute-done((bf16[1,4,64,256]{3,2,1,0:T(8,128)(2,1)S(1)}, bf16[1,4,64,256]{3,2,1,0:T(8,128)(2,1)S(1)}, u32[]{:S(2)}, u32[]{:S(2)}) %collective-permute-start.20) | collective-permute-done | bytes 131104 | tf_op jit(solution)/shard_map/ppermute | solution.py:506
  83.5 1.8 %shard_map.154 = bf16[1024,1024]{1,0:T(8,128)(2,1)} custom-call(bf16[1024,1024]{1,0:T(8,128)(2,1)S(1)} %get-tuple-element.159.g_ref, f32[1024,512]{1,0:T(8,128)S(1)} %get-tuple-element.131.in_own, f32[1024,512]{1,0:T(8,128)S(1)} %shard_map.146.in_oth, bf16[4,128,128]{2,1,0:T(8,128)(2,1)S(1)} %get-tuple-element.160.own_ref, ...), custom_call_target="tpu_custom_call" | custom-call | flops 268435456 | bytes 8388608 | tf_op jit(solution)/shard_map/pallas_call | solution.py:31
  (84 shorter events, 33.3 us)
Async XLA Ops:
  2.8 6.5 %collective-permute-start.2 = (bf16[4,128,128]{2,1,0:T(8,128)(2,1)S(1)}, bf16[4,128,128]{2,1,0:T(8,128)(2,1)S(1)}, u32[]{:S(2)}, u32[]{:S(2)}) collective-permute-start(bf16[4,128,128]{2,1,0:T(8,128)(2,1)S(1)} %shard_map.131), channel_id=1, source_target_pairs={{0,1},{1,0},{2,3},{3,2},{4,5},{5,4},{6,7},{7,6},{8,9},{9,8},{10,11... | collective-permute-start | bytes 393224 | tf_op jit(solution)/shard_map/ppermute | solution.py:506
  9.4 6.4 %collective-permute-start.3 = (bf16[4,128,128]{2,1,0:T(8,128)(2,1)S(1)}, bf16[4,128,128]{2,1,0:T(8,128)(2,1)S(1)}, u32[]{:S(2)}, u32[]{:S(2)}) collective-permute-start(bf16[4,128,128]{2,1,0:T(8,128)(2,1)S(1)} %get-tuple-element.98), channel_id=1, source_target_pairs={{0,2},{1,3},{2,0},{3,1},{4,6},{5,7},{6,4},{7,5},{8,10},{9,11},{10,... | collective-permute-start | bytes 393224 | tf_op jit(solution)/shard_map/ppermute | solution.py:506
  14.2 6.3 %collective-permute-start = (bf16[4,128,128]{2,1,0:T(8,128)(2,1)S(1)}, bf16[4,128,128]{2,1,0:T(8,128)(2,1)S(1)}, u32[]{:S(2)}, u32[]{:S(2)}) collective-permute-start(bf16[4,128,128]{2,1,0:T(8,128)(2,1)S(1)} %get-tuple-element.93), channel_id=1, source_target_pairs={{0,1},{1,0},{2,3},{3,2},{4,5},{5,4},{6,7},{7,6},{8,9},{9,8},{10,11... | collective-permute-start | bytes 393224 | tf_op jit(solution)/shard_map/ppermute | solution.py:506
  15.8 7.5 %collective-permute-start.4 = (bf16[4,128,128]{2,1,0:T(8,128)(2,1)S(1)}, bf16[4,128,128]{2,1,0:T(8,128)(2,1)S(1)}, u32[]{:S(2)}, u32[]{:S(2)}) collective-permute-start(bf16[4,128,128]{2,1,0:T(8,128)(2,1)S(1)} %get-tuple-element.102), channel_id=1, source_target_pairs={{0,4},{1,5},{2,6},{3,7},{4,0},{5,1},{6,2},{7,3},{8,12},{9,13},{10,... | collective-permute-start | bytes 393224 | tf_op jit(solution)/shard_map/ppermute | solution.py:506
  24.8 5.6 %collective-permute-start.6 = (bf16[4,128,128]{2,1,0:T(8,128)(2,1)S(1)}, bf16[4,128,128]{2,1,0:T(8,128)(2,1)S(1)}, u32[]{:S(2)}, u32[]{:S(2)}) collective-permute-start(bf16[4,128,128]{2,1,0:T(8,128)(2,1)S(1)} %get-tuple-element.109), channel_id=1, source_target_pairs={{0,16},{8,24},{16,0},{24,8},{1,17},{9,25},{17,1},{25,9},{2,18},{10... | collective-permute-start | bytes 393224 | tf_op jit(solution)/shard_map/ppermute | solution.py:506
  26.4 7.0 %collective-permute-start.1 = (bf16[4,128,128]{2,1,0:T(8,128)(2,1)S(1)}, bf16[4,128,128]{2,1,0:T(8,128)(2,1)S(1)}, u32[]{:S(2)}, u32[]{:S(2)}) collective-permute-start(bf16[4,128,128]{2,1,0:T(8,128)(2,1)S(1)} %get-tuple-element.94), channel_id=1, source_target_pairs={{0,2},{1,3},{2,0},{3,1},{4,6},{5,7},{6,4},{7,5},{8,10},{9,11},{10,... | collective-permute-start | bytes 393224 | tf_op jit(solution)/shard_map/ppermute | solution.py:506
  39.0 8.4 %collective-permute-start.12 = (bf16[2,4,64,256]{3,2,1,0:T(8,128)(2,1)S(1)}, bf16[2,4,64,256]{3,2,1,0:T(8,128)(2,1)S(1)}, u32[]{:S(2)}, u32[]{:S(2)}) collective-permute-start(bf16[2,4,64,256]{3,2,1,0:T(8,128)(2,1)S(1)} %get-tuple-element.122), channel_id=1, source_target_pairs={{0,1},{1,0},{2,3},{3,2},{4,5},{5,4},{6,7},{7,6},{8,9},{9,8},{10,11... | collective-permute-start | bytes 786440 | tf_op jit(solution)/shard_map/ppermute | solution.py:506
  40.1 9.0 %collective-permute-start.10 = (bf16[1,8,64,256]{3,2,1,0:T(8,128)(2,1)S(1)}, bf16[1,8,64,256]{3,2,1,0:T(8,128)(2,1)S(1)}, u32[]{:S(2)}, u32[]{:S(2)}) collective-permute-start(bf16[1,8,64,256]{3,2,1,0:T(8,128)(2,1)S(1)} %get-tuple-element.120), channel_id=1, source_target_pairs={{0,16},{8,24},{16,0},{24,8},{1,17},{9,25},{17,1},{25,9},{2,18},{10... | collective-permute-start | bytes 786440 | tf_op jit(solution)/shard_map/ppermute | solution.py:506
  41.7 12.0 %collective-permute-start.22 = (bf16[4,128,128]{2,1,0:T(8,128)(2,1)S(1)}, bf16[4,128,128]{2,1,0:T(8,128)(2,1)S(1)}, u32[]{:S(2)}, u32[]{:S(2)}) collective-permute-start(bf16[4,128,128]{2,1,0:T(8,128)(2,1)S(1)} %get-tuple-element.146), channel_id=1, source_target_pairs={{0,4},{1,5},{2,6},{3,7},{4,0},{5,1},{6,2},{7,3},{8,12},{9,13},{10,... | collective-permute-start | bytes 393224 | tf_op jit(solution)/shard_map/ppermute | solution.py:506
  47.5 6.3 %collective-permute-start.13 = (bf16[1,4,64,256]{3,2,1,0:T(8,128)(2,1)S(1)}, bf16[1,4,64,256]{3,2,1,0:T(8,128)(2,1)S(1)}, u32[]{:S(2)}, u32[]{:S(2)}) collective-permute-start(bf16[1,4,64,256]{3,2,1,0:T(8,128)(2,1)S(1)} %get-tuple-element.170), channel_id=1, source_target_pairs={{0,16},{8,24},{16,0},{24,8},{1,17},{9,25},{17,1},{25,9},{2,18},{10... | collective-permute-start | bytes 393224 | tf_op jit(solution)/shard_map/ppermute | solution.py:506
  53.7 7.1 %collective-permute-start.23 = (bf16[4,128,128]{2,1,0:T(8,128)(2,1)S(1)}, bf16[4,128,128]{2,1,0:T(8,128)(2,1)S(1)}, u32[]{:S(2)}, u32[]{:S(2)}) collective-permute-start(bf16[4,128,128]{2,1,0:T(8,128)(2,1)S(1)} %get-tuple-element.150), channel_id=1, source_target_pairs={{0,8},{8,0},{16,24},{24,16},{1,9},{9,1},{17,25},{25,17},{2,10},{10... | collective-permute-start | bytes 393224 | tf_op jit(solution)/shard_map/ppermute | solution.py:506
  54.2 7.5 %collective-permute-start.14 = (bf16[2,1,64,256]{3,2,1,0:T(8,128)(2,1)S(1)}, bf16[2,1,64,256]{3,2,1,0:T(8,128)(2,1)S(1)}, u32[]{:S(2)}, u32[]{:S(2)}) collective-permute-start(bf16[2,1,64,256]{3,2,1,0:T(8,128)(2,1)S(1)} %get-tuple-element.132), channel_id=1, source_target_pairs={{0,4},{1,5},{2,6},{3,7},{4,0},{5,1},{6,2},{7,3},{8,12},{9,13},{10,... | collective-permute-start | bytes 196616 | tf_op jit(solution)/shard_map/ppermute | solution.py:599
  55.4 6.3 %collective-permute-start.15 = (bf16[2,1,64,256]{3,2,1,0:T(8,128)(2,1)S(1)}, bf16[2,1,64,256]{3,2,1,0:T(8,128)(2,1)S(1)}, u32[]{:S(2)}, u32[]{:S(2)}) collective-permute-start(bf16[2,1,64,256]{3,2,1,0:T(8,128)(2,1)S(1)} %get-tuple-element.133), channel_id=1, source_target_pairs={{0,2},{1,3},{2,0},{3,1},{4,6},{5,7},{6,4},{7,5},{8,10},{9,11},{10,... | collective-permute-start | bytes 196616 | tf_op jit(solution)/shard_map/ppermute | solution.py:599
  58.0 6.1 %collective-permute-start.16 = (bf16[2,1,64,256]{3,2,1,0:T(8,128)(2,1)S(1)}, bf16[2,1,64,256]{3,2,1,0:T(8,128)(2,1)S(1)}, u32[]{:S(2)}, u32[]{:S(2)}) collective-permute-start(bf16[2,1,64,256]{3,2,1,0:T(8,128)(2,1)S(1)} %get-tuple-element.134), channel_id=1, source_target_pairs={{0,6},{1,7},{2,4},{3,5},{4,2},{5,3},{6,0},{7,1},{8,14},{9,15},{10,... | collective-permute-start | bytes 196616 | tf_op jit(solution)/shard_map/ppermute | solution.py:599
  60.8 12.1 %collective-permute-start.24 = (bf16[4,128,128]{2,1,0:T(8,128)(2,1)S(1)}, bf16[4,128,128]{2,1,0:T(8,128)(2,1)S(1)}, u32[]{:S(2)}, u32[]{:S(2)}) collective-permute-start(bf16[4,128,128]{2,1,0:T(8,128)(2,1)S(1)} %get-tuple-element.154), channel_id=1, source_target_pairs={{0,16},{8,24},{16,0},{24,8},{1,17},{9,25},{17,1},{25,9},{2,18},{10... | collective-permute-start | bytes 393224 | tf_op jit(solution)/shard_map/ppermute | solution.py:506
  64.2 6.3 %collective-permute-start.17 = (bf16[2,1,64,256]{3,2,1,0:T(8,128)(2,1)S(1)}, bf16[2,1,64,256]{3,2,1,0:T(8,128)(2,1)S(1)}, u32[]{:S(2)}, u32[]{:S(2)}) collective-permute-start(bf16[2,1,64,256]{3,2,1,0:T(8,128)(2,1)S(1)} %get-tuple-element.137.refs_0_), channel_id=1, source_target_pairs={{0,4},{1,5},{2,6},{3,7},{4,0},{5,1},{6,2},{7,3},{8,12},{9,13},{10,... | collective-permute-start | bytes 196616 | tf_op jit(solution)/shard_map/ppermute | solution.py:599
  64.9 5.7 %collective-permute-start.18 = (bf16[2,1,64,256]{3,2,1,0:T(8,128)(2,1)S(1)}, bf16[2,1,64,256]{3,2,1,0:T(8,128)(2,1)S(1)}, u32[]{:S(2)}, u32[]{:S(2)}) collective-permute-start(bf16[2,1,64,256]{3,2,1,0:T(8,128)(2,1)S(1)} %get-tuple-element.137.refs_0_), channel_id=1, source_target_pairs={{0,2},{1,3},{2,0},{3,1},{4,6},{5,7},{6,4},{7,5},{8,10},{9,11},{10,... | collective-permute-start | bytes 196616 | tf_op jit(solution)/shard_map/ppermute | solution.py:599
  65.7 6.2 %collective-permute-start.19 = (bf16[2,1,64,256]{3,2,1,0:T(8,128)(2,1)S(1)}, bf16[2,1,64,256]{3,2,1,0:T(8,128)(2,1)S(1)}, u32[]{:S(2)}, u32[]{:S(2)}) collective-permute-start(bf16[2,1,64,256]{3,2,1,0:T(8,128)(2,1)S(1)} %get-tuple-element.137.refs_0_), channel_id=1, source_target_pairs={{0,6},{1,7},{2,4},{3,5},{4,2},{5,3},{6,0},{7,1},{8,14},{9,15},{10,... | collective-permute-start | bytes 196616 | tf_op jit(solution)/shard_map/ppermute | solution.py:599
  71.9 6.1 %collective-permute-start.21 = (bf16[1,6,64,256]{3,2,1,0:T(8,128)(2,1)S(1)}, bf16[1,6,64,256]{3,2,1,0:T(8,128)(2,1)S(1)}, u32[]{:S(2)}, u32[]{:S(2)}) collective-permute-start(bf16[1,6,64,256]{3,2,1,0:T(8,128)(2,1)S(1)} %get-tuple-element.140.a_ref), channel_id=1, source_target_pairs={{0,16},{8,24},{16,0},{24,8},{1,17},{9,25},{17,1},{25,9},{2,18},{10... | collective-permute-start | bytes 589832 | tf_op jit(solution)/shard_map/ppermute | solution.py:506
  73.9 5.4 %collective-permute-start.25 = (bf16[4,128,128]{2,1,0:T(8,128)(2,1)S(1)}, bf16[4,128,128]{2,1,0:T(8,128)(2,1)S(1)}, u32[]{:S(2)}, u32[]{:S(2)}) collective-permute-start(bf16[4,128,128]{2,1,0:T(8,128)(2,1)S(1)} %get-tuple-element.156), channel_id=1, source_target_pairs={{0,1},{1,0},{2,3},{3,2},{4,5},{5,4},{6,7},{7,6},{8,9},{9,8},{10,11... | collective-permute-start | bytes 393224 | tf_op jit(solution)/shard_map/ppermute | solution.py:506
  79.3 7.3 %collective-permute-start.29 = (bf16[1,8,64,256]{3,2,1,0:T(8,128)(2,1)S(1)}, bf16[1,8,64,256]{3,2,1,0:T(8,128)(2,1)S(1)}, u32[]{:S(2)}, u32[]{:S(2)}) collective-permute-start(bf16[1,8,64,256]{3,2,1,0:T(8,128)(2,1)S(1)} %shard_map.148.refs_0_), channel_id=1, source_target_pairs={{0,8},{8,0},{16,24},{24,16},{1,9},{9,1},{17,25},{25,17},{2,10},{10... | collective-permute-start | bytes 786440 | tf_op jit(solution)/shard_map/ppermute | solution.py:506
  79.3 7.3 %collective-permute-start.30 = (bf16[2,4,64,256]{3,2,1,0:T(8,128)(2,1)S(1)}, bf16[2,4,64,256]{3,2,1,0:T(8,128)(2,1)S(1)}, u32[]{:S(2)}, u32[]{:S(2)}) collective-permute-start(bf16[2,4,64,256]{3,2,1,0:T(8,128)(2,1)S(1)} %get-tuple-element.158.refs_1_), channel_id=1, source_target_pairs={{0,8},{8,0},{16,24},{24,16},{1,9},{9,1},{17,25},{25,17},{2,10},{10... | collective-permute-start | bytes 786440 | tf_op jit(solution)/shard_map/ppermute | solution.py:506
  79.9 8.2 %collective-permute-start.32 = (bf16[2,4,64,256]{3,2,1,0:T(8,128)(2,1)S(1)}, bf16[2,4,64,256]{3,2,1,0:T(8,128)(2,1)S(1)}, u32[]{:S(2)}, u32[]{:S(2)}) collective-permute-start(bf16[2,4,64,256]{3,2,1,0:T(8,128)(2,1)S(1)} %get-tuple-element.158.refs_1_), channel_id=1, source_target_pairs={{0,1},{1,0},{2,3},{3,2},{4,5},{5,4},{6,7},{7,6},{8,9},{9,8},{10,11... | collective-permute-start | bytes 786440 | tf_op jit(solution)/shard_map/ppermute | solution.py:506
  80.7 7.9 %collective-permute-start.28 = (bf16[1,8,64,256]{3,2,1,0:T(8,128)(2,1)S(1)}, bf16[1,8,64,256]{3,2,1,0:T(8,128)(2,1)S(1)}, u32[]{:S(2)}, u32[]{:S(2)}) collective-permute-start(bf16[1,8,64,256]{3,2,1,0:T(8,128)(2,1)S(1)} %shard_map.148.refs_0_), channel_id=1, source_target_pairs={{0,16},{8,24},{16,0},{24,8},{1,17},{9,25},{17,1},{25,9},{2,18},{10... | collective-permute-start | bytes 786440 | tf_op jit(solution)/shard_map/ppermute | solution.py:506
  (13 other events, 46.0 us)

commit v5 on v4

--- a/solution.py
+++ b/solution.py
@@ -285,20 +285,6 @@
         copy.wait()
 
 
-def query_side(g, in_own, in_oth, own, oth, at, scale):
-    rows, width = g.shape
-    n = width // PAIR
-    return call(
-        functools.partial(query_body, scale, at),
-        [g, in_own, in_oth, own, oth],
-        [WHOLE] * 5,
-        [((rows, width), BF16, False)],
-        rows * width * HD,
-        8 * rows * width,
-        [pltpu.VMEM((n, rows, PAIR), BF16), dma(n)],
-    )[0]
-
-
 def turned_body(here_at, in_hbm, out_ref, buf, sem):
     size = out_ref.shape[0] // here_at.n_inner
     cols = max(size, HD)
@@ -454,10 +440,7 @@
     )
 
 
-def assemble_body(kinds, at, *refs):
-    n = len(kinds)
-    pieces, bufs = refs[:n], refs[-n - 1 : -1]
-    out_hbm, sem = refs[-n - 2], refs[-1]
+def assemble_start(kinds, at, pieces, out_hbm, bufs, sem):
     copies = []
     for i, (which, groups, start, count) in enumerate(kinds):
         size = pieces[i].shape[-1]
@@ -476,18 +459,52 @@
             copy = pltpu.make_async_copy(bufs[i].at[s], goal, sem.at[2 * i + s])
             copy.start()
             copies.append(copy)
+    return copies
+
+
+def assemble_body(kinds, at, *refs):
+    n = len(kinds)
+    for copy in assemble_start(kinds, at, refs[:n], refs[-n - 2], refs[-n - 1 : -1], refs[-1]):
+        copy.wait()
+
+
+def assemble_scratch(pieces, at):
+    part, cols = pieces[0][0].shape[2:]
+    bufs = [
+        pltpu.VMEM((len(groups), at.n_inner // 2) + (() if which else (2,)) + (part, cols), BF16)
+        for _, (which, groups, _, _) in pieces
+    ]
+    return bufs + [dma(2 * len(pieces))]
+
+
+def finish_body(scale, at, kinds, g_ref, in_own, in_oth, own_ref, oth_ref, *refs):
+    n = len(kinds)
+    pieces, (out_hbm, weights_hbm, buf, sem) = refs[:n], refs[n : n + 4]
+    copies = assemble_start(kinds, at, pieces, weights_hbm, refs[n + 4 : -1], refs[-1])
+    query_body(scale, at, g_ref, in_own, in_oth, own_ref, oth_ref, out_hbm, buf, sem)
     for copy in copies:
         copy.wait()
+
+
+def finish(g, in_own, in_oth, own, oth, at, scale, pieces):
+    rows, width = g.shape
+    n = width // PAIR
+    part = pieces[0][0].shape[2]
+    return call(
+        functools.partial(finish_body, scale, at, [kind for _, kind in pieces]),
+        [g, in_own, in_oth, own, oth, *[array for array, _ in pieces]],
+        [WHOLE] * (5 + len(pieces)),
+        [((rows, width), BF16, False), ((at.n_inner // 2, 2, 2, part, width), BF16, False)],
+        rows * width * HD,
+        8 * rows * width,
+        [pltpu.VMEM((n, rows, PAIR), BF16), dma(n)] + assemble_scratch(pieces, at),
+    )
 
 
 def assemble(pieces, at, before, width):
     n_inner = at.n_inner
     part, cols = pieces[0][0].shape[2:]
     kinds = [kind for _, kind in pieces]
-    bufs = [
-        pltpu.VMEM((len(groups), n_inner // 2) + (() if which else (2,)) + (part, cols), BF16)
-        for which, groups, _, _ in kinds
-    ]
     more = [] if before is None else [before]
     return call(
         functools.partial(assemble_body, kinds, at),
@@ -496,7 +513,7 @@
         [((n_inner // 2, 2, 2, part, width), BF16, False)],
         0,
         4 * sum(array.size for array, _ in pieces),
-        bufs + [dma(2 * len(pieces))],
+        assemble_scratch(pieces, at),
         {len(pieces): 0} if more else None,
     )[0]
 
@@ -749,19 +766,28 @@
     p_last, q_last = swap(p, "outer", 1), swap(q, "inner", 0)
     p_core, q_core = swap(p, "outer", 0), swap(q, "outer", 0)
     grads = [grad, swap(grad, "outer", 0), grad_x, swap(grad_x, "outer", 0)]
-    query_grad = query_side(tie(g, p, q), query_own, query_oth, kv_own, kv_oth, at, att_scale)
+    n = n_inner // 2
+    query_grad, weights = finish(
+        tie(g, p, q), query_own, query_oth, kv_own, kv_oth, at, att_scale,
+        [(p, (0, (0,), 0, 2 * n)), (q, (1, (0, 2), 0, n))],
+    )
     new_master, new_moment1, new_moment2 = adam_all(
-        [tie(grads[0], p, q)] + grads[1:], master, moment1, moment2, at, (0, 1, 2, 3)
-    )
-    n = n_inner // 2
+        [tie(grads[0], weights)] + grads[1:], master, moment1, moment2, at, (0, 1, 2, 3)
+    )
+    p_last, q_last, p_core, q_core, *_ = lax.optimization_barrier(
+        (p_last, q_last, p_core, q_core, weights, query_grad, new_master)
+    )
+    p_end, q_end = swap(p_last, "outer", 0), swap(q_last, "outer", 0)
     weights = assemble(
-        [(p, (0, (0,), 0, 2 * n)), (q, (1, (0, 2), 0, n)), (p_core, (0, (1,), 0, 2 * n)), (q_core, (1, (1, 3), 0, n))],
-        at, None, width,
-    )
-    done = [weights, query_grad, new_master]
-    p_core, q_core = swap(tie(p_last, *done), "outer", 0), swap(tie(q_last, *done), "outer", 0)
-    weights = assemble([(p_last, (0, (2,), 0, 2 * n)), (q_last, (1, (0, 2), n, n))], at, weights, width)
-    weights = assemble([(p_core, (0, (3,), 0, 2 * n)), (q_core, (1, (1, 3), n, n))], at, weights, width)
+        [
+            (p_last, (0, (2,), 0, 2 * n)),
+            (q_last, (1, (0, 2), n, n)),
+            (p_core, (0, (1,), 0, 2 * n)),
+            (q_core, (1, (1, 3), 0, n)),
+        ],
+        at, weights, width,
+    )
+    weights = assemble([(p_end, (0, (3,), 0, 2 * n)), (q_end, (1, (1, 3), n, n))], at, weights, width)
     return (query_grad, key_grad, new_master, new_moment1, new_moment2, weights.reshape(d, width))
 
 

time: 91.8 us -> 90.7 us (0.988)
    pallas_call x32 -> x31, Pallas kernels: 30.8 us -> 30 us  [call(): pl.pallas_call(body, in_specs=specs, out_specs=[WHOLE if near else HBM fo...]
  transfers between devices with their start and end apart: 34 -> 34, of which waited for: 19 -> 17; matrix products, arithmetic and copies ran while one was open for 0% -> 0% of each run, Pallas kernels for 30% -> 29%
where the time goes in v5:
time: 90.7 us; the launch traced here: 90.5 us
  starting transfers between devices  34.6 us (38%)
  Pallas kernels  30 us (33%)
  waiting for transfers between devices  24.6 us (27%)
  between operations  1.12 us (1%)
    pallas_call x31, Pallas kernels, call(): pl.pallas_call(body, in_specs=specs, out_specs=[WHOLE if near else HBM fo...  30 us
    ppermute x28, starting transfers between devices, swap(): return lax.ppermute(x, axis, [(i, i ^ 1 << bit) for i in range(n)])  25.7 us
    ppermute x28, waiting for transfers between devices, swap(): return lax.ppermute(x, axis, [(i, i ^ 1 << bit) for i in range(n)])  19.1 us
    ppermute x6, starting transfers between devices, swap_all(): lax.ppermute(x, 'inner', [(i, i ^ mask) for i in range(n)])  8.9 us
    ppermute x6, waiting for transfers between devices, swap_all(): lax.ppermute(x, 'inner', [(i, i ^ mask) for i in range(n)])  5.52 us
  transfers between devices with their start and end apart: 34, of which 17 were waited for; matrix products, arithmetic and copies ran while one was open for 0% of the time, Pallas kernels for 29%

profile of v5, /device:TPU:0, one launch (start us, length us, event | category | flops | bytes accessed | tf_op | source)
XLA Modules:
  0.0 90.5 jit_solution(10951289001259736328)
XLA Ops:
  0.6 2.2 %shard_map.131 = bf16[4,128,128]{2,1,0:T(8,128)(2,1)S(1)} custom-call(bf16[1024,1024]{1,0:T(8,128)(2,1)} %a_hbm.1, bf16[1024,1024]{1,0:T(8,128)(2,1)} %b_hbm.3), custom_call_target="tpu_custom_call" | custom-call | flops 134217728 | bytes 2097152 | tf_op jit(solution)/shard_map/pallas_call | solution.py:31
  2.8 3.0 %collective-permute-start.2 = (bf16[4,128,128]{2,1,0:T(8,128)(2,1)S(1)}, bf16[4,128,128]{2,1,0:T(8,128)(2,1)S(1)}, u32[]{:S(2)}, u32[]{:S(2)}) collective-permute-start(bf16[4,128,128]{2,1,0:T(8,128)(2,1)S(1)} %shard_map.131), channel_id=1, source_target_pairs={{0,1},{1,0},{2,3},{3,2},{4,5},{5,4},{6,7},{7,6},{8,9},{9,8},{10,11... | collective-permute-start | bytes 393224 | tf_op jit(solution)/shard_map/ppermute | solution.py:523
  5.8 3.3 %shard_map.127 = (f32[4,128,128]{2,1,0:T(8,128)S(1)}, bf16[1024,1024]{1,0:T(8,128)(2,1)S(1)}, bf16[1024,1024]{1,0:T(8,128)(2,1)S(1)}, bf16[1024,1024]{1,0:T(8,128)(2,1)S(1)}) custom-call(bf16[1024,1024]{1,0:T(8,128)(2,1)} %a_hbm.1, bf16[1024,1024]{1,0:T(8,128)(2,1)} %b_hbm.3, bf16[1024,1024]{1,0:T(8,128)(2,1)} %refs_2_.1), custom_call_target="tpu_custom_call" | custom-call | flops 134217728 | bytes 12582912 | tf_op jit(solution)/shard_map/pallas_call | solution.py:31
  9.4 1.9 %collective-permute-start.3 = (bf16[4,128,128]{2,1,0:T(8,128)(2,1)S(1)}, bf16[4,128,128]{2,1,0:T(8,128)(2,1)S(1)}, u32[]{:S(2)}, u32[]{:S(2)}) collective-permute-start(bf16[4,128,128]{2,1,0:T(8,128)(2,1)S(1)} %get-tuple-element.102), channel_id=1, source_target_pairs={{0,2},{1,3},{2,0},{3,1},{4,6},{5,7},{6,4},{7,5},{8,10},{9,11},{10,... | collective-permute-start | bytes 393224 | tf_op jit(solution)/shard_map/ppermute | solution.py:523
  11.2 2.9 %shard_map.128 = (bf16[4,128,128]{2,1,0:T(8,128)(2,1)S(1)}, f32[4,128,128]{2,1,0:T(8,128)S(1)}, bf16[1024,1024]{1,0:T(8,128)(2,1)S(1)}) custom-call(bf16[1024,1024]{1,0:T(8,128)(2,1)S(1)} %get-tuple-element.93.a_ref.v_ref, bf16[1024,1024]{1,0:T(8,128)(2,1)} %b_hbm.2), custom_call_target="tpu_custom_call" | custom-call | flops 268435456 | bytes 2097152 | tf_op jit(solution)/shard_map/pallas_call | solution.py:31
  14.2 1.6 %collective-permute-start = (bf16[4,128,128]{2,1,0:T(8,128)(2,1)S(1)}, bf16[4,128,128]{2,1,0:T(8,128)(2,1)S(1)}, u32[]{:S(2)}, u32[]{:S(2)}) collective-permute-start(bf16[4,128,128]{2,1,0:T(8,128)(2,1)S(1)} %get-tuple-element.97), channel_id=1, source_target_pairs={{0,1},{1,0},{2,3},{3,2},{4,5},{5,4},{6,7},{7,6},{8,9},{9,8},{10,11... | collective-permute-start | bytes 393224 | tf_op jit(solution)/shard_map/ppermute | solution.py:523
  15.8 2.7 %collective-permute-start.4 = (bf16[4,128,128]{2,1,0:T(8,128)(2,1)S(1)}, bf16[4,128,128]{2,1,0:T(8,128)(2,1)S(1)}, u32[]{:S(2)}, u32[]{:S(2)}) collective-permute-start(bf16[4,128,128]{2,1,0:T(8,128)(2,1)S(1)} %get-tuple-element.106), channel_id=1, source_target_pairs={{0,4},{1,5},{2,6},{3,7},{4,0},{5,1},{6,2},{7,3},{8,12},{9,13},{10,... | collective-permute-start | bytes 393224 | tf_op jit(solution)/shard_map/ppermute | solution.py:523
  18.5 2.0 %shard_map.129.inside_ref = f32[1024,512]{1,0:T(8,128)S(1)} custom-call(bf16[1024,1024]{1,0:T(8,128)(2,1)S(1)} %get-tuple-element.163.g_ref, bf16[1024,1024]{1,0:T(8,128)(2,1)S(1)} %get-tuple-element.96.q_ref, bf16[1024,1024]{1,0:T(8,128)(2,1)S(1)} %get-tuple-element.93.a_ref.v_ref), custom_call_target="tpu_custom_call" | custom-call | flops 805306368 | bytes 5242880 | tf_op jit(solution)/shard_map/pallas_call | solution.py:31
  20.5 2.8 %collective-permute-done.4.got_ref = bf16[4,128,128]{2,1,0:T(8,128)(2,1)S(1)} collective-permute-done((bf16[4,128,128]{2,1,0:T(8,128)(2,1)S(1)}, bf16[4,128,128]{2,1,0:T(8,128)(2,1)S(1)}, u32[]{:S(2)}, u32[]{:S(2)}) %collective-permute-start.4) | collective-permute-done | bytes 131104 | tf_op jit(solution)/shard_map/ppermute | solution.py:523
  26.5 2.0 %shard_map.136.inside_ref = f32[1024,512]{1,0:T(8,128)S(1)} custom-call(bf16[1024,1024]{1,0:T(8,128)(2,1)S(1)} %get-tuple-element.163.g_ref, bf16[1024,1024]{1,0:T(8,128)(2,1)S(1)} %get-tuple-element.96.q_ref, bf16[1024,1024]{1,0:T(8,128)(2,1)S(1)} %get-tuple-element.93.a_ref.v_ref), custom_call_target="tpu_custom_call" | custom-call | flops 805306368 | bytes 5242880 | tf_op jit(solution)/shard_map/pallas_call | solution.py:31
  28.5 1.9 %collective-permute-done.6.got_ref = bf16[4,128,128]{2,1,0:T(8,128)(2,1)S(1)} collective-permute-done((bf16[4,128,128]{2,1,0:T(8,128)(2,1)S(1)}, bf16[4,128,128]{2,1,0:T(8,128)(2,1)S(1)}, u32[]{:S(2)}, u32[]{:S(2)}) %collective-permute-start.6) | collective-permute-done | bytes 131104 | tf_op jit(solution)/shard_map/ppermute | solution.py:523
  31.4 2.0 %shard_map.138.turned_ref = bf16[1024,1024]{1,0:T(8,128)(2,1)S(1)} custom-call(bf16[1024,1024]{1,0:T(8,128)(2,1)} %in_hbm), custom_call_target="tpu_custom_call" | custom-call | bytes 4194304 | tf_op jit(solution)/shard_map/pallas_call | solution.py:31
  33.4 1.8 %shard_map.139 = (bf16[1024,256]{1,0:T(8,128)(2,1)S(1)}, bf16[1024,256]{1,0:T(8,128)(2,1)S(1)}, bf16[2,8,64,256]{3,2,1,0:T(8,128)(2,1)S(1)}, bf16[2,8,64,256]{3,2,1,0:T(8,128)(2,1)S(1)}) custom-call(f32[1024,512]{1,0:T(8,128)S(1)} %shard_map.129.inside_ref, bf16[1024,1024]{1,0:T(8,128)(2,1)S(1)} %get-tuple-element.93.a_ref.v_ref, ...), custom_call_target="tpu_custom_call" | custom-call | flops 1207959552 | bytes 6291456 | tf_op jit(solution)/shard_map/pallas_call | solution.py:31
  42.9 4.6 %collective-permute-done.12 = bf16[2,4,64,256]{3,2,1,0:T(8,128)(2,1)S(1)} collective-permute-done((bf16[2,4,64,256]{3,2,1,0:T(8,128)(2,1)S(1)}, bf16[2,4,64,256]{3,2,1,0:T(8,128)(2,1)S(1)}, u32[]{:S(2)}, u32[]{:S(2)}) %collective-permute-start.12) | collective-permute-done | bytes 262176 | tf_op jit(solution)/shard_map/ppermute | solution.py:523
  47.5 1.6 %collective-permute-start.13 = (bf16[1,4,64,256]{3,2,1,0:T(8,128)(2,1)S(1)}, bf16[1,4,64,256]{3,2,1,0:T(8,128)(2,1)S(1)}, u32[]{:S(2)}, u32[]{:S(2)}) collective-permute-start(bf16[1,4,64,256]{3,2,1,0:T(8,128)(2,1)S(1)} %get-tuple-element.178), channel_id=1, source_target_pairs={{0,16},{8,24},{16,0},{24,8},{1,17},{9,25},{17,1},{25,9},{2,18},{10... | collective-permute-start | bytes 393224 | tf_op jit(solution)/shard_map/ppermute | solution.py:523
  50.4 3.2 %shard_map.144 = (f32[1024,512]{1,0:T(8,128)S(1)}, bf16[1024,1024]{1,0:T(8,128)(2,1)}) custom-call(bf16[1024,1024]{1,0:T(8,128)(2,1)S(1)} %get-tuple-element.163.g_ref, bf16[1024,1024]{1,0:T(8,128)(2,1)S(1)} %get-tuple-element.130.k_ref, bf16[1024,1024]{1,0:T(8,128)(2,1)S(1)} %get-tuple-element.93.a_ref.v_ref, ...), custom_call_target="tpu_custom_call" | custom-call | flops 805306368 | bytes 5242880 | tf_op jit(solution)/shard_map/pallas_call | solution.py:31
  55.4 2.5 %collective-permute-start.15 = (bf16[2,1,64,256]{3,2,1,0:T(8,128)(2,1)S(1)}, bf16[2,1,64,256]{3,2,1,0:T(8,128)(2,1)S(1)}, u32[]{:S(2)}, u32[]{:S(2)}) collective-permute-start(bf16[2,1,64,256]{3,2,1,0:T(8,128)(2,1)S(1)} %get-tuple-element.137), channel_id=1, source_target_pairs={{0,2},{1,3},{2,0},{3,1},{4,6},{5,7},{6,4},{7,5},{8,10},{9,11},{10,... | collective-permute-start | bytes 196616 | tf_op jit(solution)/shard_map/ppermute | solution.py:616
  58.7 2.1 %shard_map.146.in_oth = f32[1024,512]{1,0:T(8,128)S(1)} custom-call(bf16[1024,1024]{1,0:T(8,128)(2,1)S(1)} %get-tuple-element.163.g_ref, bf16[1024,1024]{1,0:T(8,128)(2,1)S(1)} %get-tuple-element.130.k_ref, bf16[1024,1024]{1,0:T(8,128)(2,1)S(1)} %get-tuple-element.93.a_ref.v_ref), custom_call_target="tpu_custom_call" | custom-call | flops 805306368 | bytes 5242880 | tf_op jit(solution)/shard_map/pallas_call | solution.py:31
  61.7 2.3 %collective-permute-done.16.refs_3_ = bf16[2,1,64,256]{3,2,1,0:T(8,128)(2,1)S(1)} collective-permute-done((bf16[2,1,64,256]{3,2,1,0:T(8,128)(2,1)S(1)}, bf16[2,1,64,256]{3,2,1,0:T(8,128)(2,1)S(1)}, u32[]{:S(2)}, u32[]{:S(2)}) %collective-permute-start.16) | collective-permute-done | bytes 65568 | tf_op jit(solution)/shard_map/ppermute | solution.py:616
  65.7 3.0 %collective-permute-start.19 = (bf16[2,1,64,256]{3,2,1,0:T(8,128)(2,1)S(1)}, bf16[2,1,64,256]{3,2,1,0:T(8,128)(2,1)S(1)}, u32[]{:S(2)}, u32[]{:S(2)}) collective-permute-start(bf16[2,1,64,256]{3,2,1,0:T(8,128)(2,1)S(1)} %get-tuple-element.141.refs_0_), channel_id=1, source_target_pairs={{0,6},{1,7},{2,4},{3,5},{4,2},{5,3},{6,0},{7,1},{8,14},{9,15},{10,... | collective-permute-start | bytes 196616 | tf_op jit(solution)/shard_map/ppermute | solution.py:616
  68.6 1.9 %collective-permute-done.17.refs_1_ = bf16[2,1,64,256]{3,2,1,0:T(8,128)(2,1)S(1)} collective-permute-done((bf16[2,1,64,256]{3,2,1,0:T(8,128)(2,1)S(1)}, bf16[2,1,64,256]{3,2,1,0:T(8,128)(2,1)S(1)}, u32[]{:S(2)}, u32[]{:S(2)}) %collective-permute-start.17) | collective-permute-done | bytes 65568 | tf_op jit(solution)/shard_map/ppermute | solution.py:616
  75.1 2.8 %collective-permute-done.20.refs_1_ = bf16[1,4,64,256]{3,2,1,0:T(8,128)(2,1)S(1)} collective-permute-done((bf16[1,4,64,256]{3,2,1,0:T(8,128)(2,1)S(1)}, bf16[1,4,64,256]{3,2,1,0:T(8,128)(2,1)S(1)}, u32[]{:S(2)}, u32[]{:S(2)}) %collective-permute-start.20) | collective-permute-done | bytes 131104 | tf_op jit(solution)/shard_map/ppermute | solution.py:523
  78.0 2.0 %collective-permute-done.25.oth_ref = bf16[4,128,128]{2,1,0:T(8,128)(2,1)S(1)} collective-permute-done((bf16[4,128,128]{2,1,0:T(8,128)(2,1)S(1)}, bf16[4,128,128]{2,1,0:T(8,128)(2,1)S(1)}, u32[]{:S(2)}, u32[]{:S(2)}) %collective-permute-start.25) | collective-permute-done | bytes 131104 | tf_op jit(solution)/shard_map/ppermute | solution.py:523
  83.9 1.9 %shard_map.154 = (bf16[1024,1024]{1,0:T(8,128)(2,1)}, bf16[4,2,2,64,1024]{4,3,2,1,0:T(8,128)(2,1)}) custom-call(bf16[1024,1024]{1,0:T(8,128)(2,1)S(1)} %get-tuple-element.163.g_ref, f32[1024,512]{1,0:T(8,128)S(1)} %get-tuple-element.135.in_own, f32[1024,512]{1,0:T(8,128)S(1)} %shard_map.146.in_oth, bf16[4,128,128]{2,1,0:T(8,128)(2,1)S(1)} %get-tuple-element.164.own_ref, ...), custom_call_target="tpu_custom_call" | custom-call | flops 268435456 | bytes 8388608 | tf_op jit(solution)/shard_map/pallas_call | solution.py:31
  (83 shorter events, 31.6 us)
Async XLA Ops:
  2.8 6.5 %collective-permute-start.2 = (bf16[4,128,128]{2,1,0:T(8,128)(2,1)S(1)}, bf16[4,128,128]{2,1,0:T(8,128)(2,1)S(1)}, u32[]{:S(2)}, u32[]{:S(2)}) collective-permute-start(bf16[4,128,128]{2,1,0:T(8,128)(2,1)S(1)} %shard_map.131), channel_id=1, source_target_pairs={{0,1},{1,0},{2,3},{3,2},{4,5},{5,4},{6,7},{7,6},{8,9},{9,8},{10,11... | collective-permute-start | bytes 393224 | tf_op jit(solution)/shard_map/ppermute | solution.py:523
  9.4 6.4 %collective-permute-start.3 = (bf16[4,128,128]{2,1,0:T(8,128)(2,1)S(1)}, bf16[4,128,128]{2,1,0:T(8,128)(2,1)S(1)}, u32[]{:S(2)}, u32[]{:S(2)}) collective-permute-start(bf16[4,128,128]{2,1,0:T(8,128)(2,1)S(1)} %get-tuple-element.102), channel_id=1, source_target_pairs={{0,2},{1,3},{2,0},{3,1},{4,6},{5,7},{6,4},{7,5},{8,10},{9,11},{10,... | collective-permute-start | bytes 393224 | tf_op jit(solution)/shard_map/ppermute | solution.py:523
  14.2 6.3 %collective-permute-start = (bf16[4,128,128]{2,1,0:T(8,128)(2,1)S(1)}, bf16[4,128,128]{2,1,0:T(8,128)(2,1)S(1)}, u32[]{:S(2)}, u32[]{:S(2)}) collective-permute-start(bf16[4,128,128]{2,1,0:T(8,128)(2,1)S(1)} %get-tuple-element.97), channel_id=1, source_target_pairs={{0,1},{1,0},{2,3},{3,2},{4,5},{5,4},{6,7},{7,6},{8,9},{9,8},{10,11... | collective-permute-start | bytes 393224 | tf_op jit(solution)/shard_map/ppermute | solution.py:523
  15.8 7.5 %collective-permute-start.4 = (bf16[4,128,128]{2,1,0:T(8,128)(2,1)S(1)}, bf16[4,128,128]{2,1,0:T(8,128)(2,1)S(1)}, u32[]{:S(2)}, u32[]{:S(2)}) collective-permute-start(bf16[4,128,128]{2,1,0:T(8,128)(2,1)S(1)} %get-tuple-element.106), channel_id=1, source_target_pairs={{0,4},{1,5},{2,6},{3,7},{4,0},{5,1},{6,2},{7,3},{8,12},{9,13},{10,... | collective-permute-start | bytes 393224 | tf_op jit(solution)/shard_map/ppermute | solution.py:523
  24.8 5.6 %collective-permute-start.6 = (bf16[4,128,128]{2,1,0:T(8,128)(2,1)S(1)}, bf16[4,128,128]{2,1,0:T(8,128)(2,1)S(1)}, u32[]{:S(2)}, u32[]{:S(2)}) collective-permute-start(bf16[4,128,128]{2,1,0:T(8,128)(2,1)S(1)} %get-tuple-element.113), channel_id=1, source_target_pairs={{0,16},{8,24},{16,0},{24,8},{1,17},{9,25},{17,1},{25,9},{2,18},{10... | collective-permute-start | bytes 393224 | tf_op jit(solution)/shard_map/ppermute | solution.py:523
  26.4 7.0 %collective-permute-start.1 = (bf16[4,128,128]{2,1,0:T(8,128)(2,1)S(1)}, bf16[4,128,128]{2,1,0:T(8,128)(2,1)S(1)}, u32[]{:S(2)}, u32[]{:S(2)}) collective-permute-start(bf16[4,128,128]{2,1,0:T(8,128)(2,1)S(1)} %get-tuple-element.98), channel_id=1, source_target_pairs={{0,2},{1,3},{2,0},{3,1},{4,6},{5,7},{6,4},{7,5},{8,10},{9,11},{10,... | collective-permute-start | bytes 393224 | tf_op jit(solution)/shard_map/ppermute | solution.py:523
  39.0 8.4 %collective-permute-start.12 = (bf16[2,4,64,256]{3,2,1,0:T(8,128)(2,1)S(1)}, bf16[2,4,64,256]{3,2,1,0:T(8,128)(2,1)S(1)}, u32[]{:S(2)}, u32[]{:S(2)}) collective-permute-start(bf16[2,4,64,256]{3,2,1,0:T(8,128)(2,1)S(1)} %get-tuple-element.126), channel_id=1, source_target_pairs={{0,1},{1,0},{2,3},{3,2},{4,5},{5,4},{6,7},{7,6},{8,9},{9,8},{10,11... | collective-permute-start | bytes 786440 | tf_op jit(solution)/shard_map/ppermute | solution.py:523
  40.1 9.0 %collective-permute-start.10 = (bf16[1,8,64,256]{3,2,1,0:T(8,128)(2,1)S(1)}, bf16[1,8,64,256]{3,2,1,0:T(8,128)(2,1)S(1)}, u32[]{:S(2)}, u32[]{:S(2)}) collective-permute-start(bf16[1,8,64,256]{3,2,1,0:T(8,128)(2,1)S(1)} %get-tuple-element.124), channel_id=1, source_target_pairs={{0,16},{8,24},{16,0},{24,8},{1,17},{9,25},{17,1},{25,9},{2,18},{10... | collective-permute-start | bytes 786440 | tf_op jit(solution)/shard_map/ppermute | solution.py:523
  41.7 12.0 %collective-permute-start.22 = (bf16[4,128,128]{2,1,0:T(8,128)(2,1)S(1)}, bf16[4,128,128]{2,1,0:T(8,128)(2,1)S(1)}, u32[]{:S(2)}, u32[]{:S(2)}) collective-permute-start(bf16[4,128,128]{2,1,0:T(8,128)(2,1)S(1)} %get-tuple-element.150), channel_id=1, source_target_pairs={{0,4},{1,5},{2,6},{3,7},{4,0},{5,1},{6,2},{7,3},{8,12},{9,13},{10,... | collective-permute-start | bytes 393224 | tf_op jit(solution)/shard_map/ppermute | solution.py:523
  47.5 6.3 %collective-permute-start.13 = (bf16[1,4,64,256]{3,2,1,0:T(8,128)(2,1)S(1)}, bf16[1,4,64,256]{3,2,1,0:T(8,128)(2,1)S(1)}, u32[]{:S(2)}, u32[]{:S(2)}) collective-permute-start(bf16[1,4,64,256]{3,2,1,0:T(8,128)(2,1)S(1)} %get-tuple-element.178), channel_id=1, source_target_pairs={{0,16},{8,24},{16,0},{24,8},{1,17},{9,25},{17,1},{25,9},{2,18},{10... | collective-permute-start | bytes 393224 | tf_op jit(solution)/shard_map/ppermute | solution.py:523
  53.7 7.1 %collective-permute-start.23 = (bf16[4,128,128]{2,1,0:T(8,128)(2,1)S(1)}, bf16[4,128,128]{2,1,0:T(8,128)(2,1)S(1)}, u32[]{:S(2)}, u32[]{:S(2)}) collective-permute-start(bf16[4,128,128]{2,1,0:T(8,128)(2,1)S(1)} %get-tuple-element.154), channel_id=1, source_target_pairs={{0,8},{8,0},{16,24},{24,16},{1,9},{9,1},{17,25},{25,17},{2,10},{10... | collective-permute-start | bytes 393224 | tf_op jit(solution)/shard_map/ppermute | solution.py:523
  54.2 7.5 %collective-permute-start.14 = (bf16[2,1,64,256]{3,2,1,0:T(8,128)(2,1)S(1)}, bf16[2,1,64,256]{3,2,1,0:T(8,128)(2,1)S(1)}, u32[]{:S(2)}, u32[]{:S(2)}) collective-permute-start(bf16[2,1,64,256]{3,2,1,0:T(8,128)(2,1)S(1)} %get-tuple-element.136), channel_id=1, source_target_pairs={{0,4},{1,5},{2,6},{3,7},{4,0},{5,1},{6,2},{7,3},{8,12},{9,13},{10,... | collective-permute-start | bytes 196616 | tf_op jit(solution)/shard_map/ppermute | solution.py:616
  55.4 6.3 %collective-permute-start.15 = (bf16[2,1,64,256]{3,2,1,0:T(8,128)(2,1)S(1)}, bf16[2,1,64,256]{3,2,1,0:T(8,128)(2,1)S(1)}, u32[]{:S(2)}, u32[]{:S(2)}) collective-permute-start(bf16[2,1,64,256]{3,2,1,0:T(8,128)(2,1)S(1)} %get-tuple-element.137), channel_id=1, source_target_pairs={{0,2},{1,3},{2,0},{3,1},{4,6},{5,7},{6,4},{7,5},{8,10},{9,11},{10,... | collective-permute-start | bytes 196616 | tf_op jit(solution)/shard_map/ppermute | solution.py:616
  58.0 6.1 %collective-permute-start.16 = (bf16[2,1,64,256]{3,2,1,0:T(8,128)(2,1)S(1)}, bf16[2,1,64,256]{3,2,1,0:T(8,128)(2,1)S(1)}, u32[]{:S(2)}, u32[]{:S(2)}) collective-permute-start(bf16[2,1,64,256]{3,2,1,0:T(8,128)(2,1)S(1)} %get-tuple-element.138), channel_id=1, source_target_pairs={{0,6},{1,7},{2,4},{3,5},{4,2},{5,3},{6,0},{7,1},{8,14},{9,15},{10,... | collective-permute-start | bytes 196616 | tf_op jit(solution)/shard_map/ppermute | solution.py:616
  60.8 12.1 %collective-permute-start.24 = (bf16[4,128,128]{2,1,0:T(8,128)(2,1)S(1)}, bf16[4,128,128]{2,1,0:T(8,128)(2,1)S(1)}, u32[]{:S(2)}, u32[]{:S(2)}) collective-permute-start(bf16[4,128,128]{2,1,0:T(8,128)(2,1)S(1)} %get-tuple-element.158), channel_id=1, source_target_pairs={{0,16},{8,24},{16,0},{24,8},{1,17},{9,25},{17,1},{25,9},{2,18},{10... | collective-permute-start | bytes 393224 | tf_op jit(solution)/shard_map/ppermute | solution.py:523
  64.2 6.3 %collective-permute-start.17 = (bf16[2,1,64,256]{3,2,1,0:T(8,128)(2,1)S(1)}, bf16[2,1,64,256]{3,2,1,0:T(8,128)(2,1)S(1)}, u32[]{:S(2)}, u32[]{:S(2)}) collective-permute-start(bf16[2,1,64,256]{3,2,1,0:T(8,128)(2,1)S(1)} %get-tuple-element.141.refs_0_), channel_id=1, source_target_pairs={{0,4},{1,5},{2,6},{3,7},{4,0},{5,1},{6,2},{7,3},{8,12},{9,13},{10,... | collective-permute-start | bytes 196616 | tf_op jit(solution)/shard_map/ppermute | solution.py:616
  64.9 5.7 %collective-permute-start.18 = (bf16[2,1,64,256]{3,2,1,0:T(8,128)(2,1)S(1)}, bf16[2,1,64,256]{3,2,1,0:T(8,128)(2,1)S(1)}, u32[]{:S(2)}, u32[]{:S(2)}) collective-permute-start(bf16[2,1,64,256]{3,2,1,0:T(8,128)(2,1)S(1)} %get-tuple-element.141.refs_0_), channel_id=1, source_target_pairs={{0,2},{1,3},{2,0},{3,1},{4,6},{5,7},{6,4},{7,5},{8,10},{9,11},{10,... | collective-permute-start | bytes 196616 | tf_op jit(solution)/shard_map/ppermute | solution.py:616
  65.7 6.2 %collective-permute-start.19 = (bf16[2,1,64,256]{3,2,1,0:T(8,128)(2,1)S(1)}, bf16[2,1,64,256]{3,2,1,0:T(8,128)(2,1)S(1)}, u32[]{:S(2)}, u32[]{:S(2)}) collective-permute-start(bf16[2,1,64,256]{3,2,1,0:T(8,128)(2,1)S(1)} %get-tuple-element.141.refs_0_), channel_id=1, source_target_pairs={{0,6},{1,7},{2,4},{3,5},{4,2},{5,3},{6,0},{7,1},{8,14},{9,15},{10,... | collective-permute-start | bytes 196616 | tf_op jit(solution)/shard_map/ppermute | solution.py:616
  71.9 6.1 %collective-permute-start.21 = (bf16[1,6,64,256]{3,2,1,0:T(8,128)(2,1)S(1)}, bf16[1,6,64,256]{3,2,1,0:T(8,128)(2,1)S(1)}, u32[]{:S(2)}, u32[]{:S(2)}) collective-permute-start(bf16[1,6,64,256]{3,2,1,0:T(8,128)(2,1)S(1)} %get-tuple-element.144.a_ref), channel_id=1, source_target_pairs={{0,16},{8,24},{16,0},{24,8},{1,17},{9,25},{17,1},{25,9},{2,18},{10... | collective-permute-start | bytes 589832 | tf_op jit(solution)/shard_map/ppermute | solution.py:523
  73.9 6.1 %collective-permute-start.25 = (bf16[4,128,128]{2,1,0:T(8,128)(2,1)S(1)}, bf16[4,128,128]{2,1,0:T(8,128)(2,1)S(1)}, u32[]{:S(2)}, u32[]{:S(2)}) collective-permute-start(bf16[4,128,128]{2,1,0:T(8,128)(2,1)S(1)} %get-tuple-element.160), channel_id=1, source_target_pairs={{0,1},{1,0},{2,3},{3,2},{4,5},{5,4},{6,7},{7,6},{8,9},{9,8},{10,11... | collective-permute-start | bytes 393224 | tf_op jit(solution)/shard_map/ppermute | solution.py:523
  80.0 7.2 %collective-permute-start.28 = (bf16[1,8,64,256]{3,2,1,0:T(8,128)(2,1)S(1)}, bf16[1,8,64,256]{3,2,1,0:T(8,128)(2,1)S(1)}, u32[]{:S(2)}, u32[]{:S(2)}) collective-permute-start(bf16[1,8,64,256]{3,2,1,0:T(8,128)(2,1)S(1)} %shard_map.148.refs_0_), channel_id=1, source_target_pairs={{0,16},{8,24},{16,0},{24,8},{1,17},{9,25},{17,1},{25,9},{2,18},{10... | collective-permute-start | bytes 786440 | tf_op jit(solution)/shard_map/ppermute | solution.py:523
  81.1 6.4 %collective-permute-start.29 = (bf16[2,4,64,256]{3,2,1,0:T(8,128)(2,1)S(1)}, bf16[2,4,64,256]{3,2,1,0:T(8,128)(2,1)S(1)}, u32[]{:S(2)}, u32[]{:S(2)}) collective-permute-start(bf16[2,4,64,256]{3,2,1,0:T(8,128)(2,1)S(1)} %get-tuple-element.162.refs_1_), channel_id=1, source_target_pairs={{0,1},{1,0},{2,3},{3,2},{4,5},{5,4},{6,7},{7,6},{8,9},{9,8},{10,11... | collective-permute-start | bytes 786440 | tf_op jit(solution)/shard_map/ppermute | solution.py:523
  81.8 5.7 %collective-permute-start.30 = (bf16[1,8,64,256]{3,2,1,0:T(8,128)(2,1)S(1)}, bf16[1,8,64,256]{3,2,1,0:T(8,128)(2,1)S(1)}, u32[]{:S(2)}, u32[]{:S(2)}) collective-permute-start(bf16[1,8,64,256]{3,2,1,0:T(8,128)(2,1)S(1)} %shard_map.148.refs_0_), channel_id=1, source_target_pairs={{0,8},{8,0},{16,24},{24,16},{1,9},{9,1},{17,25},{25,17},{2,10},{10... | collective-permute-start | bytes 786440 | tf_op jit(solution)/shard_map/ppermute | solution.py:523
  81.8 5.7 %collective-permute-start.31 = (bf16[2,4,64,256]{3,2,1,0:T(8,128)(2,1)S(1)}, bf16[2,4,64,256]{3,2,1,0:T(8,128)(2,1)S(1)}, u32[]{:S(2)}, u32[]{:S(2)}) collective-permute-start(bf16[2,4,64,256]{3,2,1,0:T(8,128)(2,1)S(1)} %get-tuple-element.162.refs_1_), channel_id=1, source_target_pairs={{0,8},{8,0},{16,24},{24,16},{1,9},{9,1},{17,25},{25,17},{2,10},{10... | collective-permute-start | bytes 786440 | tf_op jit(solution)/shard_map/ppermute | solution.py:523
  (13 other events, 46.2 us)

commit v6 on v5

--- a/solution.py
+++ b/solution.py
@@ -156,31 +156,32 @@
     )
 
 
-def both_states_body(at, a_ref, b_hbm, sent_ref, own_ref, b_ref, sem):
+def half_states_body(at, other, n_load, a_ref, b_ref, out_ref, *refs):
     rows, width = a_ref.shape
     blocks = rows // SUB
+    source = b_ref
     copies = []
-    for b in range(blocks):
-        here = pl.ds(b * SUB, SUB)
-        copies.append(pltpu.make_async_copy(b_hbm.at[here, :], b_ref.at[here, :], sem.at[b]))
-        copies[b].start()
-    for side, ref in ((1 - at.y(), sent_ref), (at.y(), own_ref)):
-        wait = (lambda b: copies[b].wait()) if ref is sent_ref else (lambda b: None)
-        for j, total in enumerate(sums_of(a_ref, b_ref, side, width // 2, range(blocks), wait)):
-            ref[j] = total.astype(ref.dtype)
-
-
-def both_states(a, b, at):
+    if n_load:
+        source, sem = refs
+        for b in range(blocks):
+            here = pl.ds(b * SUB, SUB)
+            copies.append(pltpu.make_async_copy(b_ref.at[here, :], source.at[here, :], sem.at[b]))
+            copies[b].start()
+    wait = (lambda b: copies[b].wait()) if n_load else (lambda b: None)
+    for j, total in enumerate(sums_of(a_ref, source, at.y() ^ other, width // 2, range(blocks), wait)):
+        out_ref[j] = total.astype(out_ref.dtype)
+
+
+def half_states(a, b, at, other, dtype, n_load):
     rows, width = a.shape
-    shape = (width // 2 // HD, HD, HD)
-    return call(
-        functools.partial(both_states_body, at),
+    return call(
+        functools.partial(half_states_body, at, other, n_load),
         [a, b],
-        [WHOLE, HBM],
-        [(shape, BF16, True), (shape, F32, True), ((rows, width), BF16, True)],
-        rows * width * HD,
+        [WHOLE, HBM if n_load else WHOLE],
+        [((width // 2 // HD, HD, HD), dtype, True)] + [((rows, width), BF16, True)] * n_load,
+        rows * width * HD // 2,
         2 * rows * width,
-        [dma(rows // SUB)],
+        [dma(rows // SUB)] * n_load,
     )
 
 
@@ -408,15 +409,14 @@
     )
 
 
-def adam_all_body(picks, at, *refs):
-    n = len(picks)
-    grads, (master_ref, m1_ref, m2_ref) = refs[:n], refs[n : n + 3]
-    outs, bufs, sem = refs[n + 3 : n + 6], refs[n + 6 : n + 9], refs[n + 9]
-    size = grads[0].shape[1]
+def adam_all_body(picks, at, own_ref, core_ref, master_ref, m1_ref, m2_ref, *refs):
+    outs, bufs, sem = refs[:3], refs[3:6], refs[6]
+    size = own_ref.shape[2]
     copies = []
-    for s in range(n):
-        cols = pl.ds(pl.multiple_of(at.group(picks[s]) * size, size), size)
-        new = adam(grads[s][...].astype(F32), master_ref[:, cols], m1_ref[:, cols], m2_ref[:, cols])
+    for s, pick in enumerate(picks):
+        grad = (own_ref if s < 2 else core_ref)[s % 2].astype(F32)
+        cols = pl.ds(pl.multiple_of(at.group(pick) * size, size), size)
+        new = adam(grad, master_ref[:, cols], m1_ref[:, cols], m2_ref[:, cols])
         for i in range(3):
             bufs[i][s] = new[i]
             copy = pltpu.make_async_copy(bufs[i].at[s], outs[i].at[:, cols], sem.at[s * 3 + i])
@@ -426,13 +426,13 @@
         copy.wait()
 
 
-def adam_all(grads, master, moment1, moment2, at, picks):
-    n = len(grads)
-    rows, cols = grads[0].shape
+def adam_all(own, core, master, moment1, moment2, at, picks):
+    n = len(picks)
+    _, rows, cols = own.shape
     return call(
         functools.partial(adam_all_body, picks, at),
-        [*grads, master, moment1, moment2],
-        [WHOLE] * (n + 3),
+        [own, core, master, moment1, moment2],
+        [WHOLE] * 5,
         [(master.shape, F32, False)] * 3,
         n * rows * cols,
         26 * n * rows * cols,
@@ -662,17 +662,17 @@
     )
 
 
-def rejoin_body(a_ref, b_ref, out, grad_out):
+def rejoin_body(a_ref, b_ref, out, grads_out):
     n, part = out.shape[1:3]
-    out[0:1] = a_ref[:, :n]
-    out[1:2] = b_ref[:, :n]
-    for i in range(2):
-        grad_out[i * part : (i + 1) * part] = b_ref[0, n + i]
+    for j, ref in enumerate((a_ref, b_ref)):
+        out[j : j + 1] = ref[:, :n]
+        for i in range(2):
+            grads_out[j, i * part : (i + 1) * part] = ref[0, n + i]
 
 
 def rejoin(a, b):
     _, n, part, cols = a.shape
-    outs = [((2, n - 2, part, cols), BF16, True), ((2 * part, cols), BF16, True)]
+    outs = [((2, n - 2, part, cols), BF16, True), ((2, 2 * part, cols), BF16, True)]
     return call(rejoin_body, [a, b], [WHOLE] * 2, outs)
 
 
@@ -699,23 +699,24 @@
     next(qg)
     qg.send([])
     g, q, v = loaded[1:]
-    kv_sent, kv_own, k = both_states(v, keys, at)
+    kv_sent, k = half_states(v, keys, at, 1, BF16, 1)
+    (kv_own,) = half_states(v, tie(k, kv_sent), at, 0, F32, 0)
     kv = scan_states(lambda: kv_own, kv_sent, False, at)
     kv_stages = i_bits + 2
-    done = [kv_own]
+    done = [kv_sent]
     in_own = kv_got = None
     for _ in range(2, i_bits):
         qg.send(done)
         done = []
         if in_own is None:
-            in_own = key_inside(tie(g, kv_own), q, v, at, 0, att_scale)
+            in_own = key_inside(tie(g, kv_sent), q, v, at, 0, att_scale)
             kv_got = next(kv)
-            done = [in_own] + [kv_got] * 1
+            turned = turned_inputs(tie(inputs, in_own), at)
+            done = [in_own, turned] + [kv_got] * 1
     qg.send(done)
     qg.send([])
     in_oth = key_inside(tie(g, in_own), q, v, at, 1, att_scale)
     qg_own, qg_oth = qg.send([in_oth])
-    turned = turned_inputs(tie(inputs, in_oth), at)
 
     def kv_next(*after):
         nonlocal kv_stages, kv_got
@@ -761,18 +762,18 @@
     p, q = split(grad, weight, *swap_all([weight] * len(groups[0]), groups[0]))
     p_got, q_got = swap(p, "inner", 0), swap(q, "outer", 1)
     p = join(1, p, p_got)
-    q, grad_x = rejoin(q, q_got)
+    q, grads = rejoin(q, q_got)
     p, q, kv_oth = lax.optimization_barrier((p, q, kv_oth))
     p_last, q_last = swap(p, "outer", 1), swap(q, "inner", 0)
     p_core, q_core = swap(p, "outer", 0), swap(q, "outer", 0)
-    grads = [grad, swap(grad, "outer", 0), grad_x, swap(grad_x, "outer", 0)]
+    grads_core = swap(grads, "outer", 0)
     n = n_inner // 2
     query_grad, weights = finish(
         tie(g, p, q), query_own, query_oth, kv_own, kv_oth, at, att_scale,
         [(p, (0, (0,), 0, 2 * n)), (q, (1, (0, 2), 0, n))],
     )
     new_master, new_moment1, new_moment2 = adam_all(
-        [tie(grads[0], weights)] + grads[1:], master, moment1, moment2, at, (0, 1, 2, 3)
+        tie(grads, weights), grads_core, master, moment1, moment2, at, (0, 2, 1, 3)
     )
     p_last, q_last, p_core, q_core, *_ = lax.optimization_barrier(
         (p_last, q_last, p_core, q_core, weights, query_grad, new_master)

time: 90.7 us -> 89.3 us (0.985)
  waiting for transfers between devices: 24.6 us -> 23.2 us
    ppermute x28 -> x27, waiting for transfers between devices: 19.1 us -> 17.1 us  [swap(): return lax.ppermute(x, axis, [(i, i ^ 1 << bit) for i in range(n)])]
    ppermute x28 -> x27, starting transfers between devices: 25.7 us -> 25.9 us  [swap(): return lax.ppermute(x, axis, [(i, i ^ 1 << bit) for i in range(n)])]
    pallas_call x31 -> x32, Pallas kernels: 30 us -> 29.9 us  [call(): pl.pallas_call(body, in_specs=specs, out_specs=[WHOLE if near else HBM fo...]
  transfers between devices with their start and end apart: 34 -> 33, of which waited for: 17 -> 18; matrix products, arithmetic and copies ran while one was open for 0% -> 0% of each run, Pallas kernels for 29% -> 30%
where the time goes in v6:
time: 89.3 us; the launch traced here: 89.1 us
  starting transfers between devices  34.8 us (39%)
  Pallas kernels  29.9 us (33%)
  waiting for transfers between devices  23.2 us (26%)
  between operations  1.12 us (1%)
    pallas_call x32, Pallas kernels, call(): pl.pallas_call(body, in_specs=specs, out_specs=[WHOLE if near else HBM fo...  29.9 us
    ppermute x27, starting transfers between devices, swap(): return lax.ppermute(x, axis, [(i, i ^ 1 << bit) for i in range(n)])  25.9 us
    ppermute x27, waiting for transfers between devices, swap(): return lax.ppermute(x, axis, [(i, i ^ 1 << bit) for i in range(n)])  17.1 us
    ppermute x6, starting transfers between devices, swap_all(): lax.ppermute(x, 'inner', [(i, i ^ mask) for i in range(n)])  8.9 us
    ppermute x6, waiting for transfers between devices, swap_all(): lax.ppermute(x, 'inner', [(i, i ^ mask) for i in range(n)])  6.04 us
  transfers between devices with their start and end apart: 33, of which 18 were waited for; matrix products, arithmetic and copies ran while one was open for 0% of the time, Pallas kernels for 30%

profile of v6, /device:TPU:0, one launch (start us, length us, event | category | flops | bytes accessed | tf_op | source)
XLA Modules:
  0.0 89.1 jit_solution(505081940856303155)
XLA Ops:
  0.6 2.2 %shard_map.132 = bf16[4,128,128]{2,1,0:T(8,128)(2,1)S(1)} custom-call(bf16[1024,1024]{1,0:T(8,128)(2,1)} %a_hbm.1, bf16[1024,1024]{1,0:T(8,128)(2,1)} %b_hbm.1), custom_call_target="tpu_custom_call" | custom-call | flops 134217728 | bytes 2097152 | tf_op jit(solution)/shard_map/pallas_call | solution.py:31
  2.8 3.0 %collective-permute-start.2 = (bf16[4,128,128]{2,1,0:T(8,128)(2,1)S(1)}, bf16[4,128,128]{2,1,0:T(8,128)(2,1)S(1)}, u32[]{:S(2)}, u32[]{:S(2)}) collective-permute-start(bf16[4,128,128]{2,1,0:T(8,128)(2,1)S(1)} %shard_map.132), channel_id=1, source_target_pairs={{0,1},{1,0},{2,3},{3,2},{4,5},{5,4},{6,7},{7,6},{8,9},{9,8},{10,11... | collective-permute-start | bytes 393224 | tf_op jit(solution)/shard_map/ppermute | solution.py:523
  5.8 3.3 %shard_map.127 = (f32[4,128,128]{2,1,0:T(8,128)S(1)}, bf16[1024,1024]{1,0:T(8,128)(2,1)S(1)}, bf16[1024,1024]{1,0:T(8,128)(2,1)S(1)}, bf16[1024,1024]{1,0:T(8,128)(2,1)S(1)}) custom-call(bf16[1024,1024]{1,0:T(8,128)(2,1)} %a_hbm.1, bf16[1024,1024]{1,0:T(8,128)(2,1)} %b_hbm.1, bf16[1024,1024]{1,0:T(8,128)(2,1)} %refs_2_.1), custom_call_target="tpu_custom_call" | custom-call | flops 134217728 | bytes 12582912 | tf_op jit(solution)/shard_map/pallas_call | solution.py:31
  9.4 1.9 %collective-permute-start.3 = (bf16[4,128,128]{2,1,0:T(8,128)(2,1)S(1)}, bf16[4,128,128]{2,1,0:T(8,128)(2,1)S(1)}, u32[]{:S(2)}, u32[]{:S(2)}) collective-permute-start(bf16[4,128,128]{2,1,0:T(8,128)(2,1)S(1)} %get-tuple-element.103), channel_id=1, source_target_pairs={{0,2},{1,3},{2,0},{3,1},{4,6},{5,7},{6,4},{7,5},{8,10},{9,11},{10,... | collective-permute-start | bytes 393224 | tf_op jit(solution)/shard_map/ppermute | solution.py:523
  11.2 2.3 %shard_map.128 = (bf16[4,128,128]{2,1,0:T(8,128)(2,1)S(1)}, bf16[1024,1024]{1,0:T(8,128)(2,1)S(1)}) custom-call(bf16[1024,1024]{1,0:T(8,128)(2,1)S(1)} %get-tuple-element.93.a_ref.v_ref, bf16[1024,1024]{1,0:T(8,128)(2,1)} %b_ref.1), custom_call_target="tpu_custom_call" | custom-call | flops 134217728 | bytes 2097152 | tf_op jit(solution)/shard_map/pallas_call | solution.py:31
  13.5 1.6 %collective-permute-start = (bf16[4,128,128]{2,1,0:T(8,128)(2,1)S(1)}, bf16[4,128,128]{2,1,0:T(8,128)(2,1)S(1)}, u32[]{:S(2)}, u32[]{:S(2)}) collective-permute-start(bf16[4,128,128]{2,1,0:T(8,128)(2,1)S(1)} %get-tuple-element.94), channel_id=1, source_target_pairs={{0,1},{1,0},{2,3},{3,2},{4,5},{5,4},{6,7},{7,6},{8,9},{9,8},{10,11... | collective-permute-start | bytes 393224 | tf_op jit(solution)/shard_map/ppermute | solution.py:523
  15.1 2.7 %collective-permute-start.4 = (bf16[4,128,128]{2,1,0:T(8,128)(2,1)S(1)}, bf16[4,128,128]{2,1,0:T(8,128)(2,1)S(1)}, u32[]{:S(2)}, u32[]{:S(2)}) collective-permute-start(bf16[4,128,128]{2,1,0:T(8,128)(2,1)S(1)} %get-tuple-element.107), channel_id=1, source_target_pairs={{0,4},{1,5},{2,6},{3,7},{4,0},{5,1},{6,2},{7,3},{8,12},{9,13},{10,... | collective-permute-start | bytes 393224 | tf_op jit(solution)/shard_map/ppermute | solution.py:523
  17.8 2.0 %shard_map.129.inside_ref = f32[1024,512]{1,0:T(8,128)S(1)} custom-call(bf16[1024,1024]{1,0:T(8,128)(2,1)S(1)} %get-tuple-element.163.g_ref, bf16[1024,1024]{1,0:T(8,128)(2,1)S(1)} %get-tuple-element.96.q_ref, bf16[1024,1024]{1,0:T(8,128)(2,1)S(1)} %get-tuple-element.93.a_ref.v_ref), custom_call_target="tpu_custom_call" | custom-call | flops 805306368 | bytes 5242880 | tf_op jit(solution)/shard_map/pallas_call | solution.py:31
  19.8 2.0 %shard_map.135.turned_ref = bf16[1024,1024]{1,0:T(8,128)(2,1)S(1)} custom-call(bf16[1024,1024]{1,0:T(8,128)(2,1)} %in_hbm), custom_call_target="tpu_custom_call" | custom-call | bytes 4194304 | tf_op jit(solution)/shard_map/pallas_call | solution.py:31
  24.2 1.6 %collective-permute-start.6 = (bf16[4,128,128]{2,1,0:T(8,128)(2,1)S(1)}, bf16[4,128,128]{2,1,0:T(8,128)(2,1)S(1)}, u32[]{:S(2)}, u32[]{:S(2)}) collective-permute-start(bf16[4,128,128]{2,1,0:T(8,128)(2,1)S(1)} %get-tuple-element.115), channel_id=1, source_target_pairs={{0,16},{8,24},{16,0},{24,8},{1,17},{9,25},{17,1},{25,9},{2,18},{10... | collective-permute-start | bytes 393224 | tf_op jit(solution)/shard_map/ppermute | solution.py:523
  27.0 2.0 %shard_map.138.inside_ref = f32[1024,512]{1,0:T(8,128)S(1)} custom-call(bf16[1024,1024]{1,0:T(8,128)(2,1)S(1)} %get-tuple-element.163.g_ref, bf16[1024,1024]{1,0:T(8,128)(2,1)S(1)} %get-tuple-element.96.q_ref, bf16[1024,1024]{1,0:T(8,128)(2,1)S(1)} %get-tuple-element.93.a_ref.v_ref), custom_call_target="tpu_custom_call" | custom-call | flops 805306368 | bytes 5242880 | tf_op jit(solution)/shard_map/pallas_call | solution.py:31
  32.0 1.8 %shard_map.140 = (bf16[1024,256]{1,0:T(8,128)(2,1)S(1)}, bf16[1024,256]{1,0:T(8,128)(2,1)S(1)}, bf16[2,8,64,256]{3,2,1,0:T(8,128)(2,1)S(1)}, bf16[2,8,64,256]{3,2,1,0:T(8,128)(2,1)S(1)}) custom-call(f32[1024,512]{1,0:T(8,128)S(1)} %shard_map.129.inside_ref, bf16[1024,1024]{1,0:T(8,128)(2,1)S(1)} %get-tuple-element.93.a_ref.v_ref, ...), custom_call_target="tpu_custom_call" | custom-call | flops 1207959552 | bytes 6291456 | tf_op jit(solution)/shard_map/pallas_call | solution.py:31
  40.7 2.1 %collective-permute-start.22 = (bf16[4,128,128]{2,1,0:T(8,128)(2,1)S(1)}, bf16[4,128,128]{2,1,0:T(8,128)(2,1)S(1)}, u32[]{:S(2)}, u32[]{:S(2)}) collective-permute-start(bf16[4,128,128]{2,1,0:T(8,128)(2,1)S(1)} %get-tuple-element.150), channel_id=1, source_target_pairs={{0,4},{1,5},{2,6},{3,7},{4,0},{5,1},{6,2},{7,3},{8,12},{9,13},{10,... | collective-permute-start | bytes 393224 | tf_op jit(solution)/shard_map/ppermute | solution.py:523
  42.8 3.9 %collective-permute-done.12 = bf16[2,4,64,256]{3,2,1,0:T(8,128)(2,1)S(1)} collective-permute-done((bf16[2,4,64,256]{3,2,1,0:T(8,128)(2,1)S(1)}, bf16[2,4,64,256]{3,2,1,0:T(8,128)(2,1)S(1)}, u32[]{:S(2)}, u32[]{:S(2)}) %collective-permute-start.12) | collective-permute-done | bytes 262176 | tf_op jit(solution)/shard_map/ppermute | solution.py:523
  46.8 1.6 %collective-permute-start.13 = (bf16[1,4,64,256]{3,2,1,0:T(8,128)(2,1)S(1)}, bf16[1,4,64,256]{3,2,1,0:T(8,128)(2,1)S(1)}, u32[]{:S(2)}, u32[]{:S(2)}) collective-permute-start(bf16[1,4,64,256]{3,2,1,0:T(8,128)(2,1)S(1)} %get-tuple-element.178), channel_id=1, source_target_pairs={{0,16},{8,24},{16,0},{24,8},{1,17},{9,25},{17,1},{25,9},{2,18},{10... | collective-permute-start | bytes 393224 | tf_op jit(solution)/shard_map/ppermute | solution.py:523
  49.3 3.2 %shard_map.145 = (f32[1024,512]{1,0:T(8,128)S(1)}, bf16[1024,1024]{1,0:T(8,128)(2,1)}) custom-call(bf16[1024,1024]{1,0:T(8,128)(2,1)S(1)} %get-tuple-element.163.g_ref, bf16[1024,1024]{1,0:T(8,128)(2,1)S(1)} %get-tuple-element.98.b_ref.k_ref, bf16[1024,1024]{1,0:T(8,128)(2,1)S(1)} %get-tuple-element.93.a_ref.v_ref, ...), custom_call_target="tpu_custom_call" | custom-call | flops 805306368 | bytes 5242880 | tf_op jit(solution)/shard_map/pallas_call | solution.py:31
  53.5 2.0 %collective-permute-start.14 = (bf16[2,1,64,256]{3,2,1,0:T(8,128)(2,1)S(1)}, bf16[2,1,64,256]{3,2,1,0:T(8,128)(2,1)S(1)}, u32[]{:S(2)}, u32[]{:S(2)}) collective-permute-start(bf16[2,1,64,256]{3,2,1,0:T(8,128)(2,1)S(1)} %get-tuple-element.136), channel_id=1, source_target_pairs={{0,4},{1,5},{2,6},{3,7},{4,0},{5,1},{6,2},{7,3},{8,12},{9,13},{10,... | collective-permute-start | bytes 196616 | tf_op jit(solution)/shard_map/ppermute | solution.py:616
  55.4 1.6 %collective-permute-start.15 = (bf16[2,1,64,256]{3,2,1,0:T(8,128)(2,1)S(1)}, bf16[2,1,64,256]{3,2,1,0:T(8,128)(2,1)S(1)}, u32[]{:S(2)}, u32[]{:S(2)}) collective-permute-start(bf16[2,1,64,256]{3,2,1,0:T(8,128)(2,1)S(1)} %get-tuple-element.137), channel_id=1, source_target_pairs={{0,2},{1,3},{2,0},{3,1},{4,6},{5,7},{6,4},{7,5},{8,10},{9,11},{10,... | collective-permute-start | bytes 196616 | tf_op jit(solution)/shard_map/ppermute | solution.py:616
  57.9 2.1 %shard_map.147.in_oth = f32[1024,512]{1,0:T(8,128)S(1)} custom-call(bf16[1024,1024]{1,0:T(8,128)(2,1)S(1)} %get-tuple-element.163.g_ref, bf16[1024,1024]{1,0:T(8,128)(2,1)S(1)} %get-tuple-element.98.b_ref.k_ref, bf16[1024,1024]{1,0:T(8,128)(2,1)S(1)} %get-tuple-element.93.a_ref.v_ref), custom_call_target="tpu_custom_call" | custom-call | flops 805306368 | bytes 5242880 | tf_op jit(solution)/shard_map/pallas_call | solution.py:31
  60.7 2.4 %collective-permute-done.16.refs_3_ = bf16[2,1,64,256]{3,2,1,0:T(8,128)(2,1)S(1)} collective-permute-done((bf16[2,1,64,256]{3,2,1,0:T(8,128)(2,1)S(1)}, bf16[2,1,64,256]{3,2,1,0:T(8,128)(2,1)S(1)}, u32[]{:S(2)}, u32[]{:S(2)}) %collective-permute-start.16) | collective-permute-done | bytes 65568 | tf_op jit(solution)/shard_map/ppermute | solution.py:616
  65.1 2.5 %collective-permute-start.19 = (bf16[2,1,64,256]{3,2,1,0:T(8,128)(2,1)S(1)}, bf16[2,1,64,256]{3,2,1,0:T(8,128)(2,1)S(1)}, u32[]{:S(2)}, u32[]{:S(2)}) collective-permute-start(bf16[2,1,64,256]{3,2,1,0:T(8,128)(2,1)S(1)} %get-tuple-element.141.refs_0_), channel_id=1, source_target_pairs={{0,6},{1,7},{2,4},{3,5},{4,2},{5,3},{6,0},{7,1},{8,14},{9,15},{10,... | collective-permute-start | bytes 196616 | tf_op jit(solution)/shard_map/ppermute | solution.py:616
  67.7 2.2 %collective-permute-done.17.refs_1_ = bf16[2,1,64,256]{3,2,1,0:T(8,128)(2,1)S(1)} collective-permute-done((bf16[2,1,64,256]{3,2,1,0:T(8,128)(2,1)S(1)}, bf16[2,1,64,256]{3,2,1,0:T(8,128)(2,1)S(1)}, u32[]{:S(2)}, u32[]{:S(2)}) %collective-permute-start.17) | collective-permute-done | bytes 65568 | tf_op jit(solution)/shard_map/ppermute | solution.py:616
  74.6 2.8 %collective-permute-done.20.refs_1_ = bf16[1,4,64,256]{3,2,1,0:T(8,128)(2,1)S(1)} collective-permute-done((bf16[1,4,64,256]{3,2,1,0:T(8,128)(2,1)S(1)}, bf16[1,4,64,256]{3,2,1,0:T(8,128)(2,1)S(1)}, u32[]{:S(2)}, u32[]{:S(2)}) %collective-permute-start.20) | collective-permute-done | bytes 131104 | tf_op jit(solution)/shard_map/ppermute | solution.py:523
  81.4 1.9 %shard_map.155 = (bf16[1024,1024]{1,0:T(8,128)(2,1)}, bf16[4,2,2,64,1024]{4,3,2,1,0:T(8,128)(2,1)}) custom-call(bf16[1024,1024]{1,0:T(8,128)(2,1)S(1)} %get-tuple-element.163.g_ref, f32[1024,512]{1,0:T(8,128)S(1)} %get-tuple-element.135.in_own, f32[1024,512]{1,0:T(8,128)S(1)} %shard_map.147.in_oth, bf16[4,128,128]{2,1,0:T(8,128)(2,1)S(1)} %get-tuple-element.164.own_ref, ...), custom_call_target="tpu_custom_call" | custom-call | flops 268435456 | bytes 8388608 | tf_op jit(solution)/shard_map/pallas_call | solution.py:31
  (82 shorter events, 33.6 us)
Async XLA Ops:
  2.8 6.5 %collective-permute-start.2 = (bf16[4,128,128]{2,1,0:T(8,128)(2,1)S(1)}, bf16[4,128,128]{2,1,0:T(8,128)(2,1)S(1)}, u32[]{:S(2)}, u32[]{:S(2)}) collective-permute-start(bf16[4,128,128]{2,1,0:T(8,128)(2,1)S(1)} %shard_map.132), channel_id=1, source_target_pairs={{0,1},{1,0},{2,3},{3,2},{4,5},{5,4},{6,7},{7,6},{8,9},{9,8},{10,11... | collective-permute-start | bytes 393224 | tf_op jit(solution)/shard_map/ppermute | solution.py:523
  9.4 5.7 %collective-permute-start.3 = (bf16[4,128,128]{2,1,0:T(8,128)(2,1)S(1)}, bf16[4,128,128]{2,1,0:T(8,128)(2,1)S(1)}, u32[]{:S(2)}, u32[]{:S(2)}) collective-permute-start(bf16[4,128,128]{2,1,0:T(8,128)(2,1)S(1)} %get-tuple-element.103), channel_id=1, source_target_pairs={{0,2},{1,3},{2,0},{3,1},{4,6},{5,7},{6,4},{7,5},{8,10},{9,11},{10,... | collective-permute-start | bytes 393224 | tf_op jit(solution)/shard_map/ppermute | solution.py:523
  13.5 8.3 %collective-permute-start = (bf16[4,128,128]{2,1,0:T(8,128)(2,1)S(1)}, bf16[4,128,128]{2,1,0:T(8,128)(2,1)S(1)}, u32[]{:S(2)}, u32[]{:S(2)}) collective-permute-start(bf16[4,128,128]{2,1,0:T(8,128)(2,1)S(1)} %get-tuple-element.94), channel_id=1, source_target_pairs={{0,1},{1,0},{2,3},{3,2},{4,5},{5,4},{6,7},{7,6},{8,9},{9,8},{10,11... | collective-permute-start | bytes 393224 | tf_op jit(solution)/shard_map/ppermute | solution.py:523
  15.1 7.6 %collective-permute-start.4 = (bf16[4,128,128]{2,1,0:T(8,128)(2,1)S(1)}, bf16[4,128,128]{2,1,0:T(8,128)(2,1)S(1)}, u32[]{:S(2)}, u32[]{:S(2)}) collective-permute-start(bf16[4,128,128]{2,1,0:T(8,128)(2,1)S(1)} %get-tuple-element.107), channel_id=1, source_target_pairs={{0,4},{1,5},{2,6},{3,7},{4,0},{5,1},{6,2},{7,3},{8,12},{9,13},{10,... | collective-permute-start | bytes 393224 | tf_op jit(solution)/shard_map/ppermute | solution.py:523
  24.2 5.6 %collective-permute-start.6 = (bf16[4,128,128]{2,1,0:T(8,128)(2,1)S(1)}, bf16[4,128,128]{2,1,0:T(8,128)(2,1)S(1)}, u32[]{:S(2)}, u32[]{:S(2)}) collective-permute-start(bf16[4,128,128]{2,1,0:T(8,128)(2,1)S(1)} %get-tuple-element.115), channel_id=1, source_target_pairs={{0,16},{8,24},{16,0},{24,8},{1,17},{9,25},{17,1},{25,9},{2,18},{10... | collective-permute-start | bytes 393224 | tf_op jit(solution)/shard_map/ppermute | solution.py:523
  26.7 5.3 %collective-permute-start.1 = (bf16[4,128,128]{2,1,0:T(8,128)(2,1)S(1)}, bf16[4,128,128]{2,1,0:T(8,128)(2,1)S(1)}, u32[]{:S(2)}, u32[]{:S(2)}) collective-permute-start(bf16[4,128,128]{2,1,0:T(8,128)(2,1)S(1)} %get-tuple-element.99), channel_id=1, source_target_pairs={{0,2},{1,3},{2,0},{3,1},{4,6},{5,7},{6,4},{7,5},{8,10},{9,11},{10,... | collective-permute-start | bytes 393224 | tf_op jit(solution)/shard_map/ppermute | solution.py:523
  38.3 8.4 %collective-permute-start.12 = (bf16[2,4,64,256]{3,2,1,0:T(8,128)(2,1)S(1)}, bf16[2,4,64,256]{3,2,1,0:T(8,128)(2,1)S(1)}, u32[]{:S(2)}, u32[]{:S(2)}) collective-permute-start(bf16[2,4,64,256]{3,2,1,0:T(8,128)(2,1)S(1)} %get-tuple-element.127), channel_id=1, source_target_pairs={{0,1},{1,0},{2,3},{3,2},{4,5},{5,4},{6,7},{7,6},{8,9},{9,8},{10,11... | collective-permute-start | bytes 786440 | tf_op jit(solution)/shard_map/ppermute | solution.py:523
  39.2 9.1 %collective-permute-start.10 = (bf16[1,8,64,256]{3,2,1,0:T(8,128)(2,1)S(1)}, bf16[1,8,64,256]{3,2,1,0:T(8,128)(2,1)S(1)}, u32[]{:S(2)}, u32[]{:S(2)}) collective-permute-start(bf16[1,8,64,256]{3,2,1,0:T(8,128)(2,1)S(1)} %get-tuple-element.125), channel_id=1, source_target_pairs={{0,16},{8,24},{16,0},{24,8},{1,17},{9,25},{17,1},{25,9},{2,18},{10... | collective-permute-start | bytes 786440 | tf_op jit(solution)/shard_map/ppermute | solution.py:523
  40.7 11.7 %collective-permute-start.22 = (bf16[4,128,128]{2,1,0:T(8,128)(2,1)S(1)}, bf16[4,128,128]{2,1,0:T(8,128)(2,1)S(1)}, u32[]{:S(2)}, u32[]{:S(2)}) collective-permute-start(bf16[4,128,128]{2,1,0:T(8,128)(2,1)S(1)} %get-tuple-element.150), channel_id=1, source_target_pairs={{0,4},{1,5},{2,6},{3,7},{4,0},{5,1},{6,2},{7,3},{8,12},{9,13},{10,... | collective-permute-start | bytes 393224 | tf_op jit(solution)/shard_map/ppermute | solution.py:523
  46.8 5.9 %collective-permute-start.13 = (bf16[1,4,64,256]{3,2,1,0:T(8,128)(2,1)S(1)}, bf16[1,4,64,256]{3,2,1,0:T(8,128)(2,1)S(1)}, u32[]{:S(2)}, u32[]{:S(2)}) collective-permute-start(bf16[1,4,64,256]{3,2,1,0:T(8,128)(2,1)S(1)} %get-tuple-element.178), channel_id=1, source_target_pairs={{0,16},{8,24},{16,0},{24,8},{1,17},{9,25},{17,1},{25,9},{2,18},{10... | collective-permute-start | bytes 393224 | tf_op jit(solution)/shard_map/ppermute | solution.py:523
  52.5 7.5 %collective-permute-start.23 = (bf16[4,128,128]{2,1,0:T(8,128)(2,1)S(1)}, bf16[4,128,128]{2,1,0:T(8,128)(2,1)S(1)}, u32[]{:S(2)}, u32[]{:S(2)}) collective-permute-start(bf16[4,128,128]{2,1,0:T(8,128)(2,1)S(1)} %get-tuple-element.154), channel_id=1, source_target_pairs={{0,8},{8,0},{16,24},{24,16},{1,9},{9,1},{17,25},{25,17},{2,10},{10... | collective-permute-start | bytes 393224 | tf_op jit(solution)/shard_map/ppermute | solution.py:523
  53.5 7.2 %collective-permute-start.14 = (bf16[2,1,64,256]{3,2,1,0:T(8,128)(2,1)S(1)}, bf16[2,1,64,256]{3,2,1,0:T(8,128)(2,1)S(1)}, u32[]{:S(2)}, u32[]{:S(2)}) collective-permute-start(bf16[2,1,64,256]{3,2,1,0:T(8,128)(2,1)S(1)} %get-tuple-element.136), channel_id=1, source_target_pairs={{0,4},{1,5},{2,6},{3,7},{4,0},{5,1},{6,2},{7,3},{8,12},{9,13},{10,... | collective-permute-start | bytes 196616 | tf_op jit(solution)/shard_map/ppermute | solution.py:616
  55.4 5.2 %collective-permute-start.15 = (bf16[2,1,64,256]{3,2,1,0:T(8,128)(2,1)S(1)}, bf16[2,1,64,256]{3,2,1,0:T(8,128)(2,1)S(1)}, u32[]{:S(2)}, u32[]{:S(2)}) collective-permute-start(bf16[2,1,64,256]{3,2,1,0:T(8,128)(2,1)S(1)} %get-tuple-element.137), channel_id=1, source_target_pairs={{0,2},{1,3},{2,0},{3,1},{4,6},{5,7},{6,4},{7,5},{8,10},{9,11},{10,... | collective-permute-start | bytes 196616 | tf_op jit(solution)/shard_map/ppermute | solution.py:616
  57.0 6.1 %collective-permute-start.16 = (bf16[2,1,64,256]{3,2,1,0:T(8,128)(2,1)S(1)}, bf16[2,1,64,256]{3,2,1,0:T(8,128)(2,1)S(1)}, u32[]{:S(2)}, u32[]{:S(2)}) collective-permute-start(bf16[2,1,64,256]{3,2,1,0:T(8,128)(2,1)S(1)} %get-tuple-element.138), channel_id=1, source_target_pairs={{0,6},{1,7},{2,4},{3,5},{4,2},{5,3},{6,0},{7,1},{8,14},{9,15},{10,... | collective-permute-start | bytes 196616 | tf_op jit(solution)/shard_map/ppermute | solution.py:616
  60.1 12.4 %collective-permute-start.24 = (bf16[4,128,128]{2,1,0:T(8,128)(2,1)S(1)}, bf16[4,128,128]{2,1,0:T(8,128)(2,1)S(1)}, u32[]{:S(2)}, u32[]{:S(2)}) collective-permute-start(bf16[4,128,128]{2,1,0:T(8,128)(2,1)S(1)} %get-tuple-element.158), channel_id=1, source_target_pairs={{0,16},{8,24},{16,0},{24,8},{1,17},{9,25},{17,1},{25,9},{2,18},{10... | collective-permute-start | bytes 393224 | tf_op jit(solution)/shard_map/ppermute | solution.py:523
  63.2 6.7 %collective-permute-start.17 = (bf16[2,1,64,256]{3,2,1,0:T(8,128)(2,1)S(1)}, bf16[2,1,64,256]{3,2,1,0:T(8,128)(2,1)S(1)}, u32[]{:S(2)}, u32[]{:S(2)}) collective-permute-start(bf16[2,1,64,256]{3,2,1,0:T(8,128)(2,1)S(1)} %get-tuple-element.141.refs_0_), channel_id=1, source_target_pairs={{0,4},{1,5},{2,6},{3,7},{4,0},{5,1},{6,2},{7,3},{8,12},{9,13},{10,... | collective-permute-start | bytes 196616 | tf_op jit(solution)/shard_map/ppermute | solution.py:616
  64.6 5.5 %collective-permute-start.18 = (bf16[2,1,64,256]{3,2,1,0:T(8,128)(2,1)S(1)}, bf16[2,1,64,256]{3,2,1,0:T(8,128)(2,1)S(1)}, u32[]{:S(2)}, u32[]{:S(2)}) collective-permute-start(bf16[2,1,64,256]{3,2,1,0:T(8,128)(2,1)S(1)} %get-tuple-element.141.refs_0_), channel_id=1, source_target_pairs={{0,2},{1,3},{2,0},{3,1},{4,6},{5,7},{6,4},{7,5},{8,10},{9,11},{10,... | collective-permute-start | bytes 196616 | tf_op jit(solution)/shard_map/ppermute | solution.py:616
  65.1 6.2 %collective-permute-start.19 = (bf16[2,1,64,256]{3,2,1,0:T(8,128)(2,1)S(1)}, bf16[2,1,64,256]{3,2,1,0:T(8,128)(2,1)S(1)}, u32[]{:S(2)}, u32[]{:S(2)}) collective-permute-start(bf16[2,1,64,256]{3,2,1,0:T(8,128)(2,1)S(1)} %get-tuple-element.141.refs_0_), channel_id=1, source_target_pairs={{0,6},{1,7},{2,4},{3,5},{4,2},{5,3},{6,0},{7,1},{8,14},{9,15},{10,... | collective-permute-start | bytes 196616 | tf_op jit(solution)/shard_map/ppermute | solution.py:616
  71.3 6.1 %collective-permute-start.21 = (bf16[1,6,64,256]{3,2,1,0:T(8,128)(2,1)S(1)}, bf16[1,6,64,256]{3,2,1,0:T(8,128)(2,1)S(1)}, u32[]{:S(2)}, u32[]{:S(2)}) collective-permute-start(bf16[1,6,64,256]{3,2,1,0:T(8,128)(2,1)S(1)} %get-tuple-element.144.a_ref), channel_id=1, source_target_pairs={{0,16},{8,24},{16,0},{24,8},{1,17},{9,25},{17,1},{25,9},{2,18},{10... | collective-permute-start | bytes 589832 | tf_op jit(solution)/shard_map/ppermute | solution.py:523
  73.7 5.1 %collective-permute-start.25 = (bf16[4,128,128]{2,1,0:T(8,128)(2,1)S(1)}, bf16[4,128,128]{2,1,0:T(8,128)(2,1)S(1)}, u32[]{:S(2)}, u32[]{:S(2)}) collective-permute-start(bf16[4,128,128]{2,1,0:T(8,128)(2,1)S(1)} %get-tuple-element.160), channel_id=1, source_target_pairs={{0,1},{1,0},{2,3},{3,2},{4,5},{5,4},{6,7},{7,6},{8,9},{9,8},{10,11... | collective-permute-start | bytes 393224 | tf_op jit(solution)/shard_map/ppermute | solution.py:523
  78.8 6.4 %collective-permute-start.27 = (bf16[1,8,64,256]{3,2,1,0:T(8,128)(2,1)S(1)}, bf16[1,8,64,256]{3,2,1,0:T(8,128)(2,1)S(1)}, u32[]{:S(2)}, u32[]{:S(2)}) collective-permute-start(bf16[1,8,64,256]{3,2,1,0:T(8,128)(2,1)S(1)} %shard_map.149.refs_0_), channel_id=1, source_target_pairs={{0,16},{8,24},{16,0},{24,8},{1,17},{9,25},{17,1},{25,9},{2,18},{10... | collective-permute-start | bytes 786440 | tf_op jit(solution)/shard_map/ppermute | solution.py:523
  79.8 6.4 %collective-permute-start.28 = (bf16[2,4,64,256]{3,2,1,0:T(8,128)(2,1)S(1)}, bf16[2,4,64,256]{3,2,1,0:T(8,128)(2,1)S(1)}, u32[]{:S(2)}, u32[]{:S(2)}) collective-permute-start(bf16[2,4,64,256]{3,2,1,0:T(8,128)(2,1)S(1)} %get-tuple-element.162.refs_1_), channel_id=1, source_target_pairs={{0,1},{1,0},{2,3},{3,2},{4,5},{5,4},{6,7},{7,6},{8,9},{9,8},{10,11... | collective-permute-start | bytes 786440 | tf_op jit(solution)/shard_map/ppermute | solution.py:523
  80.9 5.3 %collective-permute-start.29 = (bf16[1,8,64,256]{3,2,1,0:T(8,128)(2,1)S(1)}, bf16[1,8,64,256]{3,2,1,0:T(8,128)(2,1)S(1)}, u32[]{:S(2)}, u32[]{:S(2)}) collective-permute-start(bf16[1,8,64,256]{3,2,1,0:T(8,128)(2,1)S(1)} %shard_map.149.refs_0_), channel_id=1, source_target_pairs={{0,8},{8,0},{16,24},{24,16},{1,9},{9,1},{17,25},{25,17},{2,10},{10... | collective-permute-start | bytes 786440 | tf_op jit(solution)/shard_map/ppermute | solution.py:523
  80.9 5.3 %collective-permute-start.30 = (bf16[2,4,64,256]{3,2,1,0:T(8,128)(2,1)S(1)}, bf16[2,4,64,256]{3,2,1,0:T(8,128)(2,1)S(1)}, u32[]{:S(2)}, u32[]{:S(2)}) collective-permute-start(bf16[2,4,64,256]{3,2,1,0:T(8,128)(2,1)S(1)} %get-tuple-element.162.refs_1_), channel_id=1, source_target_pairs={{0,8},{8,0},{16,24},{24,16},{1,9},{9,1},{17,25},{25,17},{2,10},{10... | collective-permute-start | bytes 786440 | tf_op jit(solution)/shard_map/ppermute | solution.py:523
  (12 other events, 45.5 us)

commit v7 on v6

--- a/solution.py
+++ b/solution.py
@@ -70,14 +70,14 @@
 
 
 def states_body(at, a_hbm, b_hbm, out_ref, a_buf, b_buf, a_sem, b_sem):
-    chunks, rows, cols = a_buf.shape
+    chunks, rows, cols = a_buf.shape[0] // SUB, SUB, a_buf.shape[1]
     at = pl.multiple_of((1 - at.y()) * cols, cols)
     copies = []
     for c in range(chunks):
         here = (pl.ds(c * rows, rows), pl.ds(at, cols))
         pair = (
-            pltpu.make_async_copy(a_hbm.at[here], a_buf.at[c], a_sem.at[c]),
-            pltpu.make_async_copy(b_hbm.at[here], b_buf.at[c], b_sem.at[c]),
+            pltpu.make_async_copy(a_hbm.at[here], a_buf.at[pl.ds(c * rows, rows), :], a_sem.at[c]),
+            pltpu.make_async_copy(b_hbm.at[here], b_buf.at[pl.ds(c * rows, rows), :], b_sem.at[c]),
         )
         for copy in pair:
             copy.start()
@@ -87,8 +87,8 @@
         for copy in copies[c]:
             copy.wait()
         for j in range(cols // HD):
-            here = slice(j * HD, (j + 1) * HD)
-            term = mm(a_buf[c, :, here], b_buf[c, :, here], (0, 0))
+            here = (slice(c * rows, (c + 1) * rows), slice(j * HD, (j + 1) * HD))
+            term = mm(a_buf[here], b_buf[here], (0, 0))
             sums[j] = term if c == 0 else sums[j] + term
     for j in range(cols // HD):
         out_ref[j] = sums[j].astype(out_ref.dtype)
@@ -98,16 +98,15 @@
     rows, width = a.shape
     cols = width // 2
     chunks = rows // SUB
-    buf = pltpu.VMEM((chunks, SUB, cols), BF16)
     return call(
         functools.partial(states_body, at),
         [a, b],
         [HBM, HBM],
-        [((cols // HD, HD, HD), dtype, True)],
+        [((cols // HD, HD, HD), dtype, True)] + [((rows, cols), BF16, True)] * 2,
         rows * cols * HD,
         4 * rows * cols,
-        [buf, buf, dma(chunks), dma(chunks)],
-    )[0]
+        [dma(chunks), dma(chunks)],
+    )
 
 
 def sums_of(a_ref, b_ref, at, cols, blocks, wait):
@@ -129,8 +128,9 @@
     for b in range(blocks):
         copies.append([])
         for n in range(n_load):
-            here = pl.ds(b * SUB, SUB)
-            copy = pltpu.make_async_copy(sources[n].at[here, :], loads[n].at[here, :], sem.at[n_load * b + n])
+            here, cols = pl.ds(b * SUB, SUB), loads[n].shape[1]
+            part = pl.ds(pl.multiple_of(at.y() * cols, cols), cols) if n < 2 else slice(None)
+            copy = pltpu.make_async_copy(sources[n].at[here, part], loads[n].at[here, :], sem.at[n_load * b + n])
             copy.start()
             copies[b].append(copy)
 
@@ -138,7 +138,7 @@
         for copy in copies[b]:
             copy.wait()
 
-    for j, total in enumerate(sums_of(loads[0], loads[1], at.y(), width // 2, range(blocks), wait)):
+    for j, total in enumerate(sums_of(loads[0], loads[1], 0, width // 2, range(blocks), wait)):
         out_ref[j] = total
 
 
@@ -149,7 +149,8 @@
         functools.partial(load_body, n, at),
         sources,
         [HBM] * n,
-        [((width // 2 // HD, HD, HD), F32, True)] + [((rows, width), BF16, True)] * n,
+        [((width // 2 // HD, HD, HD), F32, True)]
+        + [((rows, width // 2 if i < 2 else width), BF16, True) for i in range(n)],
         rows * width // 2 * HD,
         4 * n * rows * width,
         [dma(n * (rows // SUB))],
@@ -192,8 +193,8 @@
         from_ = pl.ds(pl.multiple_of((at.y() ^ other) * cols + to, HD), HD)
         state = None
         for b in reversed(range(rows // SUB)):
-            here = (pl.ds(b * SUB, SUB), from_)
-            g, q, v = g_ref[here], q_ref[here], v_ref[here]
+            here, there = (pl.ds(b * SUB, SUB), pl.ds(to, HD)), (pl.ds(b * SUB, SUB), from_)
+            g, q, v = g_ref[here], q_ref[here], v_ref[there]
             scores = jnp.where(later, mm(v, g, (1, 1)), 0.0).astype(BF16)
             total = mm(scores, q, (1, 0))
             if state is not None:
@@ -223,8 +224,8 @@
         from_ = pl.ds(pl.multiple_of((at.y() ^ other) * cols + to, HD), HD)
         state = None
         for b in range(rows // SUB):
-            here = (pl.ds(b * SUB, SUB), from_)
-            g, k, v = g_ref[here], k_ref[here], v_ref[here]
+            here, there = (pl.ds(b * SUB, SUB), pl.ds(to, HD)), (pl.ds(b * SUB, SUB), from_)
+            g, k, v = g_ref[here], k_ref[there], v_ref[there]
             scores = jnp.where(earlier, mm(g, v, (1, 1)), 0.0).astype(BF16)
             total = mm(scores, k, (1, 0))
             if state is not None:
@@ -238,7 +239,7 @@
 
 
 def key_inside(g, q, v, at, other, scale):
-    rows, width = g.shape
+    rows, width = v.shape
     cols = width // 2
     return call(
         functools.partial(key_inside_body, scale, other, at),
@@ -251,7 +252,7 @@
 
 
 def query_inside(g, k, v, at, other, scale, pieces=()):
-    rows, width = g.shape
+    rows, width = v.shape
     cols = width // 2
     kinds = [kind for _, kind in pieces]
     outs = [((rows, cols), F32, True)] + [((rows, width), BF16, False)] * bool(pieces)
@@ -266,17 +267,16 @@
     )
 
 
-def query_body(scale, at, g_ref, in_own, in_oth, own_ref, oth_ref, out_hbm, buf, sem):
+def query_body(scale, at, g_own, g_oth, in_own, in_oth, own_ref, oth_ref, out_hbm, buf, sem):
     n, rows, cols = buf.shape
     copies = []
-    for other, (in_ref, state_ref) in enumerate(((in_own, own_ref), (in_oth, oth_ref))):
+    for other, (g_ref, in_ref, state_ref) in enumerate(((g_own, in_own, own_ref), (g_oth, in_oth, oth_ref))):
         half = at.y() ^ other
         for p in range(n // 2):
             i = other * (n // 2) + p
             for j in range(cols // HD):
                 head = p * (cols // HD) + j
-                from_ = pl.multiple_of((half * (n // 2) + p) * cols + j * HD, HD)
-                part = mm(g_ref[:, pl.ds(from_, HD)], state_ref[head], (1, 0))
+                part = mm(g_ref[:, head * HD : (head + 1) * HD], state_ref[head], (1, 0))
                 total = in_ref[:, head * HD : (head + 1) * HD] + part * scale
                 buf[i, :, j * HD : (j + 1) * HD] = total.astype(BF16)
             to = pl.ds(pl.multiple_of((half * (n // 2) + p) * cols, cols), cols)
@@ -477,23 +477,23 @@
     return bufs + [dma(2 * len(pieces))]
 
 
-def finish_body(scale, at, kinds, g_ref, in_own, in_oth, own_ref, oth_ref, *refs):
+def finish_body(scale, at, kinds, g_own, g_oth, in_own, in_oth, own_ref, oth_ref, *refs):
     n = len(kinds)
     pieces, (out_hbm, weights_hbm, buf, sem) = refs[:n], refs[n : n + 4]
     copies = assemble_start(kinds, at, pieces, weights_hbm, refs[n + 4 : -1], refs[-1])
-    query_body(scale, at, g_ref, in_own, in_oth, own_ref, oth_ref, out_hbm, buf, sem)
+    query_body(scale, at, g_own, g_oth, in_own, in_oth, own_ref, oth_ref, out_hbm, buf, sem)
     for copy in copies:
         copy.wait()
 
 
-def finish(g, in_own, in_oth, own, oth, at, scale, pieces):
-    rows, width = g.shape
+def finish(g_own, g_oth, in_own, in_oth, own, oth, at, scale, pieces):
+    rows, width = g_own.shape[0], 2 * g_own.shape[1]
     n = width // PAIR
     part = pieces[0][0].shape[2]
     return call(
         functools.partial(finish_body, scale, at, [kind for _, kind in pieces]),
-        [g, in_own, in_oth, own, oth, *[array for array, _ in pieces]],
-        [WHOLE] * (5 + len(pieces)),
+        [g_own, g_oth, in_own, in_oth, own, oth, *[array for array, _ in pieces]],
+        [WHOLE] * (6 + len(pieces)),
         [((rows, width), BF16, False), ((at.n_inner // 2, 2, 2, part, width), BF16, False)],
         rows * width * HD,
         8 * rows * width,
@@ -688,18 +688,18 @@
     att_scale = 1.0 / math.sqrt(HD * total_tokens)
     grad_scale = 1.0 / math.sqrt(total_tokens)
 
-    qg_sent = states(out_grad, queries, at, BF16)
+    qg_sent, g_oth, q_oth = states(out_grad, queries, at, BF16)
     loaded = []
 
     def own_states():
-        loaded.extend(load([out_grad, queries, values], at))
+        loaded.extend(load([out_grad, queries, values, keys], at))
         return loaded[0]
 
     qg = scan_states(own_states, qg_sent, True, at)
     next(qg)
     qg.send([])
-    g, q, v = loaded[1:]
-    kv_sent, k = half_states(v, keys, at, 1, BF16, 1)
+    g, q, v, k = loaded[1:]
+    (kv_sent,) = half_states(v, k, at, 1, BF16, 0)
     (kv_own,) = half_states(v, tie(k, kv_sent), at, 0, F32, 0)
     kv = scan_states(lambda: kv_own, kv_sent, False, at)
     kv_stages = i_bits + 2
@@ -715,7 +715,7 @@
             done = [in_own, turned] + [kv_got] * 1
     qg.send(done)
     qg.send([])
-    in_oth = key_inside(tie(g, in_own), q, v, at, 1, att_scale)
+    in_oth = key_inside(tie(g_oth, in_own), q_oth, v, at, 1, att_scale)
     qg_own, qg_oth = qg.send([in_oth])
 
     def kv_next(*after):
@@ -747,7 +747,7 @@
     keep, *sends = fan(2, 1 + len(groups[0]), p, p_got, q, q_got)
     sends[0] = tie(sends[0], query_own)
     came = swap_all(sends, groups[0])
-    (query_oth,) = query_inside(tie(g, *sends), k, v, at, 1, att_scale)
+    (query_oth,) = query_inside(tie(g_oth, *sends), k, v, at, 1, att_scale)
     for masks in groups[1:]:
         keep, *sends = fan(1, 1 + len(masks), keep, *came)
         came = swap_all(sends, masks)
@@ -769,7 +769,7 @@
     grads_core = swap(grads, "outer", 0)
     n = n_inner // 2
     query_grad, weights = finish(
-        tie(g, p, q), query_own, query_oth, kv_own, kv_oth, at, att_scale,
+        tie(g, p, q), g_oth, query_own, query_oth, kv_own, kv_oth, at, att_scale,
         [(p, (0, (0,), 0, 2 * n)), (q, (1, (0, 2), 0, n))],
     )
     new_master, new_moment1, new_moment2 = adam_all(

time: 89.3 us -> 89.4 us (level)
  starting transfers between devices: 34.8 us -> 39.2 us
  waiting for transfers between devices: 23.2 us -> 20.6 us
  Pallas kernels: 29.9 us -> 28 us
    ppermute x27, starting transfers between devices: 25.9 us -> 30.2 us  [swap(): return lax.ppermute(x, axis, [(i, i ^ 1 << bit) for i in range(n)])]
    ppermute x27, waiting for transfers between devices: 17.1 us -> 14.3 us  [swap(): return lax.ppermute(x, axis, [(i, i ^ 1 << bit) for i in range(n)])]
    pallas_call x32, Pallas kernels: 29.9 us -> 28 us  [call(): pl.pallas_call(body, in_specs=specs, out_specs=[WHOLE if near else HBM fo...]
  transfers between devices with their start and end apart: 33 -> 33, of which waited for: 18 -> 19; matrix products, arithmetic and copies ran while one was open for 0% -> 0% of each run, Pallas kernels for 30% -> 27%
where the time goes in v7:
time: 89.4 us; the launch traced here: 89.2 us
  starting transfers between devices  39.2 us (44%)
  Pallas kernels  28 us (31%)
  waiting for transfers between devices  20.6 us (23%)
  between operations  1.12 us (1%)
    ppermute x27, starting transfers between devices, swap(): return lax.ppermute(x, axis, [(i, i ^ 1 << bit) for i in range(n)])  30.2 us
    pallas_call x32, Pallas kernels, call(): pl.pallas_call(body, in_specs=specs, out_specs=[WHOLE if near else HBM fo...  28 us
    ppermute x27, waiting for transfers between devices, swap(): return lax.ppermute(x, axis, [(i, i ^ 1 << bit) for i in range(n)])  14.3 us
    ppermute x6, starting transfers between devices, swap_all(): lax.ppermute(x, 'inner', [(i, i ^ mask) for i in range(n)])  8.92 us
    ppermute x6, waiting for transfers between devices, swap_all(): lax.ppermute(x, 'inner', [(i, i ^ mask) for i in range(n)])  6.29 us
  transfers between devices with their start and end apart: 33, of which 19 were waited for; matrix products, arithmetic and copies ran while one was open for 0% of the time, Pallas kernels for 27%

profile of v7, /device:TPU:0, one launch (start us, length us, event | category | flops | bytes accessed | tf_op | source)
XLA Modules:
  0.0 89.2 jit_solution(8070306031588829693)
XLA Ops:
  0.6 2.2 %shard_map.132 = (bf16[4,128,128]{2,1,0:T(8,128)(2,1)S(1)}, bf16[1024,512]{1,0:T(8,128)(2,1)S(1)}, bf16[1024,512]{1,0:T(8,128)(2,1)S(1)}) custom-call(bf16[1024,1024]{1,0:T(8,128)(2,1)} %a_hbm.1, bf16[1024,1024]{1,0:T(8,128)(2,1)} %b_hbm.1), custom_call_target="tpu_custom_call" | custom-call | flops 134217728 | bytes 2097152 | tf_op jit(solution)/shard_map/pallas_call | solution.py:31
  2.8 3.0 %collective-permute-start.2 = (bf16[4,128,128]{2,1,0:T(8,128)(2,1)S(1)}, bf16[4,128,128]{2,1,0:T(8,128)(2,1)S(1)}, u32[]{:S(2)}, u32[]{:S(2)}) collective-permute-start(bf16[4,128,128]{2,1,0:T(8,128)(2,1)S(1)} %get-tuple-element.103), channel_id=1, source_target_pairs={{0,1},{1,0},{2,3},{3,2},{4,5},{5,4},{6,7},{7,6},{8,9},{9,8},{10,11... | collective-permute-start | bytes 393224 | tf_op jit(solution)/shard_map/ppermute | solution.py:523
  5.8 3.2 %shard_map.127 = (f32[4,128,128]{2,1,0:T(8,128)S(1)}, bf16[1024,512]{1,0:T(8,128)(2,1)S(1)}, bf16[1024,512]{1,0:T(8,128)(2,1)S(1)}, bf16[1024,1024]{1,0:T(8,128)(2,1)S(1)}, bf16[1024,1024]{1,0:T(8,128)(2,1)S(1)}) custom-call(bf16[1024,1024]{1,0:T(8,128)(2,1)} %a_hbm.1, bf16[1024,1024]{1,0:T(8,128)(2,1)} %b_hbm.1, bf16[1024,1024]{1,0:T(8,128)(2,1)} %refs_2_.1, ...), custom_call_target="tpu_custom_call" | custom-call | flops 134217728 | bytes 16777216 | tf_op jit(solution)/shard_map/pallas_call | solution.py:31
  9.4 1.9 %collective-permute-start.3 = (bf16[4,128,128]{2,1,0:T(8,128)(2,1)S(1)}, bf16[4,128,128]{2,1,0:T(8,128)(2,1)S(1)}, u32[]{:S(2)}, u32[]{:S(2)}) collective-permute-start(bf16[4,128,128]{2,1,0:T(8,128)(2,1)S(1)} %get-tuple-element.105), channel_id=1, source_target_pairs={{0,2},{1,3},{2,0},{3,1},{4,6},{5,7},{6,4},{7,5},{8,10},{9,11},{10,... | collective-permute-start | bytes 393224 | tf_op jit(solution)/shard_map/ppermute | solution.py:523
  14.5 2.9 %collective-permute-start.4 = (bf16[4,128,128]{2,1,0:T(8,128)(2,1)S(1)}, bf16[4,128,128]{2,1,0:T(8,128)(2,1)S(1)}, u32[]{:S(2)}, u32[]{:S(2)}) collective-permute-start(bf16[4,128,128]{2,1,0:T(8,128)(2,1)S(1)} %get-tuple-element.109), channel_id=1, source_target_pairs={{0,4},{1,5},{2,6},{3,7},{4,0},{5,1},{6,2},{7,3},{8,12},{9,13},{10,... | collective-permute-start | bytes 393224 | tf_op jit(solution)/shard_map/ppermute | solution.py:523
  17.3 1.9 %shard_map.129.inside_ref = f32[1024,512]{1,0:T(8,128)S(1)} custom-call(bf16[1024,512]{1,0:T(8,128)(2,1)S(1)} %get-tuple-element.167.g_ref.g_own, bf16[1024,512]{1,0:T(8,128)(2,1)S(1)} %get-tuple-element.98.q_ref, bf16[1024,1024]{1,0:T(8,128)(2,1)S(1)} %get-tuple-element.95.a_ref.v_ref), custom_call_target="tpu_custom_call" | custom-call | flops 805306368 | bytes 5242880 | tf_op jit(solution)/shard_map/pallas_call | solution.py:31
  19.3 2.0 %shard_map.135.turned_ref = bf16[1024,1024]{1,0:T(8,128)(2,1)S(1)} custom-call(bf16[1024,1024]{1,0:T(8,128)(2,1)} %in_hbm), custom_call_target="tpu_custom_call" | custom-call | bytes 4194304 | tf_op jit(solution)/shard_map/pallas_call | solution.py:31
  23.3 1.8 %collective-permute-start.6 = (bf16[4,128,128]{2,1,0:T(8,128)(2,1)S(1)}, bf16[4,128,128]{2,1,0:T(8,128)(2,1)S(1)}, u32[]{:S(2)}, u32[]{:S(2)}) collective-permute-start(bf16[4,128,128]{2,1,0:T(8,128)(2,1)S(1)} %get-tuple-element.117), channel_id=1, source_target_pairs={{0,16},{8,24},{16,0},{24,8},{1,17},{9,25},{17,1},{25,9},{2,18},{10... | collective-permute-start | bytes 393224 | tf_op jit(solution)/shard_map/ppermute | solution.py:523
  26.9 2.0 %shard_map.138.inside_ref = f32[1024,512]{1,0:T(8,128)S(1)} custom-call(bf16[1024,512]{1,0:T(8,128)(2,1)S(1)} %get-tuple-element.144.g_ref.g_oth, bf16[1024,512]{1,0:T(8,128)(2,1)S(1)} %get-tuple-element.120.q_ref, bf16[1024,1024]{1,0:T(8,128)(2,1)S(1)} %get-tuple-element.95.a_ref.v_ref), custom_call_target="tpu_custom_call" | custom-call | flops 805306368 | bytes 5242880 | tf_op jit(solution)/shard_map/pallas_call | solution.py:31
  29.0 1.8 %collective-permute-start.7 = (bf16[4,128,128]{2,1,0:T(8,128)(2,1)S(1)}, bf16[4,128,128]{2,1,0:T(8,128)(2,1)S(1)}, u32[]{:S(2)}, u32[]{:S(2)}) collective-permute-start(bf16[4,128,128]{2,1,0:T(8,128)(2,1)S(1)} %get-tuple-element.124), channel_id=1, source_target_pairs={{0,1},{1,0},{2,3},{3,2},{4,5},{5,4},{6,7},{7,6},{8,9},{9,8},{10,11... | collective-permute-start | bytes 393224 | tf_op jit(solution)/shard_map/ppermute | solution.py:523
  31.3 1.7 %shard_map.140 = (bf16[1024,256]{1,0:T(8,128)(2,1)S(1)}, bf16[1024,256]{1,0:T(8,128)(2,1)S(1)}, bf16[2,8,64,256]{3,2,1,0:T(8,128)(2,1)S(1)}, bf16[2,8,64,256]{3,2,1,0:T(8,128)(2,1)S(1)}) custom-call(f32[1024,512]{1,0:T(8,128)S(1)} %shard_map.129.inside_ref, bf16[1024,1024]{1,0:T(8,128)(2,1)S(1)} %get-tuple-element.95.a_ref.v_ref, ...), custom_call_target="tpu_custom_call" | custom-call | flops 1207959552 | bytes 6291456 | tf_op jit(solution)/shard_map/pallas_call | solution.py:31
  37.4 1.8 %collective-permute-start.12 = (bf16[2,4,64,256]{3,2,1,0:T(8,128)(2,1)S(1)}, bf16[2,4,64,256]{3,2,1,0:T(8,128)(2,1)S(1)}, u32[]{:S(2)}, u32[]{:S(2)}) collective-permute-start(bf16[2,4,64,256]{3,2,1,0:T(8,128)(2,1)S(1)} %get-tuple-element.131), channel_id=1, source_target_pairs={{0,1},{1,0},{2,3},{3,2},{4,5},{5,4},{6,7},{7,6},{8,9},{9,8},{10,11... | collective-permute-start | bytes 786440 | tf_op jit(solution)/shard_map/ppermute | solution.py:523
  40.7 2.0 %collective-permute-start.22 = (bf16[4,128,128]{2,1,0:T(8,128)(2,1)S(1)}, bf16[4,128,128]{2,1,0:T(8,128)(2,1)S(1)}, u32[]{:S(2)}, u32[]{:S(2)}) collective-permute-start(bf16[4,128,128]{2,1,0:T(8,128)(2,1)S(1)} %get-tuple-element.154), channel_id=1, source_target_pairs={{0,4},{1,5},{2,6},{3,7},{4,0},{5,1},{6,2},{7,3},{8,12},{9,13},{10,... | collective-permute-start | bytes 393224 | tf_op jit(solution)/shard_map/ppermute | solution.py:523
  42.7 3.1 %collective-permute-done.12 = bf16[2,4,64,256]{3,2,1,0:T(8,128)(2,1)S(1)} collective-permute-done((bf16[2,4,64,256]{3,2,1,0:T(8,128)(2,1)S(1)}, bf16[2,4,64,256]{3,2,1,0:T(8,128)(2,1)S(1)}, u32[]{:S(2)}, u32[]{:S(2)}) %collective-permute-start.12) | collective-permute-done | bytes 262176 | tf_op jit(solution)/shard_map/ppermute | solution.py:523
  46.0 1.8 %collective-permute-start.13 = (bf16[1,4,64,256]{3,2,1,0:T(8,128)(2,1)S(1)}, bf16[1,4,64,256]{3,2,1,0:T(8,128)(2,1)S(1)}, u32[]{:S(2)}, u32[]{:S(2)}) collective-permute-start(bf16[1,4,64,256]{3,2,1,0:T(8,128)(2,1)S(1)} %get-tuple-element.182), channel_id=1, source_target_pairs={{0,16},{8,24},{16,0},{24,8},{1,17},{9,25},{17,1},{25,9},{2,18},{10... | collective-permute-start | bytes 393224 | tf_op jit(solution)/shard_map/ppermute | solution.py:523
  49.4 3.2 %shard_map.145 = (f32[1024,512]{1,0:T(8,128)S(1)}, bf16[1024,1024]{1,0:T(8,128)(2,1)}) custom-call(bf16[1024,512]{1,0:T(8,128)(2,1)S(1)} %get-tuple-element.167.g_ref.g_own, bf16[1024,1024]{1,0:T(8,128)(2,1)S(1)} %get-tuple-element.99.b_ref.k_ref, bf16[1024,1024]{1,0:T(8,128)(2,1)S(1)} %get-tuple-element.95.a_ref.v_ref, ...), custom_call_target="tpu_custom_call" | custom-call | flops 805306368 | bytes 5242880 | tf_op jit(solution)/shard_map/pallas_call | solution.py:31
  52.9 2.4 %collective-permute-start.14 = (bf16[2,1,64,256]{3,2,1,0:T(8,128)(2,1)S(1)}, bf16[2,1,64,256]{3,2,1,0:T(8,128)(2,1)S(1)}, u32[]{:S(2)}, u32[]{:S(2)}) collective-permute-start(bf16[2,1,64,256]{3,2,1,0:T(8,128)(2,1)S(1)} %get-tuple-element.140), channel_id=1, source_target_pairs={{0,4},{1,5},{2,6},{3,7},{4,0},{5,1},{6,2},{7,3},{8,12},{9,13},{10,... | collective-permute-start | bytes 196616 | tf_op jit(solution)/shard_map/ppermute | solution.py:616
  55.4 1.7 %collective-permute-start.15 = (bf16[2,1,64,256]{3,2,1,0:T(8,128)(2,1)S(1)}, bf16[2,1,64,256]{3,2,1,0:T(8,128)(2,1)S(1)}, u32[]{:S(2)}, u32[]{:S(2)}) collective-permute-start(bf16[2,1,64,256]{3,2,1,0:T(8,128)(2,1)S(1)} %get-tuple-element.141), channel_id=1, source_target_pairs={{0,2},{1,3},{2,0},{3,1},{4,6},{5,7},{6,4},{7,5},{8,10},{9,11},{10,... | collective-permute-start | bytes 196616 | tf_op jit(solution)/shard_map/ppermute | solution.py:616
  57.4 2.0 %shard_map.147.in_oth = f32[1024,512]{1,0:T(8,128)S(1)} custom-call(bf16[1024,512]{1,0:T(8,128)(2,1)S(1)} %get-tuple-element.144.g_ref.g_oth, bf16[1024,1024]{1,0:T(8,128)(2,1)S(1)} %get-tuple-element.99.b_ref.k_ref, bf16[1024,1024]{1,0:T(8,128)(2,1)S(1)} %get-tuple-element.95.a_ref.v_ref), custom_call_target="tpu_custom_call" | custom-call | flops 805306368 | bytes 5242880 | tf_op jit(solution)/shard_map/pallas_call | solution.py:31
  60.5 2.7 %collective-permute-done.16.refs_3_ = bf16[2,1,64,256]{3,2,1,0:T(8,128)(2,1)S(1)} collective-permute-done((bf16[2,1,64,256]{3,2,1,0:T(8,128)(2,1)S(1)}, bf16[2,1,64,256]{3,2,1,0:T(8,128)(2,1)S(1)}, u32[]{:S(2)}, u32[]{:S(2)}) %collective-permute-start.16) | collective-permute-done | bytes 65568 | tf_op jit(solution)/shard_map/ppermute | solution.py:616
  65.2 2.6 %collective-permute-start.19 = (bf16[2,1,64,256]{3,2,1,0:T(8,128)(2,1)S(1)}, bf16[2,1,64,256]{3,2,1,0:T(8,128)(2,1)S(1)}, u32[]{:S(2)}, u32[]{:S(2)}) collective-permute-start(bf16[2,1,64,256]{3,2,1,0:T(8,128)(2,1)S(1)} %get-tuple-element.145.refs_0_), channel_id=1, source_target_pairs={{0,6},{1,7},{2,4},{3,5},{4,2},{5,3},{6,0},{7,1},{8,14},{9,15},{10,... | collective-permute-start | bytes 196616 | tf_op jit(solution)/shard_map/ppermute | solution.py:616
  67.8 2.2 %collective-permute-done.17.refs_1_ = bf16[2,1,64,256]{3,2,1,0:T(8,128)(2,1)S(1)} collective-permute-done((bf16[2,1,64,256]{3,2,1,0:T(8,128)(2,1)S(1)}, bf16[2,1,64,256]{3,2,1,0:T(8,128)(2,1)S(1)}, u32[]{:S(2)}, u32[]{:S(2)}) %collective-permute-start.17) | collective-permute-done | bytes 65568 | tf_op jit(solution)/shard_map/ppermute | solution.py:616
  74.8 2.8 %collective-permute-done.20.refs_1_ = bf16[1,4,64,256]{3,2,1,0:T(8,128)(2,1)S(1)} collective-permute-done((bf16[1,4,64,256]{3,2,1,0:T(8,128)(2,1)S(1)}, bf16[1,4,64,256]{3,2,1,0:T(8,128)(2,1)S(1)}, u32[]{:S(2)}, u32[]{:S(2)}) %collective-permute-start.20) | collective-permute-done | bytes 131104 | tf_op jit(solution)/shard_map/ppermute | solution.py:523
  81.6 1.8 %shard_map.155 = (bf16[1024,1024]{1,0:T(8,128)(2,1)}, bf16[4,2,2,64,1024]{4,3,2,1,0:T(8,128)(2,1)}) custom-call(bf16[1024,512]{1,0:T(8,128)(2,1)S(1)} %get-tuple-element.167.g_ref.g_own, bf16[1024,512]{1,0:T(8,128)(2,1)S(1)} %get-tuple-element.144.g_ref.g_oth, f32[1024,512]{1,0:T(8,128)S(1)} %get-tuple-element.139.in_own, ...), custom_call_target="tpu_custom_call" | custom-call | flops 268435456 | bytes 8388608 | tf_op jit(solution)/shard_map/pallas_call | solution.py:31
  (82 shorter events, 33.8 us)
Async XLA Ops:
  2.8 6.5 %collective-permute-start.2 = (bf16[4,128,128]{2,1,0:T(8,128)(2,1)S(1)}, bf16[4,128,128]{2,1,0:T(8,128)(2,1)S(1)}, u32[]{:S(2)}, u32[]{:S(2)}) collective-permute-start(bf16[4,128,128]{2,1,0:T(8,128)(2,1)S(1)} %get-tuple-element.103), channel_id=1, source_target_pairs={{0,1},{1,0},{2,3},{3,2},{4,5},{5,4},{6,7},{7,6},{8,9},{9,8},{10,11... | collective-permute-start | bytes 393224 | tf_op jit(solution)/shard_map/ppermute | solution.py:523
  9.4 5.0 %collective-permute-start.3 = (bf16[4,128,128]{2,1,0:T(8,128)(2,1)S(1)}, bf16[4,128,128]{2,1,0:T(8,128)(2,1)S(1)}, u32[]{:S(2)}, u32[]{:S(2)}) collective-permute-start(bf16[4,128,128]{2,1,0:T(8,128)(2,1)S(1)} %get-tuple-element.105), channel_id=1, source_target_pairs={{0,2},{1,3},{2,0},{3,1},{4,6},{5,7},{6,4},{7,5},{8,10},{9,11},{10,... | collective-permute-start | bytes 393224 | tf_op jit(solution)/shard_map/ppermute | solution.py:523
  12.0 9.3 %collective-permute-start = (bf16[4,128,128]{2,1,0:T(8,128)(2,1)S(1)}, bf16[4,128,128]{2,1,0:T(8,128)(2,1)S(1)}, u32[]{:S(2)}, u32[]{:S(2)}) collective-permute-start(bf16[4,128,128]{2,1,0:T(8,128)(2,1)S(1)} %shard_map.128), channel_id=1, source_target_pairs={{0,1},{1,0},{2,3},{3,2},{4,5},{5,4},{6,7},{7,6},{8,9},{9,8},{10,11... | collective-permute-start | bytes 393224 | tf_op jit(solution)/shard_map/ppermute | solution.py:523
  14.5 7.3 %collective-permute-start.4 = (bf16[4,128,128]{2,1,0:T(8,128)(2,1)S(1)}, bf16[4,128,128]{2,1,0:T(8,128)(2,1)S(1)}, u32[]{:S(2)}, u32[]{:S(2)}) collective-permute-start(bf16[4,128,128]{2,1,0:T(8,128)(2,1)S(1)} %get-tuple-element.109), channel_id=1, source_target_pairs={{0,4},{1,5},{2,6},{3,7},{4,0},{5,1},{6,2},{7,3},{8,12},{9,13},{10,... | collective-permute-start | bytes 393224 | tf_op jit(solution)/shard_map/ppermute | solution.py:523
  23.3 5.6 %collective-permute-start.6 = (bf16[4,128,128]{2,1,0:T(8,128)(2,1)S(1)}, bf16[4,128,128]{2,1,0:T(8,128)(2,1)S(1)}, u32[]{:S(2)}, u32[]{:S(2)}) collective-permute-start(bf16[4,128,128]{2,1,0:T(8,128)(2,1)S(1)} %get-tuple-element.117), channel_id=1, source_target_pairs={{0,16},{8,24},{16,0},{24,8},{1,17},{9,25},{17,1},{25,9},{2,18},{10... | collective-permute-start | bytes 393224 | tf_op jit(solution)/shard_map/ppermute | solution.py:523
  26.0 5.3 %collective-permute-start.1 = (bf16[4,128,128]{2,1,0:T(8,128)(2,1)S(1)}, bf16[4,128,128]{2,1,0:T(8,128)(2,1)S(1)}, u32[]{:S(2)}, u32[]{:S(2)}) collective-permute-start(bf16[4,128,128]{2,1,0:T(8,128)(2,1)S(1)} %get-tuple-element.100), channel_id=1, source_target_pairs={{0,2},{1,3},{2,0},{3,1},{4,6},{5,7},{6,4},{7,5},{8,10},{9,11},{10,... | collective-permute-start | bytes 393224 | tf_op jit(solution)/shard_map/ppermute | solution.py:523
  37.4 8.4 %collective-permute-start.12 = (bf16[2,4,64,256]{3,2,1,0:T(8,128)(2,1)S(1)}, bf16[2,4,64,256]{3,2,1,0:T(8,128)(2,1)S(1)}, u32[]{:S(2)}, u32[]{:S(2)}) collective-permute-start(bf16[2,4,64,256]{3,2,1,0:T(8,128)(2,1)S(1)} %get-tuple-element.131), channel_id=1, source_target_pairs={{0,1},{1,0},{2,3},{3,2},{4,5},{5,4},{6,7},{7,6},{8,9},{9,8},{10,11... | collective-permute-start | bytes 786440 | tf_op jit(solution)/shard_map/ppermute | solution.py:523
  39.2 8.6 %collective-permute-start.10 = (bf16[1,8,64,256]{3,2,1,0:T(8,128)(2,1)S(1)}, bf16[1,8,64,256]{3,2,1,0:T(8,128)(2,1)S(1)}, u32[]{:S(2)}, u32[]{:S(2)}) collective-permute-start(bf16[1,8,64,256]{3,2,1,0:T(8,128)(2,1)S(1)} %get-tuple-element.129), channel_id=1, source_target_pairs={{0,16},{8,24},{16,0},{24,8},{1,17},{9,25},{17,1},{25,9},{2,18},{10... | collective-permute-start | bytes 786440 | tf_op jit(solution)/shard_map/ppermute | solution.py:523
  40.7 11.9 %collective-permute-start.22 = (bf16[4,128,128]{2,1,0:T(8,128)(2,1)S(1)}, bf16[4,128,128]{2,1,0:T(8,128)(2,1)S(1)}, u32[]{:S(2)}, u32[]{:S(2)}) collective-permute-start(bf16[4,128,128]{2,1,0:T(8,128)(2,1)S(1)} %get-tuple-element.154), channel_id=1, source_target_pairs={{0,4},{1,5},{2,6},{3,7},{4,0},{5,1},{6,2},{7,3},{8,12},{9,13},{10,... | collective-permute-start | bytes 393224 | tf_op jit(solution)/shard_map/ppermute | solution.py:523
  46.0 6.8 %collective-permute-start.13 = (bf16[1,4,64,256]{3,2,1,0:T(8,128)(2,1)S(1)}, bf16[1,4,64,256]{3,2,1,0:T(8,128)(2,1)S(1)}, u32[]{:S(2)}, u32[]{:S(2)}) collective-permute-start(bf16[1,4,64,256]{3,2,1,0:T(8,128)(2,1)S(1)} %get-tuple-element.182), channel_id=1, source_target_pairs={{0,16},{8,24},{16,0},{24,8},{1,17},{9,25},{17,1},{25,9},{2,18},{10... | collective-permute-start | bytes 393224 | tf_op jit(solution)/shard_map/ppermute | solution.py:523
  52.7 6.7 %collective-permute-start.23 = (bf16[4,128,128]{2,1,0:T(8,128)(2,1)S(1)}, bf16[4,128,128]{2,1,0:T(8,128)(2,1)S(1)}, u32[]{:S(2)}, u32[]{:S(2)}) collective-permute-start(bf16[4,128,128]{2,1,0:T(8,128)(2,1)S(1)} %get-tuple-element.158), channel_id=1, source_target_pairs={{0,8},{8,0},{16,24},{24,16},{1,9},{9,1},{17,25},{25,17},{2,10},{10... | collective-permute-start | bytes 393224 | tf_op jit(solution)/shard_map/ppermute | solution.py:523
  52.9 7.5 %collective-permute-start.14 = (bf16[2,1,64,256]{3,2,1,0:T(8,128)(2,1)S(1)}, bf16[2,1,64,256]{3,2,1,0:T(8,128)(2,1)S(1)}, u32[]{:S(2)}, u32[]{:S(2)}) collective-permute-start(bf16[2,1,64,256]{3,2,1,0:T(8,128)(2,1)S(1)} %get-tuple-element.140), channel_id=1, source_target_pairs={{0,4},{1,5},{2,6},{3,7},{4,0},{5,1},{6,2},{7,3},{8,12},{9,13},{10,... | collective-permute-start | bytes 196616 | tf_op jit(solution)/shard_map/ppermute | solution.py:616
  55.4 5.1 %collective-permute-start.15 = (bf16[2,1,64,256]{3,2,1,0:T(8,128)(2,1)S(1)}, bf16[2,1,64,256]{3,2,1,0:T(8,128)(2,1)S(1)}, u32[]{:S(2)}, u32[]{:S(2)}) collective-permute-start(bf16[2,1,64,256]{3,2,1,0:T(8,128)(2,1)S(1)} %get-tuple-element.141), channel_id=1, source_target_pairs={{0,2},{1,3},{2,0},{3,1},{4,6},{5,7},{6,4},{7,5},{8,10},{9,11},{10,... | collective-permute-start | bytes 196616 | tf_op jit(solution)/shard_map/ppermute | solution.py:616
  57.1 6.1 %collective-permute-start.16 = (bf16[2,1,64,256]{3,2,1,0:T(8,128)(2,1)S(1)}, bf16[2,1,64,256]{3,2,1,0:T(8,128)(2,1)S(1)}, u32[]{:S(2)}, u32[]{:S(2)}) collective-permute-start(bf16[2,1,64,256]{3,2,1,0:T(8,128)(2,1)S(1)} %get-tuple-element.142), channel_id=1, source_target_pairs={{0,6},{1,7},{2,4},{3,5},{4,2},{5,3},{6,0},{7,1},{8,14},{9,15},{10,... | collective-permute-start | bytes 196616 | tf_op jit(solution)/shard_map/ppermute | solution.py:616
  59.5 13.1 %collective-permute-start.24 = (bf16[4,128,128]{2,1,0:T(8,128)(2,1)S(1)}, bf16[4,128,128]{2,1,0:T(8,128)(2,1)S(1)}, u32[]{:S(2)}, u32[]{:S(2)}) collective-permute-start(bf16[4,128,128]{2,1,0:T(8,128)(2,1)S(1)} %get-tuple-element.162), channel_id=1, source_target_pairs={{0,16},{8,24},{16,0},{24,8},{1,17},{9,25},{17,1},{25,9},{2,18},{10... | collective-permute-start | bytes 393224 | tf_op jit(solution)/shard_map/ppermute | solution.py:523
  63.3 6.6 %collective-permute-start.17 = (bf16[2,1,64,256]{3,2,1,0:T(8,128)(2,1)S(1)}, bf16[2,1,64,256]{3,2,1,0:T(8,128)(2,1)S(1)}, u32[]{:S(2)}, u32[]{:S(2)}) collective-permute-start(bf16[2,1,64,256]{3,2,1,0:T(8,128)(2,1)S(1)} %get-tuple-element.145.refs_0_), channel_id=1, source_target_pairs={{0,4},{1,5},{2,6},{3,7},{4,0},{5,1},{6,2},{7,3},{8,12},{9,13},{10,... | collective-permute-start | bytes 196616 | tf_op jit(solution)/shard_map/ppermute | solution.py:616
  64.7 5.5 %collective-permute-start.18 = (bf16[2,1,64,256]{3,2,1,0:T(8,128)(2,1)S(1)}, bf16[2,1,64,256]{3,2,1,0:T(8,128)(2,1)S(1)}, u32[]{:S(2)}, u32[]{:S(2)}) collective-permute-start(bf16[2,1,64,256]{3,2,1,0:T(8,128)(2,1)S(1)} %get-tuple-element.145.refs_0_), channel_id=1, source_target_pairs={{0,2},{1,3},{2,0},{3,1},{4,6},{5,7},{6,4},{7,5},{8,10},{9,11},{10,... | collective-permute-start | bytes 196616 | tf_op jit(solution)/shard_map/ppermute | solution.py:616
  65.2 6.2 %collective-permute-start.19 = (bf16[2,1,64,256]{3,2,1,0:T(8,128)(2,1)S(1)}, bf16[2,1,64,256]{3,2,1,0:T(8,128)(2,1)S(1)}, u32[]{:S(2)}, u32[]{:S(2)}) collective-permute-start(bf16[2,1,64,256]{3,2,1,0:T(8,128)(2,1)S(1)} %get-tuple-element.145.refs_0_), channel_id=1, source_target_pairs={{0,6},{1,7},{2,4},{3,5},{4,2},{5,3},{6,0},{7,1},{8,14},{9,15},{10,... | collective-permute-start | bytes 196616 | tf_op jit(solution)/shard_map/ppermute | solution.py:616
  71.4 6.2 %collective-permute-start.21 = (bf16[1,6,64,256]{3,2,1,0:T(8,128)(2,1)S(1)}, bf16[1,6,64,256]{3,2,1,0:T(8,128)(2,1)S(1)}, u32[]{:S(2)}, u32[]{:S(2)}) collective-permute-start(bf16[1,6,64,256]{3,2,1,0:T(8,128)(2,1)S(1)} %get-tuple-element.148.a_ref), channel_id=1, source_target_pairs={{0,16},{8,24},{16,0},{24,8},{1,17},{9,25},{17,1},{25,9},{2,18},{10... | collective-permute-start | bytes 589832 | tf_op jit(solution)/shard_map/ppermute | solution.py:523
  73.6 5.3 %collective-permute-start.25 = (bf16[4,128,128]{2,1,0:T(8,128)(2,1)S(1)}, bf16[4,128,128]{2,1,0:T(8,128)(2,1)S(1)}, u32[]{:S(2)}, u32[]{:S(2)}) collective-permute-start(bf16[4,128,128]{2,1,0:T(8,128)(2,1)S(1)} %get-tuple-element.164), channel_id=1, source_target_pairs={{0,1},{1,0},{2,3},{3,2},{4,5},{5,4},{6,7},{7,6},{8,9},{9,8},{10,11... | collective-permute-start | bytes 393224 | tf_op jit(solution)/shard_map/ppermute | solution.py:523
  79.0 6.4 %collective-permute-start.27 = (bf16[1,8,64,256]{3,2,1,0:T(8,128)(2,1)S(1)}, bf16[1,8,64,256]{3,2,1,0:T(8,128)(2,1)S(1)}, u32[]{:S(2)}, u32[]{:S(2)}) collective-permute-start(bf16[1,8,64,256]{3,2,1,0:T(8,128)(2,1)S(1)} %shard_map.149.refs_0_), channel_id=1, source_target_pairs={{0,16},{8,24},{16,0},{24,8},{1,17},{9,25},{17,1},{25,9},{2,18},{10... | collective-permute-start | bytes 786440 | tf_op jit(solution)/shard_map/ppermute | solution.py:523
  79.9 6.4 %collective-permute-start.28 = (bf16[2,4,64,256]{3,2,1,0:T(8,128)(2,1)S(1)}, bf16[2,4,64,256]{3,2,1,0:T(8,128)(2,1)S(1)}, u32[]{:S(2)}, u32[]{:S(2)}) collective-permute-start(bf16[2,4,64,256]{3,2,1,0:T(8,128)(2,1)S(1)} %get-tuple-element.166.refs_1_), channel_id=1, source_target_pairs={{0,1},{1,0},{2,3},{3,2},{4,5},{5,4},{6,7},{7,6},{8,9},{9,8},{10,11... | collective-permute-start | bytes 786440 | tf_op jit(solution)/shard_map/ppermute | solution.py:523
  81.1 5.1 %collective-permute-start.29 = (bf16[1,8,64,256]{3,2,1,0:T(8,128)(2,1)S(1)}, bf16[1,8,64,256]{3,2,1,0:T(8,128)(2,1)S(1)}, u32[]{:S(2)}, u32[]{:S(2)}) collective-permute-start(bf16[1,8,64,256]{3,2,1,0:T(8,128)(2,1)S(1)} %shard_map.149.refs_0_), channel_id=1, source_target_pairs={{0,8},{8,0},{16,24},{24,16},{1,9},{9,1},{17,25},{25,17},{2,10},{10... | collective-permute-start | bytes 786440 | tf_op jit(solution)/shard_map/ppermute | solution.py:523
  81.1 5.1 %collective-permute-start.30 = (bf16[2,4,64,256]{3,2,1,0:T(8,128)(2,1)S(1)}, bf16[2,4,64,256]{3,2,1,0:T(8,128)(2,1)S(1)}, u32[]{:S(2)}, u32[]{:S(2)}) collective-permute-start(bf16[2,4,64,256]{3,2,1,0:T(8,128)(2,1)S(1)} %get-tuple-element.166.refs_1_), channel_id=1, source_target_pairs={{0,8},{8,0},{16,24},{24,16},{1,9},{9,1},{17,25},{25,17},{2,10},{10... | collective-permute-start | bytes 786440 | tf_op jit(solution)/shard_map/ppermute | solution.py:523
  (12 other events, 45.1 us)
